TPU v7x, 128 devices: a whole 4x4x4 slice. The times are simulated.
128 devices in a mesh: dp: 2 (over core), ctx: 16 (over y, x), head: 4 (over z).
Axes of the slice: x: 4, y: 4, z: 4, core: 2. Of those that a mesh axis runs over, the one named last changes fastest.
Arguments:
- inputs: bfloat16 [12288, 1024], P(('dp', 'ctx')), may hold values from -6 to 6
- cotangent: bfloat16 [12288, 1024], P(('dp', 'ctx')), may hold values from -6 to 6
- attention_gain: float32 [1024], replicated, may hold values from 0.1 to 1.9
- query_gain: float32 [64], replicated, may hold values from 0.1 to 1.9
- key_gain: float32 [64], replicated, may hold values from 0.1 to 1.9
- w_query: bfloat16 [1024, 1024], P(None, 'head'), may hold values from -0.1875 to 0.1875
- key_weight: bfloat16 [1024, 512], P(None, 'head'), may hold values from -0.1875 to 0.1875
- value_weight: bfloat16 [1024, 512], P(None, 'head'), may hold values from -0.1875 to 0.1875
- w_out: bfloat16 [1024, 1024], P(None, 'head'), may hold values from -3 to 3
- feed_gain: float32 [1024], replicated, may hold values from 0.1 to 1.9
- w_gate: bfloat16 [1024, 4608], P(None, 'head'), may hold values from -0.1875 to 0.1875
- w_up: bfloat16 [1024, 4608], P(None, 'head'), may hold values from -0.1875 to 0.1875
- w_down: bfloat16 [1024, 4608], P(None, 'head'), may hold values from -0.09375 to 0.09375
Outputs:
- block_out: bfloat16 [12288, 1024], P(('dp', 'ctx'))
- input_grad: float32 [12288, 1024], P(('dp', 'ctx'))
- attention_gain_grad: float32 [1024], P(('dp', 'ctx'))
- query_gain_grad: float32 [64], P(('dp', 'ctx'))
- key_gain_grad: float32 [64], P(('dp', 'ctx'))
- w_query_grad: float32 [1024, 1024], P(('dp', 'ctx'), 'head')
- w_key_grad: float32 [1024, 512], P(('dp', 'ctx'), 'head')
- w_value_grad: float32 [1024, 512], P(('dp', 'ctx'), 'head')
- w_out_grad: float32 [1024, 1024], P(('dp', 'ctx'), 'head')
- feed_gain_grad: float32 [1024], P(('dp', 'ctx'))
- w_gate_grad: float32 [1024, 4608], P(('dp', 'ctx'), 'head')
- w_up_grad: float32 [1024, 4608], P(('dp', 'ctx'), 'head')
- w_down_grad: float32 [1024, 4608], P(('dp', 'ctx'), 'head')
All inputs are finite; a program needn't handle non-finite values.
Results may differ from a plain program's by a relative error of at most 0.04.
Values may be sent and summed in bfloat16 or wider, within the bound.
A program may use at most 192 MiB of HBM per device.

v0:
```python
from functools import partial

import jax
import jax.numpy as jnp
from jax import lax
from jax.sharding import PartitionSpec as P

epsilon = 1e-05
theta_base = 1000000.0
masked_value = -1e30


def rms_scale(values):
    return lax.rsqrt(jnp.mean(values * values, axis=-1, keepdims=True) + epsilon)


def row_norm(values, gain):
    return values * rms_scale(values) * gain


def rotary_tables(positions, head_dim):
    half_width = head_dim // 2
    frequency = theta_base ** (-(jnp.arange(half_width).astype(jnp.float32) * 2.0) / head_dim)
    angles = positions.astype(jnp.float32)[:, None] * frequency[None, :]
    cosine_table = jnp.cos(angles)
    sine_table = jnp.sin(angles)
    return (
        jnp.concatenate([cosine_table, cosine_table], -1),
        jnp.concatenate([sine_table, sine_table], -1),
    )


def rotate(values, cosine_table, sine_table):
    half_width = values.shape[-1] // 2
    turned = jnp.concatenate([-values[..., half_width:], values[..., :half_width]], -1)
    return values * cosine_table + turned * sine_table


def head_norm_rotate(values, gain, cosine_table, sine_table):
    shaped = values.reshape(values.shape[0], -1, gain.shape[0])
    turned = rotate(row_norm(shaped, gain), cosine_table[:, None, :], sine_table[:, None, :])
    return turned.reshape(values.shape[0], -1)


def group_rows(values, heads_per_group, head_dim):
    block_rows = values.shape[0]
    shaped = values.reshape(block_rows, -1, heads_per_group, head_dim)
    return shaped.transpose(1, 2, 0, 3).reshape(
        shaped.shape[1], heads_per_group * block_rows, head_dim
    )


def ungroup_rows(values, block_rows):
    key_heads, stacked, head_dim = values.shape
    heads_per_group = stacked // block_rows
    return (
        values.reshape(key_heads, heads_per_group, block_rows, head_dim)
        .transpose(2, 0, 1, 3)
        .reshape(block_rows, -1)
    )


def contract_rows(left_side, right_side):
    return lax.dot_general(
        left_side, right_side, (((0,), (0,)), ((), ())), preferred_element_type=jnp.float32
    )


def contract_cols(left_side, right_side):
    return lax.dot_general(
        left_side, right_side, (((1,), (1,)), ((), ())), preferred_element_type=jnp.float32
    )


def split_heads(values, head_dim):
    return values.reshape(values.shape[0], -1, head_dim).transpose(1, 0, 2)


def attend_piece(state_in, key_piece, value_piece, first_row, query_grp, query_pos):
    head_dim = query_grp.shape[-1]
    piece_rows = key_piece.shape[0]

    def update(state):
        running_max, running_sum, accumulated = state
        key_grp = split_heads(key_piece, head_dim)
        value_grp = split_heads(value_piece, head_dim)
        scores = jnp.einsum(
            "gqd,gkd->gqk", query_grp, key_grp, preferred_element_type=jnp.float32
        ) * head_dim ** (-0.5)
        allowed = query_pos[:, None] >= jnp.arange(piece_rows, dtype=jnp.int32)[None, :]
        scores = jnp.where(allowed[None], scores, -jnp.inf)
        new_max = jnp.maximum(running_max, jnp.max(scores, axis=-1))
        weights = jnp.exp(scores - new_max[..., None])
        running_sum = jnp.sum(weights, axis=-1)
        accumulated = jnp.einsum(
            "gqk,gkd->gqd",
            weights.astype(jnp.bfloat16),
            value_grp,
            preferred_element_type=jnp.float32,
        )
        return (new_max, running_sum, accumulated)

    return lax.cond(first_row <= query_pos[-1], update, lambda state: state, state_in)


def shards(
    inputs,
    cotangent,
    attention_gain,
    query_gain,
    key_gain,
    w_query,
    key_weight,
    value_weight,
    w_out,
    feed_gain,
    w_gate,
    w_up,
    w_down,
):
    block_rows = inputs.shape[0]
    head_dim = query_gain.shape[0]
    heads_per_group = w_query.shape[1] // key_weight.shape[1]
    key_heads = key_weight.shape[1] // head_dim
    stacked_rows = heads_per_group * block_rows
    cycle_size = lax.axis_size("ctx")
    scale_factor = head_dim ** (-0.5)
    positions = lax.axis_index("ctx") * block_rows + jnp.arange(block_rows, dtype=jnp.int32)
    query_pos = jnp.tile(positions, heads_per_group)
    cosine_table, sine_table = rotary_tables(positions, head_dim)
    rotate_head = partial(head_norm_rotate, cosine_table=cosine_table, sine_table=sine_table)
    input_rows = inputs.astype(jnp.float32)
    normed_full, attention_pull = jax.vjp(row_norm, input_rows, attention_gain)
    normalized_input = normed_full.astype(jnp.bfloat16)
    query_raw = jnp.dot(normalized_input, w_query, preferred_element_type=jnp.float32)
    key_raw = jnp.dot(normalized_input, key_weight, preferred_element_type=jnp.float32)
    value_bf = jnp.dot(normalized_input, value_weight, preferred_element_type=jnp.float32).astype(
        jnp.bfloat16
    )
    query_rot, query_pull = jax.vjp(rotate_head, query_raw, query_gain)
    key_rot, key_pull = jax.vjp(rotate_head, key_raw, key_gain)
    query_grp = group_rows(query_rot.astype(jnp.bfloat16), heads_per_group, head_dim)
    key_bf = key_rot.astype(jnp.bfloat16)
    start_state = (
        jnp.full((key_heads, stacked_rows), masked_value, jnp.float32),
        jnp.zeros((key_heads, stacked_rows), jnp.float32),
        jnp.zeros((key_heads, stacked_rows, head_dim), jnp.float32),
    )
    running_max, running_sum, accumulated = attend_piece(
        start_state,
        lax.all_gather(key_bf, "ctx", axis=0, tiled=True),
        lax.all_gather(value_bf, "ctx", axis=0, tiled=True),
        jnp.int32(0),
        query_grp,
        query_pos,
    )
    log_total = running_max + jnp.log(running_sum)
    attended_grp = (accumulated / running_sum[..., None]).astype(jnp.bfloat16)
    attended_bf = ungroup_rows(attended_grp, block_rows)
    attention_part = contract_cols(attended_bf, w_out)
    hidden_first = input_rows + lax.psum(attention_part.astype(jnp.bfloat16), "head").astype(
        jnp.float32
    )
    mixed_full, feed_pull = jax.vjp(row_norm, hidden_first, feed_gain)
    mixed = mixed_full.astype(jnp.bfloat16)
    gate_rows = jnp.dot(mixed, w_gate, preferred_element_type=jnp.float32)
    up_rows = jnp.dot(mixed, w_up, preferred_element_type=jnp.float32)
    sigmoid_gate = jax.nn.sigmoid(gate_rows)
    silu_rows = gate_rows * sigmoid_gate
    inner_bf = (silu_rows * up_rows).astype(jnp.bfloat16)
    down_part = contract_cols(inner_bf, w_down)
    final_rows = hidden_first + lax.psum(down_part.astype(jnp.bfloat16), "head").astype(jnp.float32)
    block_out = final_rows.astype(jnp.bfloat16)
    w_down_grad = contract_rows(cotangent, inner_bf)
    grad_inner = jnp.dot(cotangent, w_down, preferred_element_type=jnp.float32)
    grad_gate = (
        grad_inner * up_rows * sigmoid_gate * (1.0 + gate_rows * (1.0 - sigmoid_gate))
    ).astype(jnp.bfloat16)
    grad_up = (grad_inner * silu_rows).astype(jnp.bfloat16)
    w_gate_grad = contract_rows(mixed, grad_gate)
    w_up_grad = contract_rows(mixed, grad_up)
    mixed_part = contract_cols(grad_gate, w_gate) + contract_cols(grad_up, w_up)
    grad_mixed = lax.psum(mixed_part.astype(jnp.bfloat16), "head").astype(jnp.float32)
    hidden_from_norm, feed_gain_part = feed_pull(grad_mixed)
    grad_hidden_first = cotangent.astype(jnp.float32) + hidden_from_norm
    grad_branch = grad_hidden_first.astype(jnp.bfloat16)
    w_out_grad = contract_rows(grad_branch, attended_bf)
    grad_attended = jnp.dot(grad_branch, w_out, preferred_element_type=jnp.float32).astype(
        jnp.bfloat16
    )
    dout_grp = group_rows(grad_attended, heads_per_group, head_dim)
    delta = jnp.sum(dout_grp.astype(jnp.float32) * attended_grp.astype(jnp.float32), axis=-1)
    key_all, value_all = (
        lax.all_gather(key_bf, "ctx", axis=0, tiled=True),
        lax.all_gather(value_bf, "ctx", axis=0, tiled=True),
    )
    key_width = key_bf.shape[1]

    def backward_step(block_index, state_in):
        grad_query, key_term, value_term = state_in
        first_row = block_index * block_rows
        key_piece = lax.dynamic_slice_in_dim(key_all, first_row, block_rows, 0)
        value_piece = lax.dynamic_slice_in_dim(value_all, first_row, block_rows, 0)

        def compute(unused):
            key_grp = split_heads(key_piece, head_dim)
            value_grp = split_heads(value_piece, head_dim)
            scores = (
                jnp.einsum("gqd,gkd->gqk", query_grp, key_grp, preferred_element_type=jnp.float32)
                * scale_factor
            )
            allowed = (
                query_pos[:, None] >= (first_row + jnp.arange(block_rows, dtype=jnp.int32))[None, :]
            )
            scores = jnp.where(allowed[None], scores, -jnp.inf)
            probabilities = jnp.exp(scores - log_total[..., None])
            value_grad = jnp.einsum(
                "gqk,gqd->gkd",
                probabilities.astype(jnp.bfloat16),
                dout_grp,
                preferred_element_type=jnp.float32,
            )
            prob_grad = jnp.einsum(
                "gqd,gkd->gqk", dout_grp, value_grp, preferred_element_type=jnp.float32
            )
            score_grad = (probabilities * (prob_grad - delta[..., None])).astype(jnp.bfloat16)
            query_add = (
                jnp.einsum("gqk,gkd->gqd", score_grad, key_grp, preferred_element_type=jnp.float32)
                * scale_factor
            )
            key_grad = (
                jnp.einsum(
                    "gqk,gqd->gkd", score_grad, query_grp, preferred_element_type=jnp.float32
                )
                * scale_factor
            )
            return (
                query_add,
                key_grad.transpose(1, 0, 2).reshape(block_rows, key_width),
                value_grad.transpose(1, 0, 2).reshape(block_rows, key_width),
            )

        def skipped(unused):
            return (
                jnp.zeros_like(grad_query),
                jnp.zeros((block_rows, key_width), jnp.float32),
                jnp.zeros((block_rows, key_width), jnp.float32),
            )

        query_add, key_grad, value_grad = lax.cond(first_row <= query_pos[-1], compute, skipped, 0)
        return (
            grad_query + query_add,
            lax.dynamic_update_slice_in_dim(key_term, key_grad, first_row, 0),
            lax.dynamic_update_slice_in_dim(value_term, value_grad, first_row, 0),
        )

    back_start = (
        jnp.zeros((key_heads, stacked_rows, head_dim), jnp.float32),
        jnp.zeros((block_rows * cycle_size, key_width), jnp.float32),
        jnp.zeros((block_rows * cycle_size, key_width), jnp.float32),
    )
    grad_query, key_term, value_term = lax.fori_loop(0, cycle_size, backward_step, back_start)
    key_own, value_own = (
        lax.psum_scatter(
            key_term.astype(jnp.bfloat16), "ctx", scatter_dimension=0, tiled=True
        ).astype(jnp.float32),
        lax.psum_scatter(
            value_term.astype(jnp.bfloat16), "ctx", scatter_dimension=0, tiled=True
        ).astype(jnp.float32),
    )
    query_raw_grad, query_gain_part = query_pull(ungroup_rows(grad_query, block_rows))
    key_raw_grad, key_gain_part = key_pull(key_own)
    grad_q = query_raw_grad.astype(jnp.bfloat16)
    grad_k = key_raw_grad.astype(jnp.bfloat16)
    grad_v = value_own.astype(jnp.bfloat16)
    w_query_grad = contract_rows(normalized_input, grad_q)
    w_key_grad = contract_rows(normalized_input, grad_k)
    w_value_grad = contract_rows(normalized_input, grad_v)
    normed_part = (
        contract_cols(grad_q, w_query)
        + contract_cols(grad_k, key_weight)
        + contract_cols(grad_v, value_weight)
    )
    grad_normed, query_gain_heads, key_gain_heads = (
        lax.psum(normed_part.astype(jnp.bfloat16), "head").astype(jnp.float32),
        lax.psum(query_gain_part.astype(jnp.bfloat16), "head").astype(jnp.float32),
        lax.psum(key_gain_part.astype(jnp.bfloat16), "head").astype(jnp.float32),
    )
    input_from_norm, attention_gain_part = attention_pull(grad_normed)
    input_grad = grad_hidden_first + input_from_norm
    all_sums = (
        lax.psum_scatter(
            attention_gain_part.astype(jnp.bfloat16), ("dp", "ctx"), scatter_dimension=0, tiled=True
        ).astype(jnp.float32),
        lax.psum_scatter(
            query_gain_heads.astype(jnp.bfloat16), ("dp", "ctx"), scatter_dimension=0, tiled=True
        ).astype(jnp.float32),
        lax.psum_scatter(
            key_gain_heads.astype(jnp.bfloat16), ("dp", "ctx"), scatter_dimension=0, tiled=True
        ).astype(jnp.float32),
        lax.psum_scatter(
            w_query_grad.astype(jnp.bfloat16), ("dp", "ctx"), scatter_dimension=0, tiled=True
        ).astype(jnp.float32),
        lax.psum_scatter(
            w_key_grad.astype(jnp.bfloat16), ("dp", "ctx"), scatter_dimension=0, tiled=True
        ).astype(jnp.float32),
        lax.psum_scatter(
            w_value_grad.astype(jnp.bfloat16), ("dp", "ctx"), scatter_dimension=0, tiled=True
        ).astype(jnp.float32),
        lax.psum_scatter(
            w_out_grad.astype(jnp.bfloat16), ("dp", "ctx"), scatter_dimension=0, tiled=True
        ).astype(jnp.float32),
        lax.psum_scatter(
            feed_gain_part.astype(jnp.bfloat16), ("dp", "ctx"), scatter_dimension=0, tiled=True
        ).astype(jnp.float32),
        lax.psum_scatter(
            w_gate_grad.astype(jnp.bfloat16), ("dp", "ctx"), scatter_dimension=0, tiled=True
        ).astype(jnp.float32),
        lax.psum_scatter(
            w_up_grad.astype(jnp.bfloat16), ("dp", "ctx"), scatter_dimension=0, tiled=True
        ).astype(jnp.float32),
        lax.psum_scatter(
            w_down_grad.astype(jnp.bfloat16), ("dp", "ctx"), scatter_dimension=0, tiled=True
        ).astype(jnp.float32),
    )
    late_sums = all_sums[:7]
    feed_sum, gate_sum, up_sum, down_sum = (all_sums[7], all_sums[8], all_sums[9], all_sums[10])
    return (
        block_out,
        input_grad,
        late_sums[0],
        late_sums[1],
        late_sums[2],
        late_sums[3],
        late_sums[4],
        late_sums[5],
        late_sums[6],
        feed_sum,
        gate_sum,
        up_sum,
        down_sum,
    )


def solution(mesh):
    placed = (
        P(("dp", "ctx"), None),
        P(("dp", "ctx"), None),
        P(),
        P(),
        P(),
        P(None, "head"),
        P(None, "head"),
        P(None, "head"),
        P(None, "head"),
        P(),
        P(None, "head"),
        P(None, "head"),
        P(None, "head"),
    )
    return jax.shard_map(
        shards,
        mesh=mesh,
        in_specs=placed,
        out_specs=(
            P(("dp", "ctx"), None),
            P(("dp", "ctx"), None),
            P(("dp", "ctx")),
            P(("dp", "ctx")),
            P(("dp", "ctx")),
            P(("dp", "ctx"), "head"),
            P(("dp", "ctx"), "head"),
            P(("dp", "ctx"), "head"),
            P(("dp", "ctx"), "head"),
            P(("dp", "ctx")),
            P(("dp", "ctx"), "head"),
            P(("dp", "ctx"), "head"),
            P(("dp", "ctx"), "head"),
        ),
        check_vma=False,
    )
```

profile of v0, /device:TPU:1, one launch (start us, length us, event | category | flops | bytes accessed | tf_op | source)
XLA Modules:
  0.0 1424.6 jit_solution(530520696094865821)
XLA Ops:
  23.8 38.8 %all-gather.3.cloned.1.call-done = bf16[6144,128]{0,1:T(8,128)(2,1)} async-done(((bf16[384,128]{0,1:T(8,128)(2,1)}), bf16[6144,128]{0,1:T(8,128)(2,1)}) %all-gather.3.cloned.1.call-update) | async-done | bytes 1572880 | tf_op jit(solution)/shard_map/all_gather | solution.py:151
  62.6 46.3 %all-gather.5.cloned.1.call-done = bf16[6144,128]{1,0:T(8,128)(2,1)} async-done(((bf16[384,128]{1,0:T(8,128)(2,1)}), bf16[6144,128]{1,0:T(8,128)(2,1)}) %all-gather.5.cloned.1.call-update) | async-done | bytes 1572880 | tf_op jit(solution)/shard_map/all_gather | solution.py:152
  108.9 64.4 %conditional.2 = (f32[2,768]{1,0:T(2,128)}, f32[2,768]{1,0:T(2,128)}, f32[2,768,64]{1,2,0:T(8,128)S(1)}, f32[2,768]{1,0:T(2,128)}) conditional(s32[]{:T(128)} %bitcast.14, () %tuple.44, (s32[2,384]{1,0:T(2,128)}, bf16[6144,128]{0,1:T(8,128)(2,1)}, bf16[2,768,64]{1,2,0:T(8,128)(2,1)}, bf16[6144,128]{1,0:T(8,128)(2,1)}) %tuple.136), branch_computations={%region_3.0_spmd, %region_4.7_spmd} | conditional | flops 2524445184 | bytes 139060256 | solution.py:103
  109.6 5.6 iota_compare_fusion
  115.2 18.2 %fusion.2 = (f32[2,768]{1,0:T(2,128)S(1)}, f32[2,768,6144]{2,1,0:T(8,128)}) fusion(pred[768,6144]{1,0:T(8,128)(4,1)} %iota_compare_fusion, bf16[2,768,64]{1,2,0:T(8,128)(2,1)} %get-tuple-element.258, bf16[2,6144,64]{1,2,0:T(8,128)(2,1)} %bitcast.178), kind=kOutput, calls=%fused_computation.3 | convolution fusion | flops 1236269568 | bytes 44242944 | tf_op jit(solution)/shard_map/cond/branch_1_fun/gqd,gkd->gqk/dot_general | solution.py:87
  134.0 18.5 %fusion.4 = f32[2,768]{1,0:T(2,128)} fusion(f32[2,768,6144]{2,1,0:T(8,128)} %get-tuple-element.517, f32[2,768]{1,0:T(2,128)} %broadcast_maximum_fusion, pred[768,6144]{1,0:T(8,128)(4,1)} %iota_compare_fusion), kind=kLoop, calls=%fused_computation.5 | loop fusion | flops 37747200 | bytes 42479616 | tf_op jit(solution)/shard_map/cond/branch_1_fun/reduce_sum | solution.py:94
  155.1 16.7 %fusion.5 = f32[2,768,64]{1,2,0:T(8,128)S(1)} fusion(bf16[2,6144,64]{1,2,0:T(8,128)(2,1)} %bitcast.167, f32[2,768,6144]{2,1,0:T(8,128)} %get-tuple-element.517, f32[2,768]{1,0:T(2,128)} %broadcast_maximum_fusion, pred[768,6144]{1,0:T(8,128)(4,1)} %iota_compare_fusion), kind=kOutput, calls=%fused_computation.7 | convolution fusion | flops 1245708288 | bytes 44439552 | tf_op jit(solution)/shard_map/cond/branch_1_fun/gqk,gkd->gqd/dot_general | solution.py:95
  180.4 43.4 %all-reduce.15.cloned.1.call-done = bf16[384,1024]{1,0:T(8,128)(2,1)} async-done(((bf16[384,1024]{1,0:T(8,128)(2,1)}), bf16[384,1024]{1,0:T(8,128)(2,1)}) %all-reduce.15.cloned.1.call-update) | async-done | bytes 786448 | tf_op jit(solution)/shard_map/psum | solution.py:161
  240.9 41.5 %all-reduce.17.cloned.1.call-done = bf16[384,1024]{1,0:T(8,128)(2,1)} async-done(((bf16[384,1024]{1,0:T(8,128)(2,1)}), bf16[384,1024]{1,0:T(8,128)(2,1)}) %all-reduce.17.cloned.1.call-update) | async-done | bytes 786448 | tf_op jit(solution)/shard_map/psum | solution.py:183
  291.5 116.9 %while.18 = (s32[]{:T(128)}, f32[2,768,64]{1,2,0:T(8,128)}, bf16[6144,128]{0,1:T(8,128)(2,1)}, bf16[6144,128]{0,1:T(8,128)(2,1)}, s32[768]{0:T(1024)}, /*index=5...) while((s32[]{:T(128)}, f32[2,768,64]{1,2,0:T(8,128)}, ...), condition=%wide.region_16.17_spmd.clone, body=%wide.region_13.16_spmd.clone.sunk | while | flops 384074112 | bytes 27045424 | solution.py:262
  293.4 11.4 conditional.5
  432.3 4.4 convolution_convert_fusion.2
  444.5 191.8 %reduce-scatter.28.cloned.1.call-done = bf16[384,128]{1,0:T(8,128)(2,1)} async-done(((bf16[6144,128]{1,0:T(8,128)(2,1)}), bf16[384,128]{1,0:T(8,128)(2,1)}) %reduce-scatter.28.cloned.1.call-update) | async-done | bytes 98320
  646.2 66.0 %reduce-scatter.30.cloned.1.call-done = bf16[384,128]{1,0:T(8,128)(2,1)} async-done(((bf16[6144,128]{1,0:T(8,128)(2,1)}), bf16[384,128]{1,0:T(8,128)(2,1)}) %reduce-scatter.30.cloned.1.call-update) | async-done | bytes 98320
  719.7 72.1 %reduce-scatter.16.cloned.1.call-done = bf16[32,256]{1,0:T(8,128)(2,1)} async-done(((bf16[1024,256]{1,0:T(8,128)(2,1)}), bf16[32,256]{1,0:T(8,128)(2,1)}) %reduce-scatter.16.cloned.1.call-update) | async-done | bytes 16400 | tf_op jit(solution)/shard_map/reduce_scatter | solution.py:301
  793.2 78.4 %reduce-scatter.22.cloned.1.call-done = bf16[32,256]{1,0:T(8,128)(2,1)} async-done(((bf16[1024,256]{1,0:T(8,128)(2,1)}), bf16[32,256]{1,0:T(8,128)(2,1)}) %reduce-scatter.22.cloned.1.call-update) | async-done | bytes 16400 | tf_op jit(solution)/shard_map/reduce_scatter | solution.py:310
  872.9 80.7 %reduce-scatter.32.cloned.1.call-done = bf16[32,1152]{1,0:T(8,128)(2,1)} async-done(((bf16[1024,1152]{1,0:T(8,128)(2,1)}), bf16[32,1152]{1,0:T(8,128)(2,1)}) %reduce-scatter.32.cloned.1.call-update) | async-done | bytes 73744
  955.6 80.4 %reduce-scatter.24.cloned.1.call-done = bf16[32,1152]{1,0:T(8,128)(2,1)} async-done(((bf16[1024,1152]{1,0:T(8,128)(2,1)}), bf16[32,1152]{1,0:T(8,128)(2,1)}) %reduce-scatter.24.cloned.1.call-update) | async-done | bytes 73744 | tf_op jit(solution)/shard_map/reduce_scatter | solution.py:316
  1037.6 80.6 %reduce-scatter.26.cloned.1.call-done = bf16[32,1152]{1,0:T(8,128)(2,1)} async-done(((bf16[1024,1152]{1,0:T(8,128)(2,1)}), bf16[32,1152]{1,0:T(8,128)(2,1)}) %reduce-scatter.26.cloned.1.call-update) | async-done | bytes 73744 | tf_op jit(solution)/shard_map/reduce_scatter | solution.py:319
  1119.7 77.9 %reduce-scatter.18.cloned.1.call-done = bf16[32,128]{1,0:T(8,128)(2,1)} async-done(((bf16[1024,128]{1,0:T(8,128)(2,1)}), bf16[32,128]{1,0:T(8,128)(2,1)}) %reduce-scatter.18.cloned.1.call-update) | async-done | bytes 8208 | tf_op jit(solution)/shard_map/reduce_scatter | solution.py:304
  1199.0 78.7 %reduce-scatter.20.cloned.1.call-done = bf16[32,128]{1,0:T(8,128)(2,1)} async-done(((bf16[1024,128]{1,0:T(8,128)(2,1)}), bf16[32,128]{1,0:T(8,128)(2,1)}) %reduce-scatter.20.cloned.1.call-update) | async-done | bytes 8208 | tf_op jit(solution)/shard_map/reduce_scatter | solution.py:307
  1279.0 53.9 %all-reduce.19.cloned.1.call-done = (bf16[384,1024]{1,0:T(8,128)(2,1)}, bf16[384,1024]{1,0:T(8,128)(2,1)}) async-done(((bf16[384,1024]{1,0:T(8,128)(2,1)}, bf16[384,1024]{1,0:T(8,128)(2,1)}), (bf16[384,1024]{1,0:T(8,128)(2,1)}, bf16[384,1024]{1,0:T(8,128)(2,1)})) %all-reduce.19.cloned.1.call-update) | async-done | bytes 1572880 | tf_op jit(solution)/shard_map/psum | solution.py:172
  1334.6 69.0 %all-reduce.8 = (bf16[1024]{0:T(1024)(128)(2,1)S(1)}, bf16[64]{0:T(256)(128)(2,1)S(1)}, bf16[64]{0:T(256)(128)(2,1)S(1)}, bf16[1024]{0:T(1024)(128)(2,1)S(1)}) all-reduce(bf16[1024]{0:T(1024)(128)(2,1)S(1)} %get-tuple-element.477, bf16[64]{0:T(256)(128)(2,1)S(1)} %copy-done.56, ...), channel_id=4, replica_groups=mesh['dp'=2,'ctx'=16,'head'=4] {'dp','ctx'}, use_global_device_ids=true, to_apply=%region_24.25.clone | all-reduce | flops 2176 | bytes 8704
  1403.8 7.6 all-reduce.9
  (371 shorter events, 246.0 us)
Async XLA Ops:
  7.2 223.6 %copy-start = (bf16[1024,1152]{1,0:T(8,128)(2,1)S(1)}, bf16[1024,1152]{1,0:T(8,128)(2,1)}, u32[]{:S(2)}) copy-start(bf16[1024,1152]{1,0:T(8,128)(2,1)} %param.31) | copy-start | bytes 7077892
  7.2 55.4 %all-gather.3.cloned.1.call-start = ((), (), s32[]{:S(2)}) async-start(), calls=%async_computation.9 | async-start | bytes 1671168 | tf_op jit(solution)/shard_map/all_gather | solution.py:151
  15.3 93.6 %all-gather.5.cloned.1.call-start = ((), (), s32[]{:S(2)}) async-start(), calls=%async_computation.10 | async-start | bytes 1671168 | tf_op jit(solution)/shard_map/all_gather | solution.py:152
  17.4 206.5 %all-reduce.15.cloned.1.call-start = ((), (), s32[]{:S(2)}) async-start(), calls=%async_computation.11 | async-start | bytes 1572864 | tf_op jit(solution)/shard_map/psum | solution.py:161
  180.4 102.0 %all-reduce.17.cloned.1.call-start = ((), (), s32[]{:S(2)}) async-start(), calls=%async_computation.12 | async-start | bytes 1572864 | tf_op jit(solution)/shard_map/psum | solution.py:183
  236.9 399.4 %reduce-scatter.28.cloned.1.call-start = ((), (), s32[]{:S(2)}) async-start(), calls=%async_computation.19 | async-start | bytes 1671168
  410.9 301.3 %reduce-scatter.30.cloned.1.call-start = ((), (), s32[]{:S(2)}) async-start(), calls=%async_computation.20 | async-start | bytes 1671168
  413.7 378.2 %reduce-scatter.16.cloned.1.call-start = ((), (), s32[]{:S(2)}) async-start(), calls=%async_computation.13 | async-start | bytes 540672 | tf_op jit(solution)/shard_map/reduce_scatter | solution.py:301
  420.7 450.8 %reduce-scatter.22.cloned.1.call-start = ((), (), s32[]{:S(2)}) async-start(), calls=%async_computation.16 | async-start | bytes 540672 | tf_op jit(solution)/shard_map/reduce_scatter | solution.py:310
  423.5 530.2 %reduce-scatter.32.cloned.1.call-start = ((), (), s32[]{:S(2)}) async-start(), calls=%async_computation.21 | async-start | bytes 2433024
  432.2 603.8 %reduce-scatter.24.cloned.1.call-start = ((), (), s32[]{:S(2)}) async-start(), calls=%async_computation.17 | async-start | bytes 2433024 | tf_op jit(solution)/shard_map/reduce_scatter | solution.py:316
  436.6 681.5 %reduce-scatter.26.cloned.1.call-start = ((), (), s32[]{:S(2)}) async-start(), calls=%async_computation.18 | async-start | bytes 2433024 | tf_op jit(solution)/shard_map/reduce_scatter | solution.py:319
  441.1 196.8 %copy-start.18 = (f32[384,64]{0,1:T(8,128)S(1)}, f32[384,64]{0,1:T(8,128)}, u32[]{:S(2)}) copy-start(f32[384,64]{0,1:T(8,128)} %copy-done.17) | copy-start | bytes 294916
  441.1 197.9 %copy-start.13 = (f32[384,128]{0,1:T(8,128)S(1)}, f32[384,128]{0,1:T(8,128)}, u32[]{:S(2)}) copy-start(f32[384,128]{0,1:T(8,128)} %copy-done.12) | copy-start | bytes 589828
  441.1 197.9 %copy-start.55 = (f32[64]{0:T(128)S(1)}, f32[64]{0:T(128)}, u32[]{:S(2)}) copy-start(f32[64]{0:T(128)} %param.23) | copy-start | bytes 772
  441.1 756.6 %reduce-scatter.18.cloned.1.call-start = ((), (), s32[]{:S(2)}) async-start(), calls=%async_computation.14 | async-start | bytes 270336 | tf_op jit(solution)/shard_map/reduce_scatter | solution.py:304
  444.5 197.6 %copy-start.46 = (f32[1024]{0:T(1024)S(1)}, f32[1024]{0:T(1024)}, u32[]{:S(2)}) copy-start(f32[1024]{0:T(1024)} %param.21) | copy-start | bytes 12292
  643.4 634.3 %reduce-scatter.20.cloned.1.call-start = ((), (), s32[]{:S(2)}) async-start(), calls=%async_computation.15 | async-start | bytes 270336 | tf_op jit(solution)/shard_map/reduce_scatter | solution.py:307
  646.2 69.7 %copy-start.30 = (bf16[1024,128]{1,0:T(8,128)(2,1)S(1)}, bf16[1024,128]{1,0:T(8,128)(2,1)}, u32[]{:S(2)}) copy-start(bf16[1024,128]{1,0:T(8,128)(2,1)} %param.26) | copy-start | bytes 786436
  714.4 618.5 %all-reduce.19.cloned.1.call-start = ((), (), s32[]{:S(2)}) async-start(), calls=%async_computation.22 | async-start | bytes 3145728 | tf_op jit(solution)/shard_map/psum | solution.py:172
  717.2 617.3 %copy-start.50 = (bf16[1024]{0:T(1024)(128)(2,1)S(1)}, bf16[1024]{0:T(1024)(128)(2,1)}, u32[]{:S(2)}) copy-start(bf16[1024]{0:T(1024)(128)(2,1)} %get-tuple-element.475) | copy-start | bytes 6148
  717.2 617.3 %copy-start.56 = (bf16[64]{0:T(256)(128)(2,1)S(1)}, bf16[64]{0:T(256)(128)(2,1)}, u32[]{:S(2)}) copy-start(bf16[64]{0:T(256)(128)(2,1)} %get-tuple-element.479) | copy-start | bytes 388
  717.3 617.3 %copy-start.57 = (bf16[64]{0:T(256)(128)(2,1)S(1)}, bf16[64]{0:T(256)(128)(2,1)}, u32[]{:S(2)}) copy-start(bf16[64]{0:T(256)(128)(2,1)} %get-tuple-element.481) | copy-start | bytes 388
  717.3 686.5 %copy-start.39 = (f32[384]{0:T(512)S(1)}, f32[384]{0:T(512)}, u32[]{:S(2)}) copy-start(f32[384]{0:T(512)} %copy-done.38) | copy-start | bytes 4612
  (53 other events, 147.9 us)
Sparse Core Ops, SparseCore 0:
  15.4 47.1 all-gather.2
  65.3 43.5 all-gather.4
  180.5 43.3 all-reduce.14
  237.0 45.3 all-reduce.16
  411.1 225.1 reduce-scatter.27
  639.3 72.8 reduce-scatter.29
  715.6 76.1 reduce-scatter.15
  795.3 76.2 reduce-scatter.21
  875.2 78.4 reduce-scatter.31
  957.5 78.4 reduce-scatter.23
  1039.6 78.5 reduce-scatter.25
  1121.9 75.7 reduce-scatter.17
  1201.5 76.1 reduce-scatter.19
  1280.6 52.1 all-reduce.18
where the time goes:
time: 1430 us; the launch traced here: 1420 us
  waiting for transfers between devices  1030 us (72%)
  local copies, waits for them, and re-layouts  107 us (7%)
  other arithmetic  90.7 us (6%)
  matrix products  89.9 us (6%)
  blocking collectives  76.5 us (5%)
  between operations  17.1 us (1%)
    unnamed x17, waiting for transfers between devices  339 us
    reduce_scatter x1, waiting for transfers between devices, shards(): lax.psum_scatter(w_up_grad.astype(jnp.bfloat16), ('dp', 'ctx'), scatter_d...  80.6 us
    reduce_scatter x1, waiting for transfers between devices, shards(): lax.psum_scatter(w_gate_grad.astype(jnp.bfloat16), ('dp', 'ctx'), scatter...  80.4 us
    reduce_scatter x1, waiting for transfers between devices, shards(): lax.psum_scatter(w_value_grad.astype(jnp.bfloat16), ('dp', 'ctx'), scatte...  78.7 us
    reduce_scatter x1, waiting for transfers between devices, shards(): lax.psum_scatter(w_out_grad.astype(jnp.bfloat16), ('dp', 'ctx'), scatter_...  78.4 us
    reduce_scatter x1, waiting for transfers between devices, shards(): lax.psum_scatter(w_key_grad.astype(jnp.bfloat16), ('dp', 'ctx'), scatter_...  77.9 us
    reduce_scatter x1, waiting for transfers between devices, shards(): lax.psum_scatter(w_query_grad.astype(jnp.bfloat16), ('dp', 'ctx'), scatte...  72.1 us
    unnamed x1, blocking collectives  69 us
  transfers between devices with their start and end apart: 14, of which 14 were waited for; matrix products, arithmetic and copies ran while one was open for 5% of the time, Pallas kernels for 0%

commit v1 on v0

v1 whole, which is shorter than its diff:
```python
from functools import partial

import jax
import jax.numpy as jnp
from jax import lax
from jax.experimental import pallas as pl
from jax.experimental.pallas import tpu as pltpu
from jax.sharding import PartitionSpec as P

epsilon = 1e-05
theta_base = 1000000.0
MESH = pl.DeviceIdType.MESH
F32 = jnp.float32
BF16 = jnp.bfloat16
ROWS = 384
LOG2E = 1.4426950408889634
VMEM_LIMIT = 56 * 1024 * 1024


def rms_scale(values):
    return lax.rsqrt(jnp.mean(values * values, axis=-1, keepdims=True) + epsilon)


def row_norm(values, gain):
    return values * rms_scale(values) * gain


def rotary_tables(positions, head_dim):
    half_width = head_dim // 2
    frequency = theta_base ** (-(jnp.arange(half_width).astype(F32) * 2.0) / head_dim)
    angles = positions.astype(F32)[:, None] * frequency[None, :]
    cosine_table = jnp.cos(angles)
    sine_table = jnp.sin(angles)
    return (
        jnp.concatenate([cosine_table, cosine_table], -1),
        jnp.concatenate([sine_table, sine_table], -1),
    )


def rotate(values, cosine_table, sine_table):
    half_width = values.shape[-1] // 2
    turned = jnp.concatenate([-values[..., half_width:], values[..., :half_width]], -1)
    return values * cosine_table + turned * sine_table


def head_norm_rotate(values, gain, cosine_table, sine_table):
    shaped = values.reshape(values.shape[0], -1, gain.shape[0])
    turned = rotate(row_norm(shaped, gain), cosine_table[:, None, :], sine_table[:, None, :])
    return turned.reshape(values.shape[0], -1)


def contract_rows(left_side, right_side):
    return lax.dot_general(
        left_side, right_side, (((0,), (0,)), ((), ())), preferred_element_type=F32
    )


def contract_cols(left_side, right_side):
    return lax.dot_general(
        left_side, right_side, (((1,), (1,)), ((), ())), preferred_element_type=F32
    )


def remote(src, dst, send_sem, recv_sem, d, c, z):
    return pltpu.make_async_remote_copy(
        src_ref=src,
        dst_ref=dst,
        send_sem=send_sem,
        recv_sem=recv_sem,
        device_id=(d, c, z),
        device_id_type=MESH,
    )


def local_sem(src, dst, sem):
    return pltpu.make_async_copy(src, dst, sem)


def place():
    return lax.axis_index("dp"), lax.axis_index("ctx"), lax.axis_index("head")


def plane_barrier(d, c, z, with_z):
    barrier = pltpu.get_barrier_semaphore()

    def greet(index, carry):
        other_d, other_c = index // 16, lax.rem(index, 16)

        @pl.when((other_d != d) | (other_c != c))
        def _():
            pl.semaphore_signal(
                barrier, inc=1, device_id=(other_d, other_c, z), device_id_type=MESH
            )

        return carry

    lax.fori_loop(0, 32, greet, 0)
    count = 31
    if with_z:
        for step in (1, 3):
            pl.semaphore_signal(
                barrier, inc=1, device_id=(d, c, lax.rem(z + step, 4)), device_id_type=MESH
            )
        count += 2
    pl.semaphore_wait(barrier, count)


def role_of(d, c):
    sequence = jnp.where(c >= 8, 1, 0)
    low = jnp.where(c >= 8, 15 - c, c)
    return sequence, d, low, 15 - low


def spread_heads(pair, upper):
    pair = pair.astype(F32)
    lane = lax.broadcasted_iota(jnp.int32, pair.shape, 1)
    turned = pltpu.roll(pair, 64, 1)
    if upper:
        first, second = jnp.where(lane >= 64, turned, 0.0), jnp.where(lane >= 64, pair, 0.0)
    else:
        first, second = jnp.where(lane < 64, pair, 0.0), jnp.where(lane < 64, turned, 0.0)
    return first.astype(BF16), second.astype(BF16)


def nt(left, right):
    return lax.dot_general(left, right, (((1,), (1,)), ((), ())), preferred_element_type=F32)


def nn(left, right):
    return lax.dot_general(left, right, (((1,), (0,)), ((), ())), preferred_element_type=F32)


SCORE_SCALE = LOG2E / 8.0


def attention_forward_kernel(
    q_ref,
    kv_ref,
    wo_ref,
    kvs_ref,
    qs_ref,
    os_ref,
    l2_ref,
    oall_ref,
    wall_ref,
    qz,
    acc,
    sums,
    own_o,
    q_send,
    q_recv,
    kv_send,
    kv_recv,
    o_send,
    o_recv,
    g_send,
    g_recv,
    w_send,
    w_recv,
):
    d, c, z = place()
    s, j_role, low, high = role_of(d, c)
    own_group = low
    plane_barrier(d, c, z, True)

    slot = jnp.where(c >= 8, 1, 0)
    home = jnp.where(slot == d, c, 15 - c)
    for j in range(2):
        here = (home == c) & (d == j)

        @pl.when(jnp.logical_not(here))
        def _():
            remote(q_ref.at[j], qs_ref.at[slot], q_send.at[j], q_recv.at[slot], j, home, z).start()

        @pl.when(here)
        def _():
            local_sem(q_ref.at[j], qs_ref.at[slot], q_recv.at[slot]).start()

    def kv_target(k):
        group = lax.rem(own_group + k, 8)
        target = jnp.where(d == 0, group, 15 - group)
        return target, (15 - group) >= c

    def kv_start(k, carry):
        target, needed = kv_target(k)
        for j in range(2):
            here = (target == c) & (d == j)

            @pl.when(needed & jnp.logical_not(here))
            def _():
                remote(
                    kv_ref.at[j],
                    kvs_ref.at[c],
                    kv_send.at[2 * k + j],
                    kv_recv.at[c],
                    j,
                    target,
                    z,
                ).start()

            @pl.when(needed & here)
            def _():
                local_sem(kv_ref.at[j], kvs_ref.at[c], kv_recv.at[c]).start()

        return carry

    lax.fori_loop(0, 8, kv_start, 0)

    column = pl.ds(pl.multiple_of(z * 256, 256), 256)
    up, down = lax.rem(z + 1, 4), lax.rem(z + 3, 4)
    wall_ref[:, column] = wo_ref[...]
    w_up = remote(wall_ref.at[:, column], wall_ref.at[:, column], w_send.at[0], w_recv.at[0], d, c, up)
    w_down = remote(
        wall_ref.at[:, column], wall_ref.at[:, column], w_send.at[1], w_recv.at[1], d, c, down
    )
    w_up.start()
    w_down.start()

    acc[...] = jnp.zeros_like(acc)
    sums[...] = jnp.zeros_like(sums)
    for which in range(2):
        local_sem(q_ref.at[0], qs_ref.at[which], q_recv.at[which]).wait()
        first, second = spread_heads(qs_ref[which], False)
        qz[which, 0:ROWS, :] = first
        qz[which, ROWS : 2 * ROWS, :] = second

    def kv_wait(block):
        local_sem(kv_ref.at[0], kvs_ref.at[block], kv_recv.at[block]).wait()

    def tile(block, which, masked):
        keys = kvs_ref[block]
        for head in range(2):
            rows = slice(head * ROWS, (head + 1) * ROWS)
            weights = jnp.exp2(nt(qz[which, rows, :], keys) * SCORE_SCALE)
            if masked:
                row = lax.broadcasted_iota(jnp.int32, weights.shape, 0)
                key = lax.broadcasted_iota(jnp.int32, weights.shape, 1)
                weights = jnp.where(row >= key, weights, 0.0)
            sums[which, rows, :] += weights[:, 0:128] + weights[:, 128:256] + weights[:, 256:384]
            acc[which, rows, :] += nn(weights.astype(BF16), keys)

    kv_wait(low)
    kv_wait(high)
    tile(low, 1, False)
    tile(low, 0, True)
    tile(high, 1, True)

    def step(k, carry):
        first = lax.rem(own_group + 8 - k, 8)
        below = first < own_group
        kv_wait(first)

        @pl.when(jnp.logical_not(below))
        def _():
            kv_wait(15 - first)

        tile(first, 1, False)
        tile(jnp.where(below, first, 15 - first), jnp.where(below, 0, 1), False)
        return carry

    lax.fori_loop(1, 8, step, 0)

    lane = lax.broadcasted_iota(jnp.int32, (ROWS, 128), 1)
    for which in range(2):
        total = jnp.sum(sums[which], axis=1, keepdims=True)
        result = acc[which] / total
        os_ref[which] = jnp.where(
            lane < 64, pltpu.roll(result[:ROWS], 64, 1), result[ROWS:]
        ).astype(BF16)
        logs = jnp.broadcast_to(jnp.log2(total), (2 * ROWS, 128))
        l2_ref[which] = logs.T[0:8]
        block = high if which else low
        here = (s == d) & (block == c)

        @pl.when(jnp.logical_not(here))
        def _():
            remote(
                os_ref.at[which], own_o.at[j_role], o_send.at[which], o_recv.at[j_role], s, block, z
            ).start()

        @pl.when(here)
        def _():
            local_sem(os_ref.at[which], own_o.at[j_role], o_recv.at[j_role]).start()

    w_up.wait_recv()
    w_down.wait_recv()
    below_column = pl.ds(pl.multiple_of(down * 256, 256), 256)
    above_column = pl.ds(pl.multiple_of(up * 256, 256), 256)
    w_up2 = remote(
        wall_ref.at[0:512, below_column],
        wall_ref.at[0:512, below_column],
        w_send.at[2],
        w_recv.at[2],
        d,
        c,
        up,
    )
    w_down2 = remote(
        wall_ref.at[512:1024, above_column],
        wall_ref.at[512:1024, above_column],
        w_send.at[3],
        w_recv.at[3],
        d,
        c,
        down,
    )
    w_up2.start()
    w_down2.start()

    for j in range(2):
        local_sem(os_ref.at[0], own_o.at[j], o_recv.at[j]).wait()
        oall_ref[:, pl.ds(pl.multiple_of(z * 256 + j * 128, 128), 128)] = own_o[j]
    g_up = remote(oall_ref.at[:, column], oall_ref.at[:, column], g_send.at[0], g_recv.at[0], d, c, up)
    g_down = remote(
        oall_ref.at[:, column], oall_ref.at[:, column], g_send.at[1], g_recv.at[1], d, c, down
    )
    g_up.start()
    g_down.start()
    g_up.wait_recv()
    low_half = pl.ds(pl.multiple_of(down * 256, 128), 128)
    g_up2 = remote(
        oall_ref.at[:, low_half], oall_ref.at[:, low_half], g_send.at[2], g_recv.at[2], d, c, up
    )
    g_up2.start()
    g_down.wait_recv()
    high_half = pl.ds(pl.multiple_of(up * 256 + 128, 128), 128)
    g_down2 = remote(
        oall_ref.at[:, high_half], oall_ref.at[:, high_half], g_send.at[3], g_recv.at[3], d, c, down
    )
    g_down2.start()
    g_up2.wait_recv()
    g_down2.wait_recv()
    w_up2.wait_recv()
    w_down2.wait_recv()

    for copy in (w_up, w_down, w_up2, w_down2, g_up, g_down, g_up2, g_down2):
        copy.wait_send()
    for j in range(2):

        @pl.when(jnp.logical_not((home == c) & (d == j)))
        def _():
            remote(q_ref.at[j], qs_ref.at[slot], q_send.at[j], q_recv.at[slot], j, home, z).wait_send()

    def kv_sent(k, carry):
        target, needed = kv_target(k)
        for j in range(2):

            @pl.when(needed & jnp.logical_not((target == c) & (d == j)))
            def _():
                remote(
                    kv_ref.at[j],
                    kvs_ref.at[c],
                    kv_send.at[2 * k + j],
                    kv_recv.at[c],
                    j,
                    target,
                    z,
                ).wait_send()

        return carry

    lax.fori_loop(0, 8, kv_sent, 0)
    for which in range(2):
        block = high if which else low

        @pl.when(jnp.logical_not((s == d) & (block == c)))
        def _():
            remote(
                os_ref.at[which], own_o.at[j_role], o_send.at[which], o_recv.at[j_role], s, block, z
            ).wait_send()


def attention_backward_kernel(
    do_ref,
    kvs_ref,
    qs_ref,
    os_ref,
    l2_ref,
    dq_ref,
    dkv_ref,
    qz,
    doz,
    delta,
    dos,
    dqt,
    dq_out,
    dq_in,
    dkv_out,
    dkv_in,
    do_send,
    do_recv,
    dq_send,
    dq_recv,
    dkv_send,
    dkv_recv,
):
    d, c, z = place()
    s, j_role, low, high = role_of(d, c)
    own_group = low
    plane_barrier(d, c, z, False)

    slot = jnp.where(c >= 8, 1, 0)
    home = jnp.where(slot == d, c, 15 - c)
    for j in range(2):
        here = (home == c) & (d == j)

        @pl.when(jnp.logical_not(here))
        def _():
            remote(do_ref.at[j], dos.at[slot], do_send.at[j], do_recv.at[slot], j, home, z).start()

        @pl.when(here)
        def _():
            local_sem(do_ref.at[j], dos.at[slot], do_recv.at[slot]).start()

    dqt[...] = jnp.zeros_like(dqt)
    for which in range(2):
        first, second = spread_heads(qs_ref[which], False)
        qz[which, 0:ROWS, :] = first
        qz[which, ROWS : 2 * ROWS, :] = second
    for which in range(2):
        local_sem(do_ref.at[0], dos.at[which], do_recv.at[which]).wait()
        first, second = spread_heads(dos[which], True)
        doz[which, 0:ROWS, :] = first
        doz[which, ROWS : 2 * ROWS, :] = second
        product = (dos[which].astype(F32) * os_ref[which].astype(F32)).T
        delta[which, :, 0:ROWS] = jnp.broadcast_to(
            jnp.sum(product[0:64], axis=0, keepdims=True), (8, ROWS)
        )
        delta[which, :, ROWS : 2 * ROWS] = jnp.broadcast_to(
            jnp.sum(product[64:128], axis=0, keepdims=True), (8, ROWS)
        )

    lane = lax.broadcasted_iota(jnp.int32, (ROWS, 128), 1)
    key_scale = jnp.where(lane < 64, 0.125, 1.0)

    def tile(block, which, masked):
        keys = kvs_ref[block]
        keys_t = keys.T
        result = None
        for head in range(2):
            rows = slice(head * ROWS, (head + 1) * ROWS)
            q_rows = qz[which, rows, :]
            do_rows = doz[which, rows, :]
            weights = jnp.exp2(nt(keys, q_rows) * SCORE_SCALE - l2_ref[which, 0:1, rows])
            if masked:
                key = lax.broadcasted_iota(jnp.int32, weights.shape, 0)
                row = lax.broadcasted_iota(jnp.int32, weights.shape, 1)
                weights = jnp.where(row >= key, weights, 0.0)
            score_grad = (weights * (nt(keys, do_rows) - delta[which, 0:1, rows])).astype(BF16)
            part = nn(score_grad, q_rows) + nn(weights.astype(BF16), do_rows)
            result = part if result is None else result + part
            dqt[which, :, rows] += nn(keys_t, score_grad)
        return result * key_scale

    def send(block):
        here = (s == d) & (block == c)

        @pl.when(jnp.logical_not(here))
        def _():
            remote(
                dkv_out.at[block],
                dkv_in.at[j_role, own_group],
                dkv_send.at[block],
                dkv_recv.at[j_role, own_group],
                s,
                block,
                z,
            ).start()

        @pl.when(here)
        def _():
            local_sem(
                dkv_out.at[block], dkv_in.at[j_role, own_group], dkv_recv.at[j_role, own_group]
            ).start()

    dkv_out[low] = (tile(low, 1, False) + tile(low, 0, True)).astype(BF16)
    send(low)
    dkv_out[high] = tile(high, 1, True).astype(BF16)
    send(high)

    def step(k, carry):
        first = lax.rem(own_group + 8 - k, 8)
        below = first < own_group
        one = tile(first, 1, False)
        two = tile(jnp.where(below, first, 15 - first), jnp.where(below, 0, 1), False)

        @pl.when(below)
        def _():
            dkv_out[first] = (one + two).astype(BF16)
            send(first)

        @pl.when(jnp.logical_not(below))
        def _():
            dkv_out[first] = one.astype(BF16)
            send(first)
            dkv_out[15 - first] = two.astype(BF16)
            send(15 - first)

        return carry

    lax.fori_loop(1, 8, step, 0)

    for which in range(2):
        flat = dqt[which].T * 0.125
        dq_out[which] = jnp.where(
            lane < 64, flat[:ROWS], pltpu.roll(flat[ROWS:], 64, 1)
        ).astype(BF16)
        block = high if which else low
        here = (s == d) & (block == c)

        @pl.when(jnp.logical_not(here))
        def _():
            remote(
                dq_out.at[which], dq_in.at[j_role], dq_send.at[which], dq_recv.at[j_role], s, block, z
            ).start()

        @pl.when(here)
        def _():
            local_sem(dq_out.at[which], dq_in.at[j_role], dq_recv.at[j_role]).start()

    for j in range(2):
        dkv_ref[j] = jnp.zeros((ROWS, 128), F32)

    def collect(k, carry):
        group = lax.rem(own_group + k, 8)

        @pl.when((15 - group) >= c)
        def _():
            for j in range(2):
                local_sem(dkv_out.at[0], dkv_in.at[j, group], dkv_recv.at[j, group]).wait()
                dkv_ref[j] += dkv_in[j, group].astype(F32)

        return carry

    lax.fori_loop(0, 8, collect, 0)
    for j in range(2):
        local_sem(dq_out.at[0], dq_in.at[j], dq_recv.at[j]).wait()
        dq_ref[:, j * 128 : (j + 1) * 128] = dq_in[j]

    for j in range(2):

        @pl.when(jnp.logical_not((home == c) & (d == j)))
        def _():
            remote(
                do_ref.at[j], dos.at[slot], do_send.at[j], do_recv.at[slot], j, home, z
            ).wait_send()

    for which in range(2):
        block = high if which else low

        @pl.when(jnp.logical_not((s == d) & (block == c)))
        def _():
            remote(
                dq_out.at[which], dq_in.at[j_role], dq_send.at[which], dq_recv.at[j_role], s, block, z
            ).wait_send()

    def sent(block, carry):
        @pl.when((block <= high) & jnp.logical_not((s == d) & (block == c)))
        def _():
            remote(
                dkv_out.at[block],
                dkv_in.at[j_role, own_group],
                dkv_send.at[block],
                dkv_recv.at[j_role, own_group],
                s,
                block,
                z,
            ).wait_send()

        return carry

    lax.fori_loop(0, 16, sent, 0)


def z_barrier(d, c, z):
    barrier = pltpu.get_barrier_semaphore()
    for step in (1, 2, 3):
        pl.semaphore_signal(
            barrier, inc=1, device_id=(d, c, lax.rem(z + step, 4)), device_id_type=MESH
        )
    pl.semaphore_wait(barrier, 3)


def z_reduce_kernel(count, *refs):
    parts, outs = refs[:count], refs[count : 2 * count]
    landed, send_sem, recv_sem = refs[2 * count :]
    d, c, z = place()
    z_barrier(d, c, z)
    copies = []
    for index in range(count):
        for step in (1, 2, 3):
            other = lax.rem(z + step, 4)
            copy = remote(
                parts[index].at[other],
                landed.at[index, step - 1],
                send_sem.at[index, step - 1],
                recv_sem.at[index, step - 1],
                d,
                c,
                other,
            )
            copy.start()
            copies.append(copy)
    for index in range(count):
        for step in range(3):
            copies[index * 3 + step].wait_recv()
        outs[index][...] = (
            parts[index][z].astype(F32)
            + landed[index, 0].astype(F32)
            + landed[index, 1].astype(F32)
            + landed[index, 2].astype(F32)
        )
    for copy in copies:
        copy.wait_send()


def z_reduce(parts, collective_id):
    count = len(parts)
    return pl.pallas_call(
        partial(z_reduce_kernel, count),
        out_shape=[jax.ShapeDtypeStruct((96, 1024), F32)] * count,
        in_specs=[pl.BlockSpec(memory_space=pltpu.VMEM)] * count,
        out_specs=[pl.BlockSpec(memory_space=pltpu.VMEM)] * count,
        scratch_shapes=[
            pltpu.VMEM((count, 3, 96, 1024), BF16),
            pltpu.SemaphoreType.DMA((count, 3)),
            pltpu.SemaphoreType.DMA((count, 3)),
        ],
        compiler_params=pltpu.CompilerParams(
            collective_id=collective_id, has_side_effects=True, vmem_limit_bytes=VMEM_LIMIT
        ),
        name="z_reduce",
    )(*[part.reshape(4, 96, 1024) for part in parts])


def z_gather_kernel(count, *refs):
    parts, outs = refs[:count], refs[count : 2 * count]
    send_sem, recv_sem = refs[2 * count :]
    d, c, z = place()
    z_barrier(d, c, z)
    copies = []
    for index in range(count):
        for step in (1, 2, 3):
            copy = remote(
                parts[index],
                outs[index].at[z],
                send_sem.at[index, step - 1],
                recv_sem.at[index, step - 1],
                d,
                c,
                lax.rem(z + step, 4),
            )
            copy.start()
            copies.append(copy)
    for index in range(count):
        outs[index][z] = parts[index][...]
    for copy in copies:
        copy.wait_recv()
    for copy in copies:
        copy.wait_send()


def z_gather(parts, collective_id):
    count = len(parts)
    return pl.pallas_call(
        partial(z_gather_kernel, count),
        out_shape=[jax.ShapeDtypeStruct((4,) + part.shape, part.dtype) for part in parts],
        in_specs=[pl.BlockSpec(memory_space=pltpu.VMEM)] * count,
        out_specs=[pl.BlockSpec(memory_space=pltpu.VMEM)] * count,
        scratch_shapes=[
            pltpu.SemaphoreType.DMA((count, 3)),
            pltpu.SemaphoreType.DMA((count, 3)),
        ],
        compiler_params=pltpu.CompilerParams(
            collective_id=collective_id, has_side_effects=True, vmem_limit_bytes=VMEM_LIMIT
        ),
        name="z_gather",
    )(*parts)


def weight_reduce_kernel(items, count, *refs):
    grads, outs = refs[:count], refs[count : 2 * count]
    number = len(items)
    scratch = refs[2 * count :]
    held = scratch[0 * number : 1 * number]
    from_core = scratch[1 * number : 2 * number]
    landed = scratch[2 * number : 3 * number]
    summed = scratch[3 * number : 4 * number]
    landed_last = scratch[4 * number : 5 * number]
    load_sem, core_sems, first_sems, last_sems = scratch[5 * number :]
    d, c, z = place()
    y, x = c // 4, lax.rem(c, 4)
    barrier = pltpu.get_barrier_semaphore()
    pl.semaphore_signal(barrier, inc=1, device_id=(1 - d, c, z), device_id_type=MESH)
    for step in (1, 2, 3):
        for other in (lax.rem(y + step, 4) * 4 + x, y * 4 + lax.rem(x + step, 4)):
            pl.semaphore_signal(barrier, inc=1, device_id=(d, other, z), device_id_type=MESH)
    pl.semaphore_wait(barrier, 7)

    loads, cores = [], []
    for i, (index, start, width, y_first) in enumerate(items):
        columns = pl.ds(start, width)
        core = remote(
            grads[index].at[1 - d, :, :, :, columns],
            from_core[i],
            core_sems.at[0, i],
            core_sems.at[1, i],
            1 - d,
            c,
            z,
        )
        core.start()
        load = local_sem(grads[index].at[d, :, :, :, columns], held[i], load_sem.at[i])
        load.start()
        cores.append(core)
        loads.append(load)

    firsts = []
    for i, (index, start, width, y_first) in enumerate(items):
        loads[i].wait()
        cores[i].wait_recv()

        def add(row, carry):
            held[i][row] = (held[i][row].astype(F32) + from_core[i][row].astype(F32)).astype(BF16)
            return carry

        lax.fori_loop(0, 4, add, 0)
        copies = []
        for step in (1, 2, 3):
            if y_first:
                other = lax.rem(y + step, 4)
                source, chip = held[i].at[other], other * 4 + x
            else:
                other = lax.rem(x + step, 4)
                source, chip = held[i].at[:, other], y * 4 + other
            copy = remote(
                source,
                landed[i].at[step - 1],
                first_sems.at[0, i, step - 1],
                first_sems.at[1, i, step - 1],
                d,
                chip,
                z,
            )
            copy.start()
            copies.append(copy)
        firsts.append(copies)

    lasts = []
    for i, (index, start, width, y_first) in enumerate(items):
        for copy in firsts[i]:
            copy.wait_recv()
        own = held[i][y] if y_first else held[i][:, x]
        total = own.astype(F32)
        for step in range(3):
            total = total + landed[i][step].astype(F32)
        summed[i][...] = total.astype(BF16)
        copies = []
        for step in (1, 2, 3):
            if y_first:
                other = lax.rem(x + step, 4)
                chip = y * 4 + other
            else:
                other = lax.rem(y + step, 4)
                chip = other * 4 + x
            copy = remote(
                summed[i].at[other],
                landed_last[i].at[step - 1],
                last_sems.at[0, i, step - 1],
                last_sems.at[1, i, step - 1],
                d,
                chip,
                z,
            )
            copy.start()
            copies.append(copy)
        lasts.append(copies)

    for i, (index, start, width, y_first) in enumerate(items):
        for copy in lasts[i]:
            copy.wait_recv()
        mine = x if y_first else y
        total = summed[i][mine].astype(F32)
        for step in range(3):
            total = total + landed_last[i][step].astype(F32)
        outs[index][:, start : start + width] = total
    for i in range(number):
        cores[i].wait_send()
        for copy in firsts[i] + lasts[i]:
            copy.wait_send()


def weight_reduce(grads, items, collective_id):
    count, number = len(grads), len(items)
    widths = [grad.shape[1] for grad in grads]
    shaped = [grad.reshape(2, 4, 4, 32, width) for grad, width in zip(grads, widths)]
    scratch = []
    for lead in ((4, 4), (4, 4), (3, 4), (4,), (3,)):
        scratch += [pltpu.VMEM(lead + (32, item[2]), BF16) for item in items]
    return pl.pallas_call(
        partial(weight_reduce_kernel, items, count),
        out_shape=[jax.ShapeDtypeStruct((32, width), F32) for width in widths],
        in_specs=[pl.BlockSpec(memory_space=pl.ANY)] * count,
        out_specs=[pl.BlockSpec(memory_space=pltpu.VMEM)] * count,
        scratch_shapes=scratch
        + [
            pltpu.SemaphoreType.DMA((number,)),
            pltpu.SemaphoreType.DMA((2, number)),
            pltpu.SemaphoreType.DMA((2, number, 3)),
            pltpu.SemaphoreType.DMA((2, number, 3)),
        ],
        compiler_params=pltpu.CompilerParams(
            collective_id=collective_id, has_side_effects=True, vmem_limit_bytes=VMEM_LIMIT
        ),
        name="weight_reduce",
    )(*shaped)


EARLY_ITEMS = (
    (0, 0, 640, True),
    (0, 640, 512, False),
    (1, 0, 640, True),
    (1, 640, 512, False),
    (2, 0, 512, True),
    (2, 512, 640, False),
)
LATE_ITEMS = (
    (0, 0, 256, True),
    (3, 0, 256, False),
    (1, 0, 128, False),
    (2, 0, 128, True),
    (4, 0, 128, False),
)


def attention_forward(query_pairs, key_values, w_out):
    sems = pltpu.SemaphoreType.DMA
    vmem = pl.BlockSpec(memory_space=pltpu.VMEM)
    return pl.pallas_call(
        attention_forward_kernel,
        out_shape=[
            jax.ShapeDtypeStruct((16, ROWS, 128), BF16),
            jax.ShapeDtypeStruct((2, ROWS, 128), BF16),
            jax.ShapeDtypeStruct((2, ROWS, 128), BF16),
            jax.ShapeDtypeStruct((2, 8, 2 * ROWS), F32),
            jax.ShapeDtypeStruct((ROWS, 1024), BF16),
            jax.ShapeDtypeStruct((1024, 1024), BF16),
        ],
        in_specs=[vmem] * 3,
        out_specs=[vmem] * 6,
        scratch_shapes=[
            pltpu.VMEM((2, 2 * ROWS, 128), BF16),
            pltpu.VMEM((2, 2 * ROWS, 128), F32),
            pltpu.VMEM((2, 2 * ROWS, 128), F32),
            pltpu.VMEM((2, ROWS, 128), BF16),
            sems((2,)),
            sems((2,)),
            sems((16,)),
            sems((16,)),
            sems((2,)),
            sems((2,)),
            sems((4,)),
            sems((4,)),
            sems((4,)),
            sems((4,)),
        ],
        compiler_params=pltpu.CompilerParams(
            collective_id=1, has_side_effects=True, vmem_limit_bytes=VMEM_LIMIT
        ),
        name="attention_forward",
    )(query_pairs, key_values, w_out)


def attention_backward(dout_pairs, key_values, queries, outputs, logs):
    sems = pltpu.SemaphoreType.DMA
    vmem = pl.BlockSpec(memory_space=pltpu.VMEM)
    return pl.pallas_call(
        attention_backward_kernel,
        out_shape=[
            jax.ShapeDtypeStruct((ROWS, 256), BF16),
            jax.ShapeDtypeStruct((2, ROWS, 128), F32),
        ],
        in_specs=[vmem] * 5,
        out_specs=[vmem] * 2,
        scratch_shapes=[
            pltpu.VMEM((2, 2 * ROWS, 128), BF16),
            pltpu.VMEM((2, 2 * ROWS, 128), BF16),
            pltpu.VMEM((2, 8, 2 * ROWS), F32),
            pltpu.VMEM((2, ROWS, 128), BF16),
            pltpu.VMEM((2, 128, 2 * ROWS), F32),
            pltpu.VMEM((2, ROWS, 128), BF16),
            pltpu.VMEM((2, ROWS, 128), BF16),
            pltpu.VMEM((16, ROWS, 128), BF16),
            pltpu.VMEM((2, 8, ROWS, 128), BF16),
            sems((2,)),
            sems((2,)),
            sems((2,)),
            sems((2,)),
            sems((16,)),
            sems((2, 8)),
        ],
        compiler_params=pltpu.CompilerParams(
            collective_id=2, has_side_effects=True, vmem_limit_bytes=VMEM_LIMIT
        ),
        name="attention_backward",
    )(dout_pairs, key_values, queries, outputs, logs)


def head_pairs(values):
    return values.reshape(values.shape[0], 2, 128).transpose(1, 0, 2)


def shards(
    inputs,
    cotangent,
    attention_gain,
    query_gain,
    key_gain,
    w_query,
    key_weight,
    value_weight,
    w_out,
    feed_gain,
    w_gate,
    w_up,
    w_down,
):
    block_rows = inputs.shape[0]
    head_dim = query_gain.shape[0]
    z = lax.axis_index("head")
    positions = lax.axis_index("ctx") * block_rows + jnp.arange(block_rows, dtype=jnp.int32)
    cosine_table, sine_table = rotary_tables(positions, head_dim)
    rotate_head = partial(head_norm_rotate, cosine_table=cosine_table, sine_table=sine_table)
    input_rows = inputs.astype(F32)
    normalized_input = row_norm(input_rows, attention_gain).astype(BF16)
    query_raw = jnp.dot(normalized_input, w_query, preferred_element_type=F32)
    key_raw = jnp.dot(normalized_input, key_weight, preferred_element_type=F32)
    value_bf = jnp.dot(normalized_input, value_weight, preferred_element_type=F32).astype(BF16)
    query_rot, query_pull = jax.vjp(rotate_head, query_raw, query_gain)
    key_rot, key_pull = jax.vjp(rotate_head, key_raw, key_gain)
    key_bf = key_rot.astype(BF16)
    key_values = jnp.concatenate(
        [key_bf.reshape(block_rows, 2, head_dim), value_bf.reshape(block_rows, 2, head_dim)], -1
    ).transpose(1, 0, 2)
    role_kv, role_q, role_o, role_logs, attended, w_out_all = attention_forward(
        head_pairs(query_rot.astype(BF16)), key_values, w_out
    )
    attended_own = lax.dynamic_slice_in_dim(attended, z * 256, 256, 1)
    hidden_first = input_rows + contract_cols(attended, w_out_all)

    def own_rows(values):
        return lax.dynamic_slice_in_dim(values, z * 96, 96, 0)

    hidden_rows = own_rows(hidden_first)
    mixed = row_norm(hidden_first, feed_gain).astype(BF16)
    gate_rows = jnp.dot(mixed, w_gate, preferred_element_type=F32)
    up_rows = jnp.dot(mixed, w_up, preferred_element_type=F32)
    sigmoid_gate = jax.nn.sigmoid(gate_rows)
    silu_rows = gate_rows * sigmoid_gate
    inner_bf = (silu_rows * up_rows).astype(BF16)
    down_part = contract_cols(inner_bf, w_down)
    w_down_grad = contract_rows(cotangent, inner_bf)
    grad_inner = jnp.dot(cotangent, w_down, preferred_element_type=F32)
    grad_gate = (
        grad_inner * up_rows * sigmoid_gate * (1.0 + gate_rows * (1.0 - sigmoid_gate))
    ).astype(BF16)
    grad_up = (grad_inner * silu_rows).astype(BF16)
    w_gate_grad = contract_rows(mixed, grad_gate)
    w_up_grad = contract_rows(mixed, grad_up)
    mixed_part = contract_cols(grad_gate, w_gate) + contract_cols(grad_up, w_up)
    down_rows, grad_mixed_rows = z_reduce([down_part.astype(BF16), mixed_part.astype(BF16)], 3)
    block_out_rows = (hidden_rows + down_rows).astype(BF16)
    _, feed_pull = jax.vjp(row_norm, hidden_rows, feed_gain)
    hidden_from_norm, feed_gain_part = feed_pull(grad_mixed_rows)
    grad_hidden_rows = own_rows(cotangent).astype(F32) + hidden_from_norm
    block_out, grad_branch = z_gather([block_out_rows, grad_hidden_rows.astype(BF16)], 4)
    block_out = block_out.reshape(block_rows, -1)
    grad_branch = grad_branch.reshape(block_rows, -1)
    gate_sum, up_sum, down_sum = weight_reduce(
        [w_gate_grad.astype(BF16), w_up_grad.astype(BF16), w_down_grad.astype(BF16)],
        EARLY_ITEMS,
        5,
    )
    w_out_grad = contract_rows(grad_branch, attended_own)
    grad_attended = jnp.dot(grad_branch, w_out, preferred_element_type=F32).astype(BF16)
    grad_query, grad_kv = attention_backward(
        head_pairs(grad_attended), role_kv, role_q, role_o, role_logs
    )
    grad_key = grad_kv[:, :, :head_dim].transpose(1, 0, 2).reshape(block_rows, -1)
    grad_v = grad_kv[:, :, head_dim:].transpose(1, 0, 2).reshape(block_rows, -1).astype(BF16)
    query_raw_grad, query_gain_part = query_pull(grad_query.astype(F32))
    key_raw_grad, key_gain_part = key_pull(grad_key)
    grad_q = query_raw_grad.astype(BF16)
    grad_k = key_raw_grad.astype(BF16)
    w_query_grad = contract_rows(normalized_input, grad_q)
    w_key_grad = contract_rows(normalized_input, grad_k)
    w_value_grad = contract_rows(normalized_input, grad_v)
    normed_part = (
        contract_cols(grad_q, w_query)
        + contract_cols(grad_k, key_weight)
        + contract_cols(grad_v, value_weight)
    )
    (grad_normed_rows,) = z_reduce([normed_part.astype(BF16)], 6)
    _, attention_pull = jax.vjp(row_norm, own_rows(input_rows), attention_gain)
    input_from_norm, attention_gain_part = attention_pull(grad_normed_rows)
    input_grad_rows = grad_hidden_rows + input_from_norm
    gains = jnp.zeros((8, 1024), F32)
    gains = gains.at[0].set(attention_gain_part).at[1].set(feed_gain_part)
    gains = gains.at[2, :64].set(query_gain_part).at[3, :64].set(key_gain_part)
    input_grad, gains = z_gather([input_grad_rows.astype(BF16), gains], 7)
    input_grad = input_grad.reshape(block_rows, -1).astype(F32)
    gains = jnp.sum(gains, axis=0)

    def two_per_device(vector):
        return jnp.pad(vector[:64].reshape(32, 2), ((0, 0), (0, 30))).reshape(1024)

    chunk = jnp.stack(
        [gains[0], gains[1], two_per_device(gains[2]), two_per_device(gains[3])], axis=1
    )
    chunk = jnp.pad(chunk, ((0, 0), (0, 124)))
    query_sum, key_sum, value_sum, out_sum, gain_sum = weight_reduce(
        [
            w_query_grad.astype(BF16),
            w_key_grad.astype(BF16),
            w_value_grad.astype(BF16),
            w_out_grad.astype(BF16),
            chunk.astype(BF16),
        ],
        LATE_ITEMS,
        8,
    )
    return (
        block_out,
        input_grad,
        gain_sum[:, 0],
        gain_sum[:2, 2],
        gain_sum[:2, 3],
        query_sum,
        key_sum,
        value_sum,
        out_sum,
        gain_sum[:, 1],
        gate_sum,
        up_sum,
        down_sum,
    )


def solution(mesh):
    both = ("dp", "ctx")
    by_head = P(None, "head")
    reduced = P(both, "head")
    return jax.shard_map(
        shards,
        mesh=mesh,
        in_specs=(
            P(both, None),
            P(both, None),
            P(),
            P(),
            P(),
            by_head,
            by_head,
            by_head,
            by_head,
            P(),
            by_head,
            by_head,
            by_head,
        ),
        out_specs=(
            P(both, None),
            P(both, None),
            P(both),
            P(both),
            P(both),
            reduced,
            reduced,
            reduced,
            reduced,
            P(both),
            reduced,
            reduced,
            reduced,
        ),
        check_vma=False,
    )
```

time: 1430 us -> 324 us (0.23)
  waiting for transfers between devices: 1030 us -> 0 us
  Pallas kernels: 0 us -> 224 us
  local copies, waits for them, and re-layouts: 107 us -> 28.2 us
  blocking collectives: 76.5 us -> 0 us
  other arithmetic: 90.7 us -> 26.7 us
  matrix products: 89.9 us -> 42.8 us
  between operations: 17.1 us -> 1.57 us
    reduce_scatter x6 -> x0, waiting for transfers between devices: 468 us -> none  [the longest x1 80.6 us: shards(): lax.psum_scatter(w_up_grad.astype(jnp.bfloat16), ('dp', 'ctx'), scatter_d...]
    unnamed x17 -> x0, waiting for transfers between devices: 339 us -> none
    pallas_call x0 -> x8, Pallas kernels: none -> 224 us  [the longest x1 56.5 us: attention_forward(): pl.pallas_call(attention_forward_kernel, out_shape=[jax.ShapeDtypeStruct(...]
    psum x3 -> x0, waiting for transfers between devices: 139 us -> none  [the longest x1 53.9 us: shards(): lax.psum(down_part.astype(jnp.bfloat16), 'head').astype(jnp.float32)]
    all_gather x2 -> x0, waiting for transfers between devices: 85 us -> none  [the longest x1 46.3 us: shards(): lax.all_gather(value_bf, 'ctx', axis=0, tiled=True)]
    unnamed x1 -> x0, blocking collectives: 69 us -> none
    dot_general x14 -> x7, matrix products: 55.1 us -> 11.7 us  [the longest x1 2.13 us: shards(): key_raw = jnp.dot(normalized_input, key_weight, preferred_element_type=F32)]
    add x21 -> x0, other arithmetic: 33.9 us -> none  [the longest x16 27.8 us: backward_step(): grad_query + query_add]
  transfers between devices with their start and end apart: 14 -> 0, of which waited for: 14 -> 0; matrix products, arithmetic and copies ran while one was open for 5% -> 0% of each run, Pallas kernels for 0% -> 0%
where the time goes in v1:
time: 324 us; the launch traced here: 323 us
  Pallas kernels  224 us (69%)
  matrix products  42.8 us (13%)
  local copies, waits for them, and re-layouts  28.2 us (9%)
  other arithmetic  26.7 us (8%)
    pallas_call x1, Pallas kernels, attention_forward(): pl.pallas_call(attention_forward_kernel, out_shape=[jax.ShapeDtypeStruct(...  56.5 us
    pallas_call x2, Pallas kernels, weight_reduce(): pl.pallas_call(partial(weight_reduce_kernel, items, count), out_shape=[ja...  50.4 us
    pallas_call x1, Pallas kernels, attention_backward(): pl.pallas_call(attention_backward_kernel, out_shape=[jax.ShapeDtypeStruct...  41.4 us
    pallas_call x2, Pallas kernels, z_reduce(): pl.pallas_call(partial(z_reduce_kernel, count), out_shape=[jax.ShapeDtype...  38 us
    pallas_call x2, Pallas kernels, z_gather(): pl.pallas_call(partial(z_gather_kernel, count), out_shape=[jax.ShapeDtype...  37.2 us
    dot_general x7, matrix products, contract_cols(): lax.dot_general(left_side, right_side, (((1,), (1,)), ((), ())), preferre...  15.9 us
    dot_general x7, matrix products, contract_rows(): lax.dot_general(left_side, right_side, (((0,), (0,)), ((), ())), preferre...  15.2 us
    unnamed x131, local copies, waits for them, and re-layouts  10.4 us

profile of v1, /device:TPU:1, one launch (start us, length us, event | category | flops | bytes accessed | tf_op | source)
XLA Modules:
  0.0 322.8 jit_solution(3608427026276953214)
XLA Ops:
  17.0 2.1 convolution_convert_fusion.9
  20.8 2.1 multiply_reduce_fusion.13
  30.2 56.5 %attention_forward.1 = (bf16[16,384,128]{2,1,0:T(8,128)(2,1)}, bf16[2,384,128]{2,1,0:T(8,128)(2,1)}, bf16[2,384,128]{2,1,0:T(8,128)(2,1)}, f32[2,8,768]{2,1,0:T(...) custom-call(bf16[2,384,128]{2,1,0:T(8,128)(2,1)} %bitcast.127, ...), custom_call_target="tpu_custom_call" | custom-call | tf_op jit(solution)/shard_map/attention_forward/pallas_call | solution.py:839
  86.7 3.1 multiply_reduce_fusion
  90.1 2.0 copy-done.53
  96.9 2.1 convolution_convert_fusion.3
  100.2 2.1 add_convert_fusion.1
  102.4 24.0 %z_reduce.2 = (f32[96,1024]{1,0:T(8,128)}, f32[96,1024]{1,0:T(8,128)}) custom-call(bf16[4,96,1024]{2,1,0:T(8,128)(2,1)} %bitcast.133, bf16[4,96,1024]{2,1,0:T(8,128)(2,1)} %bitcast.134), custom_call_target="tpu_custom_call" | custom-call | tf_op jit(solution)/shard_map/z_reduce/pallas_call | solution.py:619
  127.5 1.9 multiply_reduce_fusion.4
  129.4 2.1 fusion.18
  131.5 22.2 %z_gather.2 = (bf16[4,96,1024]{2,1,0:T(8,128)(2,1)}, bf16[4,96,1024]{2,1,0:T(8,128)(2,1)}) custom-call(bf16[96,1024]{1,0:T(8,128)(2,1)} %get-tuple-element.125.refs_0_, bf16[96,1024]{1,0:T(8,128)(2,1)} %get-tuple-element.124.refs_1_), custom_call_target="tpu_custom_call" | custom-call | tf_op jit(solution)/shard_map/z_gather/pallas_call | solution.py:665
  156.3 41.4 %attention_backward.1 = (bf16[384,256]{1,0:T(8,128)(2,1)}, f32[2,384,128]{2,1,0:T(8,128)}) custom-call(bf16[2,384,128]{2,1,0:T(8,128)(2,1)} %bitcast.128, bf16[16,384,128]{2,1,0:T(8,128)(2,1)} %get-tuple-element.89.kvs_ref, bf16[2,384,128]{2,1,0:T(8,128)(2,1)} %get-tuple-element.90.qs_ref, bf16[2,384,128]{2,1,0:T(8,128)(2,1)} %get-tuple-element.91.os_ref, ...), custom_call_target="tpu_custom_call" | custom-call | tf_op jit(solution)/shard_map/attention_backward/pallas_call | solution.py:877
  205.2 2.6 fusion.28
  208.1 3.2 add_convert_fusion
  211.3 14.1 %z_reduce.3 = f32[96,1024]{1,0:T(8,128)} custom-call(bf16[4,96,1024]{2,1,0:T(8,128)(2,1)} %bitcast.120), custom_call_target="tpu_custom_call" | custom-call | tf_op jit(solution)/shard_map/z_reduce/pallas_call | solution.py:619
  226.5 2.0 fusion.5.refs_0_
  229.8 15.0 %z_gather.3 = (bf16[4,96,1024]{2,1,0:T(8,128)(2,1)}, f32[4,8,1024]{2,1,0:T(8,128)}) custom-call(bf16[96,1024]{1,0:T(8,128)(2,1)} %fusion.5.refs_0_, f32[8,1024]{1,0:T(8,128)} %copy-done.27), custom_call_target="tpu_custom_call" | custom-call | tf_op jit(solution)/shard_map/z_gather/pallas_call | solution.py:665
  244.8 2.5 bitcast_convert_fusion
  251.1 2.5 convolution_convert_fusion.4
  255.1 17.6 %weight_reduce.2 = (f32[32,256]{1,0:T(8,128)}, f32[32,128]{1,0:T(8,128)}, f32[32,128]{1,0:T(8,128)}, f32[32,256]{1,0:T(8,128)}, f32[32,128]{1,0:T(8,128)}) custom-call(bf16[2,4,4,32,256]{4,3,2,1,0:T(8,128)(2,1)} %bitcast.137, bf16[2,4,4,32,128]{4,3,2,1,0:T(8,128)(2,1)} %bitcast.144, bf16[2,4,4,32,128]{4,3,2,1,0:T(8,128)(2,1)} %bitcast.145, ...), custom_call_target="tpu_custom_call" | custom-call | tf_op jit(solution)/shard_map/weight_reduce/pallas_call | solution.py:800
  275.7 3.0 convolution_convert_fusion.2
  278.6 2.9 convolution_convert_fusion.1
  281.5 3.0 convolution_convert_fusion
  284.5 32.9 %weight_reduce.3 = (f32[32,1152]{1,0:T(8,128)}, f32[32,1152]{1,0:T(8,128)}, f32[32,1152]{1,0:T(8,128)}) custom-call(bf16[2,4,4,32,1152]{4,3,2,1,0:T(8,128)(2,1)} %bitcast.121, bf16[2,4,4,32,1152]{4,3,2,1,0:T(8,128)(2,1)} %bitcast.122, bf16[2,4,4,32,1152]{4,3,2,1,0:T(8,128)(2,1)} %bitcast.123), custom_call_target="tpu_custom_call" | custom-call | tf_op jit(solution)/shard_map/weight_reduce/pallas_call | solution.py:800
  (210 shorter events, 58.6 us)
Async XLA Ops:
  0.6 94.6 %copy-start = (bf16[1024,1152]{1,0:T(8,128)(2,1)S(1)}, bf16[1024,1152]{1,0:T(8,128)(2,1)}, u32[]{:S(2)}) copy-start(bf16[1024,1152]{1,0:T(8,128)(2,1)} %param.33) | copy-start | bytes 7077892
  0.7 3.5 %copy-start.41 = (f32[64]{0:T(128)S(1)}, f32[64]{0:T(128)}, u32[]{:S(2)}) copy-start(f32[64]{0:T(128)} %param.24) | copy-start | bytes 772
  6.8 10.2 %copy-start.4 = (bf16[384,1024]{1,0:T(8,128)(2,1)S(1)}, bf16[384,1024]{1,0:T(8,128)(2,1)}, u32[]{:S(2)}) copy-start(bf16[384,1024]{1,0:T(8,128)(2,1)} %param.21) | copy-start | bytes 2359300
  6.8 10.2 %copy-start.34 = (f32[1024]{0:T(1024)S(1)}, f32[1024]{0:T(1024)}, u32[]{:S(2)}) copy-start(f32[1024]{0:T(1024)} %param.23) | copy-start | bytes 12292
  22.9 3.1 copy-start.39
  86.7 3.2 copy-start.29
  89.8 3.4 %copy-start.1 = (f32[384,1024]{1,0:T(8,128)}, f32[384,1024]{1,0:T(8,128)S(1)}, u32[]{:S(2)}) copy-start(f32[384,1024]{1,0:T(8,128)S(1)} %get-tuple-element.143) | copy-start | bytes 4718596
  96.9 3.3 %copy-start.55 = (bf16[384,1152]{1,0:T(8,128)(2,1)}, bf16[384,1152]{1,0:T(8,128)(2,1)S(1)}, u32[]{:S(2)}) copy-start(bf16[384,1152]{1,0:T(8,128)(2,1)S(1)} %get-tuple-element.121) | copy-start | bytes 2654212
  127.5 26.3 %copy-start.9 = (bf16[1024,256]{1,0:T(8,128)(2,1)S(1)}, bf16[1024,256]{1,0:T(8,128)(2,1)}, u32[]{:S(2)}) copy-start(bf16[1024,256]{1,0:T(8,128)(2,1)} %wo_ref.1) | copy-start | bytes 1572868
  127.5 26.3 %copy-start.45 = (f32[96]{0:T(128)}, f32[96]{0:T(128)S(1)}, u32[]{:S(2)}) copy-start(f32[96]{0:T(128)S(1)} %fusion.16) | copy-start | bytes 1156
  129.4 24.4 %copy-start.47 = (f32[96]{0:T(128)}, f32[96]{0:T(128)S(1)}, u32[]{:S(2)}) copy-start(f32[96]{0:T(128)S(1)} %multiply_multiply_fusion.5) | copy-start | bytes 1156
  205.1 3.0 copy-start.21
  211.3 14.1 %copy-start.5 = (bf16[384,1024]{1,0:T(8,128)(2,1)S(1)}, bf16[384,1024]{1,0:T(8,128)(2,1)}, u32[]{:S(2)}) copy-start(bf16[384,1024]{1,0:T(8,128)(2,1)} %param.21) | copy-start | bytes 2359300
  225.6 3.1 copy-start.49
  225.6 3.3 %copy-start.50 = (f32[64]{0:T(128)S(1)}, f32[64]{0:T(128)}, u32[]{:S(2)}) copy-start(f32[64]{0:T(128)} %get-tuple-element.109) | copy-start | bytes 772
  228.5 18.7 %copy-start.14 = (bf16[384,4,64]{0,2,1:T(8,128)(2,1)S(1)}, bf16[384,4,64]{0,2,1:T(8,128)(2,1)}, u32[]{:S(2)}) copy-start(bf16[384,4,64]{0,2,1:T(8,128)(2,1)} %copy-done.13) | copy-start | bytes 589828
  228.5 18.7 %copy-start.52 = (f32[384]{0:T(512)S(1)}, f32[384]{0:T(512)}, u32[]{:S(2)}) copy-start(f32[384]{0:T(512)} %copy-done.51) | copy-start | bytes 4612
  253.6 22.1 %copy-start.17 = (bf16[384,1024]{1,0:T(8,128)(2,1)S(1)}, bf16[384,1024]{1,0:T(8,128)(2,1)}, u32[]{:S(2)}) copy-start(bf16[384,1024]{1,0:T(8,128)(2,1)} %copy-done.16) | copy-start | bytes 2359300
  254.3 21.3 %copy-start.58 = (bf16[384,1152]{1,0:T(8,128)(2,1)S(1)}, bf16[384,1152]{1,0:T(8,128)(2,1)}, u32[]{:S(2)}) copy-start(bf16[384,1152]{1,0:T(8,128)(2,1)} %copy-done.57) | copy-start | bytes 2654212
  275.7 3.0 copy-start.56
  284.5 32.9 %copy-start.15 = (bf16[4,96,1024]{2,1,0:T(8,128)(2,1)S(1)}, bf16[4,96,1024]{2,1,0:T(8,128)(2,1)}, u32[]{:S(2)}) copy-start(bf16[4,96,1024]{2,1,0:T(8,128)(2,1)} %get-tuple-element.87) | copy-start | bytes 2359300
  317.4 3.4 %copy-start.26 = (f32[32,1152]{1,0:T(8,128)S(1)}, f32[32,1152]{1,0:T(8,128)}, u32[]{:S(2)}) copy-start(f32[32,1152]{1,0:T(8,128)} %get-tuple-element.169) | copy-start | bytes 442372
  317.4 4.0 %copy-start.25 = (f32[32,1152]{1,0:T(8,128)S(1)}, f32[32,1152]{1,0:T(8,128)}, u32[]{:S(2)}) copy-start(f32[32,1152]{1,0:T(8,128)} %get-tuple-element.170) | copy-start | bytes 442372
  317.4 4.7 %copy-start.24 = (f32[32,1152]{1,0:T(8,128)S(1)}, f32[32,1152]{1,0:T(8,128)}, u32[]{:S(2)}) copy-start(f32[32,1152]{1,0:T(8,128)} %get-tuple-element.171) | copy-start | bytes 442372
  (37 other events, 65.9 us)

commit v2 on v1

v2 whole, which is shorter than its diff:
```python
from functools import partial

import jax
import jax.numpy as jnp
import numpy as np
from jax import lax
from jax.experimental import pallas as pl
from jax.experimental.pallas import tpu as pltpu
from jax.sharding import PartitionSpec as P

epsilon = 1e-05
theta_base = 1000000.0
MESH = pl.DeviceIdType.MESH
F32 = jnp.float32
BF16 = jnp.bfloat16
ROWS = 384
LOG2E = 1.4426950408889634
VMEM_LIMIT = 56 * 1024 * 1024


def remote(src, dst, send_sem, recv_sem, d, c, z):
    return pltpu.make_async_remote_copy(
        src_ref=src,
        dst_ref=dst,
        send_sem=send_sem,
        recv_sem=recv_sem,
        device_id=(d, c, z),
        device_id_type=MESH,
    )


def local_sem(src, dst, sem):
    return pltpu.make_async_copy(src, dst, sem)


def place():
    return lax.axis_index("dp"), lax.axis_index("ctx"), lax.axis_index("head")


def role_of(d, c):
    sequence = jnp.where(c >= 8, 1, 0)
    low = jnp.where(c >= 8, 15 - c, c)
    return sequence, d, low, 15 - low


def spread_heads(pair, upper):
    pair = pair.astype(F32)
    lane = lax.broadcasted_iota(jnp.int32, pair.shape, 1)
    turned = pltpu.roll(pair, 64, 1)
    if upper:
        first, second = jnp.where(lane >= 64, turned, 0.0), jnp.where(lane >= 64, pair, 0.0)
    else:
        first, second = jnp.where(lane < 64, pair, 0.0), jnp.where(lane < 64, turned, 0.0)
    return first.astype(BF16), second.astype(BF16)


def nt(left, right):
    return lax.dot_general(left, right, (((1,), (1,)), ((), ())), preferred_element_type=F32)


def nn(left, right):
    return lax.dot_general(left, right, (((1,), (0,)), ((), ())), preferred_element_type=F32)


SCORE_SCALE = LOG2E / 8.0


def split_columns(half_width=32, rows=ROWS, blocks=16):
    lane = np.arange(128) % half_width
    frequency = theta_base ** (-2.0 * lane / (2 * half_width))
    row_angle = np.arange(rows)[:, None] * frequency[None, :]
    block_angle = (np.arange(blocks) * rows)[:, None] * frequency[None, :]
    return [
        np.asarray(table, np.float32)
        for table in (
            np.cos(row_angle),
            np.sin(row_angle),
            np.cos(block_angle),
            np.sin(block_angle),
        )
    ]


def tables(c, row_cos, row_sin, block_cos, block_sin):
    bc, bs = block_cos[pl.ds(c, 1), :], block_sin[pl.ds(c, 1), :]
    rc, rs = row_cos[...], row_sin[...]
    return rc * bc - rs * bs, rs * bc + rc * bs


def lanes(rows=ROWS):
    return lax.broadcasted_iota(jnp.int32, (rows, 128), 1)


def half_sums(values):
    lane = lanes(values.shape[0])
    first = jnp.sum(jnp.where(lane < 64, values, 0.0), axis=1, keepdims=True)
    second = jnp.sum(jnp.where(lane >= 64, values, 0.0), axis=1, keepdims=True)
    return jnp.where(lane < 64, first, second)


def turn(values):
    lane = lanes(values.shape[0])
    return jnp.where(lax.rem(lane, 64) < 32, -pltpu.roll(values, 96, 1), pltpu.roll(values, 32, 1))


def turn_back(values):
    lane = lanes(values.shape[0])
    return jnp.where(lax.rem(lane, 64) < 32, pltpu.roll(values, 96, 1), -pltpu.roll(values, 32, 1))


def pair_forward(raw, gain, cosine, sine):
    scale = lax.rsqrt(half_sums(raw * raw) * (1.0 / 64.0) + epsilon)
    normed = raw * scale * gain
    return normed * cosine + turn(normed) * sine


def pair_backward(grad, raw, gain, cosine, sine):
    incoming = grad * cosine + turn_back(grad * sine)
    scale = lax.rsqrt(half_sums(raw * raw) * (1.0 / 64.0) + epsilon)
    weighted = incoming * gain
    inner = half_sums(weighted * raw) * (1.0 / 64.0)
    raw_grad = scale * weighted - raw * (scale * scale * scale) * inner
    return raw_grad, jnp.sum(incoming * raw * scale, axis=0, keepdims=True)


def attention_forward_kernel(
    x_ref,
    gain_ref,
    wq_ref,
    wk_ref,
    wv_ref,
    qgain_ref,
    kgain_ref,
    row_cos,
    row_sin,
    block_cos,
    block_sin,
    wo_ref,
    kvs_ref,
    qs_ref,
    os_ref,
    l2_ref,
    oall_ref,
    wall_ref,
    normed_ref,
    qraw_ref,
    kraw_ref,
    q_ref,
    kv_ref,
    qz,
    acc,
    sums,
    q_send,
    q_recv,
    kv_send,
    kv_recv,
    o_send,
    o_recv,
    w_send,
    w_recv,
    wc_send,
    wc_recv,
):
    d, c, z = place()
    s, j_role, low, high = role_of(d, c)
    own_group = low
    slot = jnp.where(c >= 8, 1, 0)
    home = jnp.where(slot == d, c, 15 - c)

    barrier = pltpu.get_barrier_semaphore()

    def greet(index, carry):
        other_d, other_c = index // 16, lax.rem(index, 16)

        @pl.when((other_d != d) | (other_c != c))
        def _():
            pl.semaphore_signal(
                barrier, inc=1, device_id=(other_d, other_c, z), device_id_type=MESH
            )

        return carry

    lax.fori_loop(0, 32, greet, 0)
    for step in (1, 2, 3):
        other = lax.rem(z + step, 4)
        pl.semaphore_signal(barrier, inc=1, device_id=(d, c, other), device_id_type=MESH)
        for j in range(2):
            pl.semaphore_signal(barrier, inc=1, device_id=(j, home, other), device_id_type=MESH)

    x = x_ref[...].astype(F32)
    scale = lax.rsqrt(jnp.mean(x * x, axis=1, keepdims=True) + epsilon)
    normed_ref[...] = (x * scale * gain_ref[...]).astype(BF16)
    normed = normed_ref[...]
    cosine, sine = tables(c, row_cos, row_sin, block_cos, block_sin)
    key_raw = nn(normed, wk_ref[...])
    kraw_ref[...] = key_raw
    value = nn(normed, wv_ref[...])
    key = pair_forward(key_raw, kgain_ref[...], cosine, sine)
    lane = lanes()
    kv_ref[0] = jnp.where(lane < 64, key, pltpu.roll(value, 64, 1)).astype(BF16)
    kv_ref[1] = jnp.where(lane < 64, pltpu.roll(key, 64, 1), value).astype(BF16)
    pl.semaphore_wait(barrier, 31 + 3 + 6)

    def kv_target(k):
        group = lax.rem(own_group + k, 8)
        target = jnp.where(d == 0, group, 15 - group)
        return target, (15 - group) >= c

    def kv_copy(k, j, target):
        return remote(
            kv_ref.at[j], kvs_ref.at[c], kv_send.at[2 * k + j], kv_recv.at[c], j, target, z
        )

    def kv_start(k, carry):
        target, needed = kv_target(k)
        for j in range(2):
            here = (target == c) & (d == j)

            @pl.when(needed & jnp.logical_not(here))
            def _():
                kv_copy(k, j, target).start()

            @pl.when(needed & here)
            def _():
                local_sem(kv_ref.at[j], kvs_ref.at[c], kv_recv.at[c]).start()

        return carry

    kv_start(0, 0)
    query_raw = nn(normed, wq_ref[...])
    qraw_ref[...] = query_raw
    for j in range(2):
        pair = query_raw[:, j * 128 : (j + 1) * 128]
        q_ref[j] = pair_forward(pair, qgain_ref[...], cosine, sine).astype(BF16)
        here = (home == c) & (d == j)

        @pl.when(jnp.logical_not(here))
        def _():
            remote(q_ref.at[j], qs_ref.at[slot], q_send.at[j], q_recv.at[slot], j, home, z).start()

        @pl.when(here)
        def _():
            local_sem(q_ref.at[j], qs_ref.at[slot], q_recv.at[slot]).start()

    lax.fori_loop(1, 8, kv_start, 0)

    column = pl.ds(pl.multiple_of(z * 256, 256), 256)
    mine = pl.ds(pl.multiple_of(d * 512, 512), 512)
    wall_ref[:, column] = wo_ref[...]
    w_copies = []
    for step in (1, 2, 3):
        copy = remote(
            wall_ref.at[mine, column],
            wall_ref.at[mine, column],
            w_send.at[step - 1],
            w_recv.at[step - 1],
            d,
            c,
            lax.rem(z + step, 4),
        )
        copy.start()
        w_copies.append(copy)

    acc[...] = jnp.zeros_like(acc)
    sums[...] = jnp.zeros_like(sums)
    for which in range(2):
        local_sem(q_ref.at[0], qs_ref.at[which], q_recv.at[which]).wait()
        first, second = spread_heads(qs_ref[which], False)
        qz[which, 0:ROWS, :] = first
        qz[which, ROWS : 2 * ROWS, :] = second

    def kv_wait(block):
        local_sem(kv_ref.at[0], kvs_ref.at[block], kv_recv.at[block]).wait()

    def tile(block, which, masked):
        keys = kvs_ref[block]
        for head in range(2):
            rows = slice(head * ROWS, (head + 1) * ROWS)
            weights = jnp.exp2(nt(qz[which, rows, :], keys) * SCORE_SCALE)
            if masked:
                row = lax.broadcasted_iota(jnp.int32, weights.shape, 0)
                key = lax.broadcasted_iota(jnp.int32, weights.shape, 1)
                weights = jnp.where(row >= key, weights, 0.0)
            sums[which, rows, :] += weights[:, 0:128] + weights[:, 128:256] + weights[:, 256:384]
            acc[which, rows, :] += nn(weights.astype(BF16), keys)

    kv_wait(low)
    kv_wait(high)
    tile(low, 1, False)
    tile(low, 0, True)
    tile(high, 1, True)

    def step(k, carry):
        first = lax.rem(own_group + 8 - k, 8)
        below = first < own_group
        kv_wait(first)

        @pl.when(jnp.logical_not(below))
        def _():
            kv_wait(15 - first)

        tile(first, 1, False)
        tile(jnp.where(below, first, 15 - first), jnp.where(below, 0, 1), False)
        return carry

    lax.fori_loop(1, 8, step, 0)

    def o_copy(which, step):
        block = high if which else low
        other = lax.rem(z + step, 4)
        there = oall_ref.at[:, pl.ds(pl.multiple_of(z * 256 + j_role * 128, 128), 128)]
        arrived = o_recv.at[z * 2 + j_role]
        return os_ref.at[which], there, o_send.at[which, step], arrived, s, block, other

    for which in range(2):
        total = jnp.sum(sums[which], axis=1, keepdims=True)
        result = acc[which] / total
        os_ref[which] = jnp.where(
            lane < 64, pltpu.roll(result[:ROWS], 64, 1), result[ROWS:]
        ).astype(BF16)
        block = high if which else low
        here = (s == d) & (block == c)
        for step in (2, 1, 3):
            remote(*o_copy(which, step)).start()

        @pl.when(jnp.logical_not(here))
        def _():
            remote(*o_copy(which, 0)).start()

        @pl.when(here)
        def _():
            source, there, _, arrived = o_copy(which, 0)[:4]
            local_sem(source, there, arrived).start()

        logs = jnp.broadcast_to(jnp.log2(total), (2 * ROWS, 128))
        l2_ref[which] = logs.T[0:8]

    forwards = []
    for step in (1, 2, 3):
        w_copies[step - 1].wait_recv()
        other = pl.ds(pl.multiple_of(lax.rem(z + 4 - step, 4) * 256, 256), 256)
        copy = remote(
            wall_ref.at[mine, other],
            wall_ref.at[mine, other],
            wc_send.at[step - 1],
            wc_recv.at[step - 1],
            1 - d,
            c,
            z,
        )
        copy.start()
        forwards.append(copy)
    for copy in forwards:
        copy.wait_recv()
    for source in range(4):
        for j in range(2):
            there = oall_ref.at[:, source * 256 + j * 128 : source * 256 + (j + 1) * 128]
            local_sem(os_ref.at[0], there, o_recv.at[source * 2 + j]).wait()

    for copy in w_copies + forwards:
        copy.wait_send()
    for j in range(2):

        @pl.when(jnp.logical_not((home == c) & (d == j)))
        def _():
            remote(q_ref.at[j], qs_ref.at[slot], q_send.at[j], q_recv.at[slot], j, home, z).wait_send()

    def kv_sent(k, carry):
        target, needed = kv_target(k)
        for j in range(2):

            @pl.when(needed & jnp.logical_not((target == c) & (d == j)))
            def _():
                kv_copy(k, j, target).wait_send()

        return carry

    lax.fori_loop(0, 8, kv_sent, 0)
    for which in range(2):
        block = high if which else low
        for step in (1, 2, 3):
            remote(*o_copy(which, step)).wait_send()

        @pl.when(jnp.logical_not((s == d) & (block == c)))
        def _():
            remote(*o_copy(which, 0)).wait_send()


def z_send(source_of, landed, send_sem, recv_sem, d, c, z):
    copies = []
    for step in (1, 2, 3):
        other = lax.rem(z + step, 4)
        copy = remote(
            source_of(other),
            landed(step),
            send_sem.at[step - 1],
            recv_sem.at[step - 1],
            d,
            c,
            other,
        )
        copy.start()
        copies.append(copy)
    return copies


def feed_kernel(
    x_ref,
    oall_ref,
    wall_ref,
    gain_ref,
    cot_ref,
    wg_ref,
    wu_ref,
    wd_ref,
    down_ref,
    hrows_ref,
    ghrows_ref,
    branch_ref,
    dob_ref,
    feed_ref,
    held_g,
    held_u,
    held_d,
    hidden,
    scale,
    mixed,
    mixed_t,
    cot_t,
    inner,
    grad_gate,
    grad_up,
    mixed_part,
    part_send,
    part_land,
    dw_g,
    dw_u,
    dw_d,
    land_g,
    land_u,
    land_d,
    z_sems,
    core_sems,
):
    d, c, z = place()
    barrier = pltpu.get_barrier_semaphore()
    for step in (1, 2, 3):
        pl.semaphore_signal(
            barrier, inc=1, device_id=(d, c, lax.rem(z + step, 4)), device_id_type=MESH
        )
    pl.semaphore_signal(barrier, inc=1, device_id=(1 - d, c, z), device_id_type=MESH)

    def project(t, carry):
        columns = pl.ds(pl.multiple_of(t * 256, 256), 256)
        hidden[:, columns] = x_ref[:, columns].astype(F32) + nt(oall_ref[...], wall_ref[columns, :])
        return carry

    lax.fori_loop(0, 4, project, 0)

    def normalize(r, carry):
        rows = pl.ds(pl.multiple_of(r * 96, 96), 96)
        values = hidden[rows, :]
        factor = lax.rsqrt(jnp.mean(values * values, axis=1, keepdims=True) + epsilon)
        scale[rows, :] = jnp.broadcast_to(factor, (96, 128))
        mixed[rows, :] = (values * factor * gain_ref[...]).astype(BF16)
        return carry

    lax.fori_loop(0, 4, normalize, 0)
    mixed_part[...] = jnp.zeros_like(mixed_part)

    def units(t, carry):
        columns = pl.ds(pl.multiple_of(t * 384, 384), 384)
        gate = nn(mixed[...], wg_ref[:, columns])
        up = nn(mixed[...], wu_ref[:, columns])
        sigmoid = 1.0 / (1.0 + jnp.exp(-gate))
        silu = gate * sigmoid
        inner[:, columns] = (silu * up).astype(BF16)
        grad_inner = nn(cot_ref[...], wd_ref[:, columns])
        grad_up[:, columns] = (grad_inner * silu).astype(BF16)
        grad_gate[:, columns] = (
            grad_inner * up * sigmoid * (1.0 + gate * (1.0 - sigmoid))
        ).astype(BF16)
        mixed_part[...] += nt(grad_gate[:, columns], wg_ref[:, columns]) + nt(
            grad_up[:, columns], wu_ref[:, columns]
        )
        return carry

    lax.fori_loop(0, 3, units, 0)
    for other in range(4):
        part_send[other] = mixed_part[other * 96 : (other + 1) * 96, :].astype(BF16)
    pl.semaphore_wait(barrier, 4)
    reduce = z_send(
        lambda other: part_send.at[other],
        lambda step: part_land.at[step - 1],
        z_sems.at[0],
        z_sems.at[1],
        d,
        c,
        z,
    )

    def transpose(t, carry):
        columns = pl.ds(pl.multiple_of(t * 128, 128), 128)
        mixed_t[columns, :] = mixed[:, columns].T
        cot_t[columns, :] = cot_ref[:, columns].T
        return carry

    lax.fori_loop(0, 8, transpose, 0)
    theirs = pl.ds(pl.multiple_of((1 - d) * 512, 512), 512)
    ours = pl.multiple_of(d * 512, 512)
    cores = []
    for index, (left, right, out, land) in enumerate(
        (
            (mixed_t, grad_gate, dw_g, land_g),
            (mixed_t, grad_up, dw_u, land_u),
            (cot_t, inner, dw_d, land_d),
        )
    ):

        def weights(t, carry):
            columns = pl.ds(pl.multiple_of(t * 384, 384), 384)
            out[:, columns] = nn(left[...], right[:, columns]).astype(BF16)
            return carry

        lax.fori_loop(0, 3, weights, 0)
        copy = remote(
            out.at[theirs], land, core_sems.at[0, index], core_sems.at[1, index], 1 - d, c, z
        )
        copy.start()
        cores.append(copy)

    for copy in reduce:
        copy.wait_recv()
    rows = pl.ds(pl.multiple_of(z * 96, 96), 96)
    incoming = mixed_part[rows, :]
    for step in range(3):
        incoming = incoming + part_land[step].astype(F32)
    values = hidden[rows, :]
    factor = scale[rows, 0:1]
    hrows_ref[...] = values
    weighted = incoming * gain_ref[...]
    projected = jnp.sum(weighted * values, axis=1, keepdims=True) * (1.0 / 1024.0)
    grad_rows = (
        cot_ref[rows, :].astype(F32)
        + factor * weighted
        - values * (factor * factor * factor * projected)
    )
    feed_ref[...] = jnp.broadcast_to(
        jnp.sum(incoming * values * factor, axis=0, keepdims=True), (8, 1024)
    )
    ghrows_ref[...] = grad_rows
    branch_ref[...] = grad_rows.astype(BF16)

    def attended(t, carry):
        columns = pl.ds(pl.multiple_of(t * 256, 256), 256)
        dob_ref[:, columns] = nn(branch_ref[...], wall_ref[:, columns]).astype(BF16)
        return carry

    lax.fori_loop(0, 4, attended, 0)

    def down(t, carry):
        columns = pl.ds(pl.multiple_of(t * 256, 256), 256)
        value = nt(inner[...], wd_ref[columns, :])
        for other in range(4):
            down_ref[other, :, columns] = value[other * 96 : (other + 1) * 96].astype(BF16)
        return carry

    lax.fori_loop(0, 4, down, 0)
    for copy, out, land, held in zip(
        cores, (dw_g, dw_u, dw_d), (land_g, land_u, land_d), (held_g, held_u, held_d)
    ):
        copy.wait_recv()

        def add(r, carry):
            here = pl.ds(pl.multiple_of(ours + r * 128, 128), 128)
            there = pl.ds(pl.multiple_of(r * 128, 128), 128)
            held[there, :] = (out[here, :].astype(F32) + land[there, :].astype(F32)).astype(BF16)
            return carry

        lax.fori_loop(0, 4, add, 0)
    for copy in reduce + cores:
        copy.wait_send()


class PlaneSum:
    def __init__(self, index, source, y_first, buffers, sems):
        self.index, self.source, self.y_first = index, source, y_first
        self.own, self.landed, self.summed, self.landed_last = buffers
        self.own_sem, self.first_sems, self.last_sems = sems
        self.d, c, self.z = place()
        self.y, self.x = c // 4, lax.rem(c, 4)

    def along(self, first, step):
        if first == self.y_first:
            other = lax.rem(self.y + step, 4)
            return other, other * 4 + self.x
        other = lax.rem(self.x + step, 4)
        return other, self.y * 4 + other

    def part(self, place_):
        return self.source.at[place_] if self.y_first else self.source.at[:, place_]

    def start(self):
        self.firsts = []
        for step in (2, 1, 3):
            other, chip = self.along(True, step)
            copy = remote(
                self.part(other),
                self.landed.at[step - 1],
                self.first_sems.at[0, self.index, step - 1],
                self.first_sems.at[1, self.index, step - 1],
                self.d,
                chip,
                self.z,
            )
            copy.start()
            self.firsts.append(copy)
        self.load = local_sem(
            self.part(self.y if self.y_first else self.x), self.own, self.own_sem.at[self.index]
        )
        self.load.start()

    def middle(self):
        self.load.wait()
        for copy in self.firsts:
            copy.wait_recv()

        def add(r, carry):
            total = self.own[r].astype(F32)
            for step in range(3):
                total = total + self.landed[step, r].astype(F32)
            self.summed[r] = total.astype(BF16)
            return carry

        lax.fori_loop(0, 4, add, 0)
        self.lasts = []
        for step in (2, 1, 3):
            other, chip = self.along(False, step)
            copy = remote(
                self.summed.at[other],
                self.landed_last.at[step - 1],
                self.last_sems.at[0, self.index, step - 1],
                self.last_sems.at[1, self.index, step - 1],
                self.d,
                chip,
                self.z,
            )
            copy.start()
            self.lasts.append(copy)

    def finish(self):
        for copy in self.lasts:
            copy.wait_recv()
        total = self.summed[self.x if self.y_first else self.y].astype(F32)
        for step in range(3):
            total = total + self.landed_last[step].astype(F32)
        return total

    def sent(self):
        for copy in self.firsts + self.lasts:
            copy.wait_send()


def plane_sum_scratch(widths):
    number = len(widths)
    scratch = []
    for width in widths:
        for lead in ((4,), (3, 4), (4,), (3,)):
            scratch.append(pltpu.VMEM(lead + (32, width), BF16))
    return scratch + [
        pltpu.SemaphoreType.DMA((number,)),
        pltpu.SemaphoreType.DMA((2, number, 3)),
        pltpu.SemaphoreType.DMA((2, number, 3)),
    ]


def plane_sums(sources, y_firsts, scratch):
    number = len(sources)
    return [
        PlaneSum(i, sources[i], y_firsts[i], scratch[4 * i : 4 * i + 4], scratch[4 * number :])
        for i in range(number)
    ]


BACKWARD_ITEMS = ((0, 0, 640, True), (0, 640, 512, False), (1, 0, 256, True), (1, 256, 384, False))
FINAL_ITEMS = ((0, 640, 256, True), (0, 896, 256, False), (1, 0, 512, True), (1, 512, 640, False))
LATE_ITEMS = ((0, 384, True), (384, 384, False))


def attention_backward_kernel(
    dob_ref,
    kvs_ref,
    qs_ref,
    os_ref,
    l2_ref,
    down_ref,
    hrows_ref,
    branch_ref,
    held_g,
    held_u,
    dq_ref,
    dkv_ref,
    block_ref,
    branches_ref,
    gate_ref,
    up_ref,
    qz,
    doz,
    delta,
    dos,
    dqt,
    dq_out,
    dq_in,
    dkv_out,
    dkv_in,
    down_land,
    do_send,
    do_recv,
    dq_send,
    dq_recv,
    dkv_send,
    dkv_recv,
    z_sems,
    *sum_scratch,
):
    d, c, z = place()
    s, j_role, low, high = role_of(d, c)
    own_group = low
    slot = jnp.where(c >= 8, 1, 0)
    home = jnp.where(slot == d, c, 15 - c)
    barrier = pltpu.get_barrier_semaphore()

    def greet(index, carry):
        other_d, other_c = index // 16, lax.rem(index, 16)

        @pl.when((other_d != d) | (other_c != c))
        def _():
            pl.semaphore_signal(
                barrier, inc=1, device_id=(other_d, other_c, z), device_id_type=MESH
            )

        return carry

    lax.fori_loop(0, 32, greet, 0)
    for step in (1, 2, 3):
        other = lax.rem(z + step, 4)
        pl.semaphore_signal(barrier, inc=1, device_id=(d, c, other), device_id_type=MESH)
        for block in (low, high):
            pl.semaphore_signal(barrier, inc=1, device_id=(s, block, other), device_id_type=MESH)
    pl.semaphore_wait(barrier, 31 + 3 + 6)

    def do_copy(j, step):
        other = lax.rem(z + step, 4)
        source = dob_ref.at[:, pl.ds(pl.multiple_of(other * 256 + j * 128, 128), 128)]
        there = dos.at[slot, pl.ds(pl.multiple_of(z * 96, 96), 96)]
        return source, there, do_send.at[j, step], do_recv.at[slot, z], j, home, other

    for j in range(2):
        for step in (2, 1, 3):
            remote(*do_copy(j, step)).start()
        here = (home == c) & (d == j)

        @pl.when(jnp.logical_not(here))
        def _():
            remote(*do_copy(j, 0)).start()

        @pl.when(here)
        def _():
            source, there, _, arrived = do_copy(j, 0)[:4]
            local_sem(source, there, arrived).start()

    reduce = z_send(
        lambda other: down_ref.at[other],
        lambda step: down_land.at[step - 1],
        z_sems.at[0, 0],
        z_sems.at[0, 1],
        d,
        c,
        z,
    )
    gather = z_send(
        lambda other: branch_ref,
        lambda step: branches_ref.at[z],
        z_sems.at[1, 0],
        z_sems.at[1, 1],
        d,
        c,
        z,
    )
    sources = [
        (held_g, held_u)[index].at[:, :, :, start : start + width]
        for index, start, width, _ in BACKWARD_ITEMS
    ]
    sums = plane_sums(sources, [item[3] for item in BACKWARD_ITEMS], sum_scratch)
    for item in sums:
        item.start()
    branches_ref[z] = branch_ref[...]

    dqt[...] = jnp.zeros_like(dqt)
    for which in range(2):
        first, second = spread_heads(qs_ref[which], False)
        qz[which, 0:ROWS, :] = first
        qz[which, ROWS : 2 * ROWS, :] = second
    for which in range(2):
        for source in range(4):
            there = dos.at[which, source * 96 : (source + 1) * 96]
            local_sem(dob_ref.at[:, 0:128], there, do_recv.at[which, source]).wait()
        first, second = spread_heads(dos[which], True)
        doz[which, 0:ROWS, :] = first
        doz[which, ROWS : 2 * ROWS, :] = second
        product = (dos[which].astype(F32) * os_ref[which].astype(F32)).T
        delta[which, :, 0:ROWS] = jnp.broadcast_to(
            jnp.sum(product[0:64], axis=0, keepdims=True), (8, ROWS)
        )
        delta[which, :, ROWS : 2 * ROWS] = jnp.broadcast_to(
            jnp.sum(product[64:128], axis=0, keepdims=True), (8, ROWS)
        )

    lane = lanes()
    key_scale = jnp.where(lane < 64, 0.125, 1.0)

    def tile(block, which, masked):
        keys = kvs_ref[block]
        keys_t = keys.T
        result = None
        for head in range(2):
            rows = slice(head * ROWS, (head + 1) * ROWS)
            q_rows = qz[which, rows, :]
            do_rows = doz[which, rows, :]
            weights = jnp.exp2(nt(keys, q_rows) * SCORE_SCALE - l2_ref[which, 0:1, rows])
            if masked:
                key = lax.broadcasted_iota(jnp.int32, weights.shape, 0)
                row = lax.broadcasted_iota(jnp.int32, weights.shape, 1)
                weights = jnp.where(row >= key, weights, 0.0)
            score_grad = (weights * (nt(keys, do_rows) - delta[which, 0:1, rows])).astype(BF16)
            part = nn(score_grad, q_rows) + nn(weights.astype(BF16), do_rows)
            result = part if result is None else result + part
            dqt[which, :, rows] += nn(keys_t, score_grad)
        return result * key_scale

    def dkv_copy(block):
        return (
            dkv_out.at[block],
            dkv_in.at[j_role, own_group],
            dkv_send.at[block],
            dkv_recv.at[j_role, own_group],
            s,
            block,
            z,
        )

    def send(block):
        here = (s == d) & (block == c)

        @pl.when(jnp.logical_not(here))
        def _():
            remote(*dkv_copy(block)).start()

        @pl.when(here)
        def _():
            source, there, _, arrived = dkv_copy(block)[:4]
            local_sem(source, there, arrived).start()

    dkv_out[low] = (tile(low, 1, False) + tile(low, 0, True)).astype(BF16)
    send(low)
    dkv_out[high] = tile(high, 1, True).astype(BF16)
    send(high)

    def step(k, carry):
        first = lax.rem(own_group + 8 - k, 8)
        below = first < own_group
        one = tile(first, 1, False)
        two = tile(jnp.where(below, first, 15 - first), jnp.where(below, 0, 1), False)

        @pl.when(below)
        def _():
            dkv_out[first] = (one + two).astype(BF16)
            send(first)

        @pl.when(jnp.logical_not(below))
        def _():
            dkv_out[first] = one.astype(BF16)
            send(first)
            dkv_out[15 - first] = two.astype(BF16)
            send(15 - first)

        return carry

    lax.fori_loop(1, 8, step, 0)

    def dq_copy(which):
        block = high if which else low
        return (
            dq_out.at[which],
            dq_in.at[j_role],
            dq_send.at[which],
            dq_recv.at[j_role],
            s,
            block,
            z,
        )

    for which in range(2):
        flat = dqt[which].T * 0.125
        dq_out[which] = jnp.where(
            lane < 64, flat[:ROWS], pltpu.roll(flat[ROWS:], 64, 1)
        ).astype(BF16)
        block = high if which else low
        here = (s == d) & (block == c)

        @pl.when(jnp.logical_not(here))
        def _():
            remote(*dq_copy(which)).start()

        @pl.when(here)
        def _():
            source, there, _, arrived = dq_copy(which)[:4]
            local_sem(source, there, arrived).start()

    for copy in reduce:
        copy.wait_recv()
    total = hrows_ref[...] + down_ref[z].astype(F32)
    for step in range(3):
        total = total + down_land[step].astype(F32)
    block_ref[z] = total.astype(BF16)
    last = z_send(
        lambda other: block_ref.at[z],
        lambda step: block_ref.at[z],
        z_sems.at[2, 0],
        z_sems.at[2, 1],
        d,
        c,
        z,
    )
    for item in sums:
        item.middle()

    for j in range(2):
        dkv_ref[j] = jnp.zeros((ROWS, 128), F32)

    def collect(k, carry):
        group = lax.rem(own_group + k, 8)

        @pl.when((15 - group) >= c)
        def _():
            for j in range(2):
                local_sem(dkv_out.at[0], dkv_in.at[j, group], dkv_recv.at[j, group]).wait()
                dkv_ref[j] += dkv_in[j, group].astype(F32)

        return carry

    lax.fori_loop(0, 8, collect, 0)
    for j in range(2):
        local_sem(dq_out.at[0], dq_in.at[j], dq_recv.at[j]).wait()
        dq_ref[:, j * 128 : (j + 1) * 128] = dq_in[j]
    for item, (index, start, width, _) in zip(sums, BACKWARD_ITEMS):
        (gate_ref, up_ref)[index][:, start : start + width] = item.finish()
    for copy in gather + last:
        copy.wait_recv()

    for item in sums:
        item.sent()
    for copy in reduce + gather + last:
        copy.wait_send()
    for j in range(2):
        for step in (1, 2, 3):
            remote(*do_copy(j, step)).wait_send()

        @pl.when(jnp.logical_not((home == c) & (d == j)))
        def _():
            remote(*do_copy(j, 0)).wait_send()

    for which in range(2):
        block = high if which else low

        @pl.when(jnp.logical_not((s == d) & (block == c)))
        def _():
            remote(*dq_copy(which)).wait_send()

    def sent(block, carry):
        @pl.when((block <= high) & jnp.logical_not((s == d) & (block == c)))
        def _():
            remote(*dkv_copy(block)).wait_send()

        return carry

    lax.fori_loop(0, 16, sent, 0)


def final_kernel(
    dq_ref,
    dkv_ref,
    qraw_ref,
    kraw_ref,
    normed_ref,
    x_ref,
    gain_ref,
    qgain_ref,
    kgain_ref,
    row_cos,
    row_sin,
    block_cos,
    block_sin,
    wq_ref,
    wk_ref,
    wv_ref,
    oall_ref,
    branches_ref,
    ghrows_ref,
    feed_ref,
    held_u,
    held_d,
    input_ref,
    late_ref,
    gains_ref,
    up_ref,
    down_ref,
    grads,
    transposed,
    part,
    part_land,
    late,
    late_land,
    late_held,
    gather_rows,
    gains,
    gains_land,
    chunk_in,
    chunk,
    chunk_land,
    chunk_held,
    z_sems,
    core_sems,
    *sum_scratch,
):
    d, c, z = place()
    y, x = c // 4, lax.rem(c, 4)
    barrier = pltpu.get_barrier_semaphore()
    pl.semaphore_signal(barrier, inc=1, device_id=(1 - d, c, z), device_id_type=MESH)
    for step in (1, 2, 3):
        for other in (lax.rem(y + step, 4) * 4 + x, y * 4 + lax.rem(x + step, 4)):
            pl.semaphore_signal(barrier, inc=1, device_id=(d, other, z), device_id_type=MESH)
        pl.semaphore_signal(
            barrier, inc=1, device_id=(d, c, lax.rem(z + step, 4)), device_id_type=MESH
        )
    pl.semaphore_wait(barrier, 10)
    sources = [
        (held_u, held_d)[index].at[:, :, :, start : start + width]
        for index, start, width, _ in FINAL_ITEMS
    ]
    sources += [late_held.at[:, :, :, start : start + width] for start, width, _ in LATE_ITEMS]
    sources += [chunk_held]
    y_firsts = [item[3] for item in FINAL_ITEMS] + [item[2] for item in LATE_ITEMS] + [True]
    sums = plane_sums(sources, y_firsts, sum_scratch)
    early_sums, late_sums, gain_sum = sums[:4], sums[4:6], sums[6]
    for item in early_sums:
        item.start()

    cosine, sine = tables(c, row_cos, row_sin, block_cos, block_sin)
    lane = lanes()
    query_part = jnp.zeros((1, 128), F32)
    for j in range(2):
        columns = slice(j * 128, (j + 1) * 128)
        raw_grad, gain_part = pair_backward(
            dq_ref[:, columns].astype(F32), qraw_ref[:, columns], qgain_ref[...], cosine, sine
        )
        grads[:, columns] = raw_grad.astype(BF16)
        query_part = query_part + gain_part
    first, second = dkv_ref[0], dkv_ref[1]
    raw_grad, key_part = pair_backward(
        jnp.where(lane < 64, first, pltpu.roll(second, 64, 1)),
        kraw_ref[...],
        kgain_ref[...],
        cosine,
        sine,
    )
    grads[:, 256:384] = raw_grad.astype(BF16)
    grads[:, 384:512] = jnp.where(lane < 64, pltpu.roll(first, 64, 1), second).astype(BF16)

    def project(t, carry):
        columns = pl.ds(pl.multiple_of(t * 256, 256), 256)
        value = (
            nt(grads[:, 0:256], wq_ref[columns, :])
            + nt(grads[:, 256:384], wk_ref[columns, :])
            + nt(grads[:, 384:512], wv_ref[columns, :])
        ).astype(BF16)
        for other in range(4):
            part[other, :, columns] = value[other * 96 : (other + 1) * 96]
        return carry

    lax.fori_loop(0, 4, project, 0)
    reduce = z_send(
        lambda other: part.at[other],
        lambda step: part_land.at[step - 1],
        z_sems.at[0, 0],
        z_sems.at[0, 1],
        d,
        c,
        z,
    )

    def transpose(t, carry):
        columns = pl.ds(pl.multiple_of(t * 128, 128), 128)
        transposed[columns, :] = normed_ref[:, columns].T
        return carry

    lax.fori_loop(0, 8, transpose, 0)
    late[:, 0:512] = nn(transposed[...], grads[...]).astype(BF16)

    def transpose_branch(t, carry):
        columns = pl.ds(pl.multiple_of(t * 128, 128), 128)
        transposed[columns, :] = branches_ref[:, columns].T
        return carry

    lax.fori_loop(0, 8, transpose_branch, 0)
    own_heads = oall_ref[:, pl.ds(pl.multiple_of(z * 256, 256), 256)]
    late[:, 512:768] = nn(transposed[...], own_heads).astype(BF16)
    theirs = pl.ds(pl.multiple_of((1 - d) * 512, 512), 512)
    ours = pl.multiple_of(d * 512, 512)
    late_core = remote(
        late.at[theirs], late_land, core_sems.at[0, 0], core_sems.at[1, 0], 1 - d, c, z
    )
    late_core.start()

    for copy in reduce:
        copy.wait_recv()
    rows = pl.ds(pl.multiple_of(z * 96, 96), 96)
    incoming = part[z].astype(F32)
    for step in range(3):
        incoming = incoming + part_land[step].astype(F32)
    values = x_ref[rows, :].astype(F32)
    factor = lax.rsqrt(jnp.mean(values * values, axis=1, keepdims=True) + epsilon)
    weighted = incoming * gain_ref[...]
    projected = jnp.sum(weighted * values, axis=1, keepdims=True) * (1.0 / 1024.0)
    gains[...] = jnp.zeros_like(gains)
    gains[0:1, :] = jnp.sum(incoming * values * factor, axis=0, keepdims=True)
    gains[1:2, :] = feed_ref[0:1, :]
    gains[2:3, 0:128] = query_part + pltpu.roll(query_part, 64, 1)
    gains[3:4, 0:128] = key_part + pltpu.roll(key_part, 64, 1)
    gains_copies = z_send(
        lambda other: gains,
        lambda step: gains_land.at[step - 1],
        z_sems.at[1, 0],
        z_sems.at[1, 1],
        d,
        c,
        z,
    )
    gather_rows[z] = (
        ghrows_ref[...] + factor * weighted - values * (factor * factor * factor * projected)
    ).astype(BF16)
    gather = z_send(
        lambda other: gather_rows.at[z],
        lambda step: gather_rows.at[z],
        z_sems.at[2, 0],
        z_sems.at[2, 1],
        d,
        c,
        z,
    )

    late_core.wait_recv()

    def add_late(r, carry):
        for part_ in range(4):
            here = pl.ds(pl.multiple_of(ours + r * 128 + part_ * 32, 32), 32)
            there = pl.ds(pl.multiple_of(r * 128 + part_ * 32, 32), 32)
            late_held[r, part_] = (
                late[here, :].astype(F32) + late_land[there, :].astype(F32)
            ).astype(BF16)
        return carry

    lax.fori_loop(0, 4, add_late, 0)
    for item in late_sums:
        item.start()

    for copy in gains_copies:
        copy.wait_recv()
    chunk_in[...] = jnp.zeros_like(chunk_in)
    chunk_in[0:8, :] = gains[...] + gains_land[0] + gains_land[1] + gains_land[2]
    column_part = chunk_in[...].T
    row_index = lax.broadcasted_iota(jnp.int32, (1024, 128), 0)
    lane_index = lax.broadcasted_iota(jnp.int32, (1024, 128), 1)
    row_kind = lax.rem(row_index, 32)
    query_total, key_total = chunk_in[2:3, 0:128], chunk_in[3:4, 0:128]
    spread = jnp.where(
        row_kind == 0, query_total, jnp.where(row_kind == 1, key_total, 0.0)
    )
    chunk[...] = jnp.where(lane_index < 64, column_part, spread).astype(BF16)
    chunk_core = remote(
        chunk.at[theirs], chunk_land, core_sems.at[0, 1], core_sems.at[1, 1], 1 - d, c, z
    )
    chunk_core.start()
    for item in early_sums:
        item.middle()
    chunk_core.wait_recv()
    for r in range(4):
        for part_ in range(4):
            here = pl.ds(pl.multiple_of(ours + r * 128 + part_ * 32, 32), 32)
            there = slice(r * 128 + part_ * 32, r * 128 + part_ * 32 + 32)
            chunk_held[r, part_] = (
                chunk[here, :].astype(F32) + chunk_land[there, :].astype(F32)
            ).astype(BF16)
    gain_sum.start()
    for item in late_sums:
        item.middle()
    gain_sum.middle()
    for copy in gather:
        copy.wait_recv()
    for other in range(4):
        input_ref[other * 96 : (other + 1) * 96, :] = gather_rows[other].astype(F32)
    for item, (index, start, width, _) in zip(early_sums, FINAL_ITEMS):
        offset = start - 640 if index == 0 else start
        (up_ref, down_ref)[index][:, offset : offset + width] = item.finish()
    for item, (start, width, _) in zip(late_sums, LATE_ITEMS):
        late_ref[:, start : start + width] = item.finish()
    gains_ref[...] = gain_sum.finish()
    for item in sums:
        item.sent()
    late_core.wait_send()
    chunk_core.wait_send()
    for copy in reduce + gains_copies + gather:
        copy.wait_send()


def kernel_call(body, collective_id, name, ins, outs, scratch, any_inputs=()):
    vmem, anywhere = pl.BlockSpec(memory_space=pltpu.VMEM), pl.BlockSpec(memory_space=pl.ANY)
    return pl.pallas_call(
        body,
        out_shape=[jax.ShapeDtypeStruct(shape, kind) for shape, kind in outs],
        in_specs=[anywhere if i in any_inputs else vmem for i in range(len(ins))],
        out_specs=[vmem] * len(outs),
        scratch_shapes=scratch,
        compiler_params=pltpu.CompilerParams(
            collective_id=collective_id, has_side_effects=True, vmem_limit_bytes=VMEM_LIMIT
        ),
        name=name,
    )(*ins)


def shards(
    inputs,
    cotangent,
    attention_gain,
    query_gain,
    key_gain,
    w_query,
    key_weight,
    value_weight,
    w_out,
    feed_gain,
    w_gate,
    w_up,
    w_down,
):
    dma, v = pltpu.SemaphoreType.DMA, pltpu.VMEM
    position_tables = [jnp.asarray(table) for table in split_columns()]
    attention_gain = attention_gain.reshape(1, 1024)
    feed_gain = feed_gain.reshape(1, 1024)
    query_gain = jnp.tile(query_gain, 2).reshape(1, 128)
    key_gain = jnp.tile(key_gain, 2).reshape(1, 128)
    role_kv, role_q, role_o, role_logs, attended, w_out_all, normed, query_raw, key_raw = kernel_call(
        attention_forward_kernel,
        1,
        "attention_forward",
        [
            inputs,
            attention_gain,
            w_query,
            key_weight,
            value_weight,
            query_gain,
            key_gain,
            *position_tables,
            w_out,
        ],
        [
            ((16, ROWS, 128), BF16),
            ((2, ROWS, 128), BF16),
            ((2, ROWS, 128), BF16),
            ((2, 8, 2 * ROWS), F32),
            ((ROWS, 1024), BF16),
            ((1024, 1024), BF16),
            ((ROWS, 1024), BF16),
            ((ROWS, 256), F32),
            ((ROWS, 128), F32),
        ],
        [
            v((2, ROWS, 128), BF16),
            v((2, ROWS, 128), BF16),
            v((2, 2 * ROWS, 128), BF16),
            v((2, 2 * ROWS, 128), F32),
            v((2, 2 * ROWS, 128), F32),
            dma((2,)),
            dma((2,)),
            dma((16,)),
            dma((16,)),
            dma((2, 4)),
            dma((8,)),
            dma((3,)),
            dma((3,)),
            dma((3,)),
            dma((3,)),
        ],
    )
    (
        down_part,
        hidden_rows,
        grad_hidden_rows,
        branch_rows,
        dob_rows,
        feed_part,
        held_gate,
        held_up,
        held_down,
    ) = kernel_call(
        feed_kernel,
        2,
        "feed_forward",
        [inputs, attended, w_out_all, feed_gain, cotangent, w_gate, w_up, w_down],
        [
            ((4, 96, 1024), BF16),
            ((96, 1024), F32),
            ((96, 1024), F32),
            ((96, 1024), BF16),
            ((96, 1024), BF16),
            ((8, 1024), F32),
            ((512, 1152), BF16),
            ((512, 1152), BF16),
            ((512, 1152), BF16),
        ],
        [
            v((ROWS, 1024), F32),
            v((ROWS, 128), F32),
            v((ROWS, 1024), BF16),
            v((1024, ROWS), BF16),
            v((1024, ROWS), BF16),
            v((ROWS, 1152), BF16),
            v((ROWS, 1152), BF16),
            v((ROWS, 1152), BF16),
            v((ROWS, 1024), F32),
            v((4, 96, 1024), BF16),
            v((3, 96, 1024), BF16),
            v((1024, 1152), BF16),
            v((1024, 1152), BF16),
            v((1024, 1152), BF16),
            v((512, 1152), BF16),
            v((512, 1152), BF16),
            v((512, 1152), BF16),
            dma((2, 3)),
            dma((2, 3)),
        ],
    )
    held_gate, held_up, held_down = [
        held.reshape(4, 4, 32, 1152) for held in (held_gate, held_up, held_down)
    ]
    grad_query, grad_kv, block_out, branches, gate_sum, up_sum = kernel_call(
        attention_backward_kernel,
        3,
        "attention_backward",
        [
            dob_rows,
            role_kv,
            role_q,
            role_o,
            role_logs,
            down_part,
            hidden_rows,
            branch_rows,
            held_gate,
            held_up,
        ],
        [
            ((ROWS, 256), BF16),
            ((2, ROWS, 128), F32),
            ((4, 96, 1024), BF16),
            ((4, 96, 1024), BF16),
            ((32, 1152), F32),
            ((32, 640), F32),
        ],
        [
            v((2, 2 * ROWS, 128), BF16),
            v((2, 2 * ROWS, 128), BF16),
            v((2, 8, 2 * ROWS), F32),
            v((2, ROWS, 128), BF16),
            v((2, 128, 2 * ROWS), F32),
            v((2, ROWS, 128), BF16),
            v((2, ROWS, 128), BF16),
            v((16, ROWS, 128), BF16),
            v((2, 8, ROWS, 128), BF16),
            v((3, 96, 1024), BF16),
            dma((2, 4)),
            dma((2, 4)),
            dma((2,)),
            dma((2,)),
            dma((16,)),
            dma((2, 8)),
            dma((3, 2, 3)),
        ]
        + plane_sum_scratch([item[2] for item in BACKWARD_ITEMS]),
        any_inputs=(8, 9),
    )
    block_out = block_out.reshape(ROWS, 1024)
    branches = branches.reshape(ROWS, 1024)
    input_grad, late_sum, gain_sum, up_sum_2, down_sum = kernel_call(
        final_kernel,
        4,
        "final",
        [
            grad_query,
            grad_kv,
            query_raw,
            key_raw,
            normed,
            inputs,
            attention_gain,
            query_gain,
            key_gain,
            *position_tables,
            w_query,
            key_weight,
            value_weight,
            attended,
            branches,
            grad_hidden_rows,
            feed_part,
            held_up,
            held_down,
        ],
        [
            ((ROWS, 1024), F32),
            ((32, 768), F32),
            ((32, 128), F32),
            ((32, 512), F32),
            ((32, 1152), F32),
        ],
        [
            v((ROWS, 512), BF16),
            v((1024, ROWS), BF16),
            v((4, 96, 1024), BF16),
            v((3, 96, 1024), BF16),
            v((1024, 768), BF16),
            v((512, 768), BF16),
            v((4, 4, 32, 768), BF16),
            v((4, 96, 1024), BF16),
            v((8, 1024), F32),
            v((3, 8, 1024), F32),
            v((128, 1024), F32),
            v((1024, 128), BF16),
            v((512, 128), BF16),
            v((4, 4, 32, 128), BF16),
            dma((3, 2, 3)),
            dma((2, 2)),
        ]
        + plane_sum_scratch(
            [item[2] for item in FINAL_ITEMS] + [item[1] for item in LATE_ITEMS] + [128]
        ),
        any_inputs=(20, 21),
    )
    place_index = lax.axis_index("dp") * 16 + lax.axis_index("ctx")
    pair = 64 + 2 * place_index
    return (
        block_out,
        input_grad,
        gain_sum[:, 0],
        lax.dynamic_slice(gain_sum[0], (pair,), (2,)),
        lax.dynamic_slice(gain_sum[1], (pair,), (2,)),
        late_sum[:, 0:256],
        late_sum[:, 256:384],
        late_sum[:, 384:512],
        late_sum[:, 512:768],
        gain_sum[:, 1],
        gate_sum,
        jnp.concatenate([up_sum, up_sum_2], axis=1),
        down_sum,
    )


def solution(mesh):
    both = ("dp", "ctx")
    by_head = P(None, "head")
    reduced = P(both, "head")
    return jax.shard_map(
        shards,
        mesh=mesh,
        in_specs=(
            P(both, None),
            P(both, None),
            P(),
            P(),
            P(),
            by_head,
            by_head,
            by_head,
            by_head,
            P(),
            by_head,
            by_head,
            by_head,
        ),
        out_specs=(
            P(both, None),
            P(both, None),
            P(both),
            P(both),
            P(both),
            reduced,
            reduced,
            reduced,
            reduced,
            P(both),
            reduced,
            reduced,
            reduced,
        ),
        check_vma=False,
    )
```

time: 324 us -> 183 us (0.56)
  Pallas kernels: 224 us -> 166 us
  matrix products: 42.8 us -> 0 us
  other arithmetic: 26.7 us -> 1.63 us
  local copies, waits for them, and re-layouts: 28.2 us -> 11.4 us
    pallas_call x8 -> x4, Pallas kernels: 224 us -> 166 us  [kernel_call(): pl.pallas_call(body, out_shape=[jax.ShapeDtypeStruct(shape, kind) for sha...]
    dot_general x21 -> x0, matrix products: 42.8 us -> none  [the longest x7 15.9 us: contract_cols(): lax.dot_general(left_side, right_side, (((1,), (1,)), ((), ())), preferre...]
    convert_element_type x10 -> x0, other arithmetic: 10.2 us -> none  [the longest x1 2.45 us: shards(): input_grad = input_grad.reshape(block_rows, -1).astype(F32)]
    reduce_sum x8 -> x0, other arithmetic: 7.07 us -> none  [the longest x4 4.29 us: row_norm(): return values * rms_scale(values) * gain]
    unnamed x131 -> x14, local copies, waits for them, and re-layouts: 10.4 us -> 3.36 us
    reshape x8 -> x0, local copies, waits for them, and re-layouts: 6.86 us -> none  [the longest x2 2.58 us: head_pairs(): return values.reshape(values.shape[0], 2, 128).transpose(1, 0, 2)]
    mul x6 -> x0, other arithmetic: 4.69 us -> none  [the longest x4 3.78 us: rotate(): return values * cosine_table + turned * sine_table]
    concatenate x2 -> x0, local copies, waits for them, and re-layouts: 3.44 us -> none  [the longest x1 1.76 us: rotary_tables(): jnp.concatenate([sine_table, sine_table], -1)]
where the time goes in v2:
time: 183 us; the launch traced here: 179 us
  Pallas kernels  166 us (91%)
  local copies, waits for them, and re-layouts  11.4 us (6%)
    pallas_call x4, Pallas kernels, kernel_call(): pl.pallas_call(body, out_shape=[jax.ShapeDtypeStruct(shape, kind) for sha...  166 us

profile of v2, /device:TPU:1, one launch (start us, length us, event | category | flops | bytes accessed | tf_op | source)
XLA Modules:
  0.0 179.4 jit_solution(6664316719559940240)
XLA Ops:
  0.6 0.7 tile.4
  1.3 0.6 reshape_tile.6.qgain_ref
  1.9 0.7 tile.5
  2.6 0.6 reshape_tile.7.kgain_ref
  3.1 51.8 %attention_forward.1 = (bf16[16,384,128]{2,1,0:T(8,128)(2,1)}, bf16[2,384,128]{2,1,0:T(8,128)(2,1)}, bf16[2,384,128]{2,1,0:T(8,128)(2,1)}, f32[2,8,768]{2,1,0:T(...) custom-call(bf16[384,1024]{1,0:T(8,128)(2,1)} %x_ref.5, ...), custom_call_target="tpu_custom_call" | custom-call | tf_op jit(solution)/shard_map/attention_forward/pallas_call | solution.py:1228
  55.0 30.8 %feed_forward.1 = (bf16[4,96,1024]{2,1,0:T(8,128)(2,1)}, f32[96,1024]{1,0:T(8,128)}, f32[96,1024]{1,0:T(8,128)}, bf16[96,1024]{1,0:T(8,128)(2,1)}, bf16[96,1024]...) custom-call(bf16[384,1024]{1,0:T(8,128)(2,1)} %x_ref.5, ...), custom_call_target="tpu_custom_call" | custom-call | tf_op jit(solution)/shard_map/feed_forward/pallas_call | solution.py:1228
  85.8 47.2 %attention_backward.1 = (bf16[384,256]{1,0:T(8,128)(2,1)}, f32[2,384,128]{2,1,0:T(8,128)}, bf16[4,96,1024]{2,1,0:T(8,128)(2,1)}, bf16[4,96,1024]{2,1,0:T(8,128)(...) custom-call(bf16[96,1024]{1,0:T(8,128)(2,1)} %get-tuple-element.44.dob_ref, ...), custom_call_target="tpu_custom_call" | custom-call | tf_op jit(solution)/shard_map/attention_backward/pallas_call | solution.py:1228
  133.0 0.0 copy-start.4
  133.0 0.0 copy-start.1
  133.1 35.8 %final.1 = (f32[384,1024]{1,0:T(8,128)}, f32[32,768]{1,0:T(8,128)}, f32[32,128]{1,0:T(8,128)}, f32[32,512]{1,0:T(8,128)}, f32[32,1152]{1,0:T(8,128)}) custom-call(bf16[384,256]{1,0:T(8,128)(2,1)} %get-tuple-element.55.dq_ref, f32[2,384,128]{2,1,0:T(8,128)} %get-tuple-element.56.dkv_ref, f32[384,256]{1,0:T(8,128)} %get-tuple-element.57.qraw_ref, ...), custom_call_target="tpu_custom_call" | custom-call | tf_op jit(solution)/shard_map/final/pallas_call | solution.py:1228
  168.8 0.0 copy-start
  168.8 0.0 copy-done.4
  168.8 1.6 pad_maximum_fusion
  170.5 0.8 fusion.2
  171.2 0.6 dynamic-slice_bitcast_fusion
  171.8 1.4 fusion
  173.2 1.3 fusion.1
  174.6 1.5 slice_reduce_fusion
  176.0 0.0 copy-done.1
  176.0 0.9 copy.34
  176.9 0.0 copy-done
  176.9 1.1 copy.35
  178.1 0.7 copy.36
  178.7 0.7 copy.37
  (4 shorter events, 0.0 us)
Async XLA Ops:
  133.0 35.8 %copy-start.4 = (f32[32,640]{1,0:T(8,128)S(1)}, f32[32,640]{1,0:T(8,128)}, u32[]{:S(2)}) copy-start(f32[32,640]{1,0:T(8,128)} %get-tuple-element.68) | copy-start | bytes 245764
  133.0 43.0 %copy-start.1 = (bf16[4,96,1024]{2,1,0:T(8,128)(2,1)S(1)}, bf16[4,96,1024]{2,1,0:T(8,128)(2,1)}, u32[]{:S(2)}) copy-start(bf16[4,96,1024]{2,1,0:T(8,128)(2,1)} %get-tuple-element.54) | copy-start | bytes 2359300
  168.8 8.1 %copy-start = (f32[384,1024]{1,0:T(8,128)S(1)}, f32[384,1024]{1,0:T(8,128)}, u32[]{:S(2)}) copy-start(f32[384,1024]{1,0:T(8,128)} %get-tuple-element.95) | copy-start | bytes 4718596
  176.9 1.1 copy-start.2
  176.9 1.8 %copy-start.3 = (f32[32,1152]{1,0:T(8,128)S(1)}, f32[32,1152]{1,0:T(8,128)}, u32[]{:S(2)}) copy-start(f32[32,1152]{1,0:T(8,128)} %get-tuple-element.106) | copy-start | bytes 442372

commit v3 on v0

v3 whole, which is shorter than its diff:
```python
from types import SimpleNamespace

import jax
import jax.numpy as jnp
import numpy as np
from jax import lax
from jax.experimental import pallas as pl
from jax.experimental.pallas import tpu as pltpu
from jax.sharding import PartitionSpec as P

epsilon = 1e-05
theta_base = 1000000.0
MESH = pl.DeviceIdType.MESH
F32 = jnp.float32
BF16 = jnp.bfloat16
ROWS = 384
LOG2E = 1.4426950408889634
VMEM_LIMIT = 63 * 1024 * 1024


def remote(src, dst, send_sem, recv_sem, d, c, z):
    return pltpu.make_async_remote_copy(
        src_ref=src,
        dst_ref=dst,
        send_sem=send_sem,
        recv_sem=recv_sem,
        device_id=(d, c, z),
        device_id_type=MESH,
    )


def local_sem(src, dst, sem):
    return pltpu.make_async_copy(src, dst, sem)


def place():
    return lax.axis_index("dp"), lax.axis_index("ctx"), lax.axis_index("head")


def role_of(d, c):
    row, column = c // 4, lax.rem(c, 4)
    low = jnp.where(d == 0, column, 7 - column)
    return row // 2, lax.rem(row, 2), low, 15 - low


def lower(block):
    return jnp.minimum(block, 15 - block)


def spread_heads(pair, upper):
    pair = pair.astype(F32)
    lane = lax.broadcasted_iota(jnp.int32, pair.shape, 1)
    turned = pltpu.roll(pair, 64, 1)
    if upper:
        first, second = jnp.where(lane >= 64, turned, 0.0), jnp.where(lane >= 64, pair, 0.0)
    else:
        first, second = jnp.where(lane < 64, pair, 0.0), jnp.where(lane < 64, turned, 0.0)
    return first.astype(BF16), second.astype(BF16)


def nt(left, right):
    return lax.dot_general(left, right, (((1,), (1,)), ((), ())), preferred_element_type=F32)


def nn(left, right):
    return lax.dot_general(left, right, (((1,), (0,)), ((), ())), preferred_element_type=F32)


SCORE_SCALE = LOG2E / 8.0


def split_columns(half_width=32, rows=ROWS, blocks=16):
    lane = np.arange(128) % half_width
    frequency = theta_base ** (-2.0 * lane / (2 * half_width))
    row_angle = np.arange(rows)[:, None] * frequency[None, :]
    block_angle = (np.arange(blocks) * rows)[:, None] * frequency[None, :]
    return [
        np.asarray(table, np.float32)
        for table in (
            np.cos(row_angle),
            np.sin(row_angle),
            np.cos(block_angle),
            np.sin(block_angle),
        )
    ]


def tables(c, row_cos, row_sin, block_cos, block_sin):
    bc, bs = block_cos[pl.ds(c, 1), :], block_sin[pl.ds(c, 1), :]
    rc, rs = row_cos[...], row_sin[...]
    return rc * bc - rs * bs, rs * bc + rc * bs


def lanes(rows=ROWS):
    return lax.broadcasted_iota(jnp.int32, (rows, 128), 1)


def half_sums(values):
    lane = lanes(values.shape[0])
    first = jnp.sum(jnp.where(lane < 64, values, 0.0), axis=1, keepdims=True)
    second = jnp.sum(jnp.where(lane >= 64, values, 0.0), axis=1, keepdims=True)
    return jnp.where(lane < 64, first, second)


def turn(values):
    lane = lanes(values.shape[0])
    return jnp.where(lax.rem(lane, 64) < 32, -pltpu.roll(values, 96, 1), pltpu.roll(values, 32, 1))


def turn_back(values):
    lane = lanes(values.shape[0])
    return jnp.where(lax.rem(lane, 64) < 32, pltpu.roll(values, 96, 1), -pltpu.roll(values, 32, 1))


def pair_forward(raw, gain, cosine, sine):
    scale = lax.rsqrt(half_sums(raw * raw) * (1.0 / 64.0) + epsilon)
    normed = raw * scale * gain
    return normed * cosine + turn(normed) * sine


def pair_backward(grad, raw, gain, cosine, sine):
    incoming = grad * cosine + turn_back(grad * sine)
    scale = lax.rsqrt(half_sums(raw * raw) * (1.0 / 64.0) + epsilon)
    weighted = incoming * gain
    inner = half_sums(weighted * raw) * (1.0 / 64.0)
    raw_grad = scale * weighted - raw * (scale * scale * scale) * inner
    return raw_grad, jnp.sum(incoming * raw * scale, axis=0, keepdims=True)


def z_send(source_of, landed, sems, d, c, z):
    copies = []
    for step in (2, 1, 3):
        other = lax.rem(z + step, 4)
        copy = remote(
            source_of(other),
            landed(step),
            sems.at[0, step - 1],
            sems.at[1, step - 1],
            d,
            c,
            other,
        )
        copy.start()
        copies.append(copy)
    return copies


class ZReduce:
    def __init__(self, part, land, sems, d, c, z):
        self.part, self.land, self.sems = part, land, sems
        self.d, self.c = d, c
        self.up, self.down, self.across = lax.rem(z + 1, 4), lax.rem(z + 3, 4), lax.rem(z + 2, 4)

    def copy(self, index, source, there, plane):
        copy = remote(
            source, there, self.sems.at[0, index], self.sems.at[1, index], self.d, self.c, plane
        )
        copy.start()
        return copy

    def start(self):
        part, land = self.part, self.land
        self.copies = [
            self.copy(0, part.at[self.across, 0:48], land.at[0, 0:48], self.up),
            self.copy(1, part.at[self.across, 48:96], land.at[0, 48:96], self.down),
            self.copy(2, part.at[self.up, 48:96], land.at[1, 48:96], self.up),
            self.copy(3, part.at[self.down, 0:48], land.at[2, 0:48], self.down),
        ]
        return self

    def relay(self):
        part, land = self.part, self.land
        for index, rows, plane in ((0, slice(0, 48), self.up), (1, slice(48, 96), self.down)):
            self.copies[index].wait_recv()
            part[plane, rows, :] = (
                part[plane, rows, :].astype(F32) + land[0, rows, :].astype(F32)
            ).astype(BF16)
            self.copies.append(
                self.copy(4 + index, part.at[plane, rows], land.at[1 + index, rows], plane)
            )

    def finish(self):
        for copy in self.copies[2:]:
            copy.wait_recv()
        return self.land[1].astype(F32) + self.land[2].astype(F32)


class ZGather(ZReduce):
    def __init__(self, slots, sems, d, c, z):
        super().__init__(slots, None, sems, d, c, z)
        self.z = z

    def start(self):
        low, high = self.part.at[self.z, 0:48], self.part.at[self.z, 48:96]
        self.copies = [
            self.copy(0, low, low, self.up),
            self.copy(1, high, high, self.down),
            self.copy(2, high, high, self.up),
            self.copy(3, low, low, self.down),
        ]
        return self

    def relay(self):
        self.copies[0].wait_recv()
        low = self.part.at[self.down, 0:48]
        self.copies.append(self.copy(4, low, low, self.up))
        self.copies[1].wait_recv()
        high = self.part.at[self.up, 48:96]
        self.copies.append(self.copy(5, high, high, self.down))

    def finish(self):
        for copy in self.copies[2:]:
            copy.wait_recv()


class PlaneSum:
    def __init__(self, index, source, y_first, landed, landed_last, sems):
        self.index, self.source, self.y_first = index, source, y_first
        self.landed, self.landed_last = landed, landed_last
        self.first_sems, self.last_sems = sems
        self.d, c, self.z = place()
        self.y, self.x = c // 4, lax.rem(c, 4)

    def along(self, first, step):
        if first == self.y_first:
            other = lax.rem(self.y + step, 4)
            return other, other * 4 + self.x
        other = lax.rem(self.x + step, 4)
        return other, self.y * 4 + other

    def start(self):
        self.firsts = []
        for step in (2, 1, 3):
            other, chip = self.along(True, step)
            copy = remote(
                self.source.at[other] if self.y_first else self.source.at[:, other],
                self.landed.at[step - 1],
                self.first_sems.at[0, self.index, step - 1],
                self.first_sems.at[1, self.index, step - 1],
                self.d,
                chip,
                self.z,
            )
            copy.start()
            self.firsts.append(copy)

    def middle(self):
        for copy in self.firsts:
            copy.wait_recv()

        def add(r, carry):
            own = self.source.at[self.y, r] if self.y_first else self.source.at[r, self.x]
            total = own[...].astype(F32)
            for step in range(3):
                total = total + self.landed[step, r].astype(F32)
            own[...] = total.astype(BF16)
            return carry

        lax.fori_loop(0, 4, add, 0)
        self.lasts = []
        for step in (2, 1, 3):
            other, chip = self.along(False, step)
            own = self.source.at[self.y, other] if self.y_first else self.source.at[other, self.x]
            copy = remote(
                own,
                self.landed_last.at[step - 1],
                self.last_sems.at[0, self.index, step - 1],
                self.last_sems.at[1, self.index, step - 1],
                self.d,
                chip,
                self.z,
            )
            copy.start()
            self.lasts.append(copy)

    def finish(self):
        for copy in self.lasts:
            copy.wait_recv()
        total = self.source[self.y, self.x].astype(F32)
        for step in range(3):
            total = total + self.landed_last[step].astype(F32)
        return total

    def sent(self):
        for copy in self.firsts + self.lasts:
            copy.wait_send()


FF_ITEMS = (
    (0, 0, 640, True),
    (0, 640, 512, False),
    (1, 0, 512, True),
    (1, 512, 640, False),
    (2, 0, 640, True),
    (2, 640, 512, False),
)
LATE_ITEMS = ((0, 384, True), (384, 384, False))
SUM_WIDTHS = [item[2] for item in FF_ITEMS] + [item[1] for item in LATE_ITEMS] + [128]

INPUTS = [
    "x",
    "attention_gain",
    "wq",
    "wk",
    "wv",
    "query_gain",
    "key_gain",
    "row_cos",
    "row_sin",
    "block_cos",
    "block_sin",
    "feed_gain",
]
STREAMED = ["cot", "wo", "wg", "wu", "wd"]
OUTPUTS = {
    "block": ((4, 96, 1024), BF16),
    "rows_out": ((4, 96, 1024), BF16),
    "gate_sum": ((32, 1152), F32),
    "up_sum": ((32, 1152), F32),
    "down_sum": ((32, 1152), F32),
    "late_sum": ((32, 768), F32),
    "gain_sum": ((32, 128), F32),
}
BUFFERS = {
    "cot": ((ROWS, 1024), BF16),
    "wg": ((1024, 1152), BF16),
    "wu": ((1024, 1152), BF16),
    "wd": ((1024, 1152), BF16),
    "wall": ((1024, 1024), BF16),
    "normed": ((ROWS, 1024), BF16),
    "normed_t": ((1024, ROWS), BF16),
    "pair_gains": ((8, 128), F32),
    "qraw": ((ROWS, 256), F32),
    "kraw": ((ROWS, 128), F32),
    "q": ((2, ROWS, 128), BF16),
    "kv": ((2, ROWS, 128), BF16),
    "kvs": ((16, ROWS, 128), BF16),
    "qs": ((2, ROWS, 128), BF16),
    "os": ((2, ROWS, 128), BF16),
    "l2": ((2, 8, 2 * ROWS), F32),
    "qz": ((2, 2 * ROWS, 128), BF16),
    "acc": ((2, 2 * ROWS, 128), F32),
    "sums": ((2, 2 * ROWS, 128), F32),
    "oall": ((ROWS, 1024), BF16),
    "hidden": ((ROWS, 1024), F32),
    "scale": ((ROWS, 128), F32),
    "mixed": ((ROWS, 1024), BF16),
    "mixed_t": ((1024, ROWS), BF16),
    "cot_t": ((1024, ROWS), BF16),
    "inner": ((ROWS, 1152), BF16),
    "grad_gate": ((ROWS, 1152), BF16),
    "grad_up": ((ROWS, 1152), BF16),
    "total": ((ROWS, 1024), F32),
    "part_send": ((4, 96, 1024), BF16),
    "part_land": ((3, 96, 1024), BF16),
    "down_send": ((4, 96, 1024), BF16),
    "down_land": ((3, 96, 1024), BF16),
    "dw_g": ((2, 4, 4, 32, 1152), BF16),
    "dw_u": ((2, 4, 4, 32, 1152), BF16),
    "dw_d": ((2, 4, 4, 32, 1152), BF16),
    "land_g": ((4, 4, 32, 1152), BF16),
    "land_u": ((4, 4, 32, 1152), BF16),
    "land_d": ((4, 4, 32, 1152), BF16),
    "grad_rows": ((96, 1024), F32),
    "branch": ((4, 96, 1024), BF16),
    "dob": ((96, 1024), BF16),
    "doz": ((2, 2 * ROWS, 128), BF16),
    "delta": ((2, 8, 2 * ROWS), F32),
    "dos": ((2, ROWS, 128), BF16),
    "dqt": ((2, 128, 2 * ROWS), F32),
    "dq_out": ((2, ROWS, 128), BF16),
    "dq_in": ((2, ROWS, 128), BF16),
    "dkv_out": ((16, ROWS, 128), BF16),
    "dkv_in": ((2, 4, ROWS, 128), BF16),
    "dkv_part": ((8, ROWS, 128), BF16),
    "dkv": ((2, ROWS, 128), F32),
    "grads": ((ROWS, 512), BF16),
    "last_send": ((4, 96, 1024), BF16),
    "last_land": ((3, 96, 1024), BF16),
    "late": ((2, 4, 4, 32, 768), BF16),
    "late_land": ((4, 4, 32, 768), BF16),
    "gains": ((8, 1024), F32),
    "gains_land": ((3, 8, 1024), F32),
    "chunk_in": ((128, 1024), F32),
    "chunk": ((2, 4, 4, 32, 128), BF16),
    "chunk_land": ((4, 4, 32, 128), BF16),
}
SEMAPHORES = {
    "load": (5,),
    "q_send": (2,),
    "q_recv": (2,),
    "kv_send": (8,),
    "hand_send": (8,),
    "kv_recv": (16,),
    "o_send": (2, 4),
    "o_recv": (8,),
    "w_sems": (2, 3),
    "wc_sems": (2, 3),
    "mixed_sems": (2, 6),
    "core_sems": (2, 5),
    "do_send": (2, 4),
    "do_recv": (2, 4),
    "branch_sems": (2, 6),
    "down_sems": (2, 6),
    "block_sems": (2, 6),
    "dq_send": (2,),
    "dq_recv": (2,),
    "dkv_send": (16,),
    "dkv_recv": (2, 4),
    "part_send_sem": (16,),
    "part_recv_sem": (8,),
    "last_sems": (2, 6),
    "gain_sems": (2, 3),
    "rows_sems": (2, 6),
    "sum_first": (2, len(SUM_WIDTHS), 3),
    "sum_last": (2, len(SUM_WIDTHS), 3),
}


def columns_of(t, width):
    return pl.ds(pl.multiple_of(t * width, width), width)


def transpose_into(out, source):
    def move(t, carry):
        columns = columns_of(t, 128)
        out[columns, :] = source[:, columns].T
        return carry

    lax.fori_loop(0, 8, move, 0)


def block_kernel(*refs):
    names = INPUTS + ["hbm_" + name for name in STREAMED] + list(OUTPUTS) + list(BUFFERS)
    names += list(SEMAPHORES)
    r = SimpleNamespace(**dict(zip(names, refs)))
    landings = refs[len(names) :]
    d, c, z = place()
    s, j_role, low, high = role_of(d, c)
    x = lax.rem(c, 4)
    slot = jnp.where(c >= 8, 1, 0)
    home_core = jnp.where(lower(c) < 4, 0, 1)
    home_column = jnp.where(home_core == 0, lower(c), 7 - lower(c))

    def home(j):
        return (2 * d + j) * 4 + home_column

    def own(i):
        return jnp.where(d == 0, lax.rem(x - i + 8, 4), 4 + lax.rem(11 - x - i, 4))

    def others(i):
        return jnp.where(d == 0, 4 + lax.rem(11 - x - i, 4), lax.rem(x - i + 8, 4))

    column = columns_of(z, 256)
    lane = lanes()

    barrier = pltpu.get_barrier_semaphore()

    def signal(*device):
        pl.semaphore_signal(barrier, inc=1, device_id=device, device_id_type=MESH)

    def greet(index, carry):
        other_d, other_c = index // 16, lax.rem(index, 16)

        @pl.when((other_d != d) | (other_c != c))
        def _():
            signal(other_d, other_c, z)

        return carry

    lax.fori_loop(0, 32, greet, 0)
    for step in (1, 2, 3):
        other = lax.rem(z + step, 4)
        signal(d, c, other)
        for j in range(2):
            signal(home_core, home(j), other)
        for block in (low, high):
            signal(s, block, other)

    load_wo = local_sem(r.hbm_wo, r.wall.at[:, column], r.load.at[0])
    load_cot = local_sem(r.hbm_cot, r.cot, r.load.at[1])
    load_wg = local_sem(r.hbm_wg, r.wg, r.load.at[2])
    load_wu = local_sem(r.hbm_wu, r.wu, r.load.at[3])
    load_wd = local_sem(r.hbm_wd, r.wd, r.load.at[4])
    for copy in (load_wo, load_cot, load_wg, load_wu, load_wd):
        copy.start()

    def first_norm(t, carry):
        rows = columns_of(t, 96)
        values = r.x[rows, :].astype(F32)
        factor = lax.rsqrt(jnp.mean(values * values, axis=1, keepdims=True) + epsilon)
        r.normed[rows, :] = (values * factor * r.attention_gain[...]).astype(BF16)
        return carry

    lax.fori_loop(0, 4, first_norm, 0)
    normed = r.normed[...]
    for half in (0, 64):
        r.pair_gains[0:1, half : half + 64] = r.query_gain[...]
        r.pair_gains[1:2, half : half + 64] = r.key_gain[...]
    query_gain, key_gain = r.pair_gains[0:1, :], r.pair_gains[1:2, :]
    cosine, sine = tables(c, r.row_cos, r.row_sin, r.block_cos, r.block_sin)
    key_raw = nn(normed, r.wk[...])
    r.kraw[...] = key_raw
    value = nn(normed, r.wv[...])
    key = pair_forward(key_raw, key_gain, cosine, sine)
    r.kv[0] = jnp.where(lane < 64, key, pltpu.roll(value, 64, 1)).astype(BF16)
    r.kv[1] = jnp.where(lane < 64, pltpu.roll(key, 64, 1), value).astype(BF16)
    pl.semaphore_wait(barrier, 31 + 3 + 6 + 6)

    def kv_target(k, j):
        column = lax.rem(jnp.where(home_core == 0, home_column + k, home_column - k + 4), 4)
        core = jnp.where((home_core == 1) & (c <= 8 + column), 1, 0)
        return core, (2 * d + j) * 4 + column, c <= 15 - column

    def kv_copy(k, j):
        core, chip, _ = kv_target(k, j)
        return remote(
            r.kv.at[j], r.kvs.at[c], r.kv_send.at[2 * k + j], r.kv_recv.at[c], core, chip, z
        )

    def kv_start(k, carry):
        for j in range(2):
            core, chip, needed = kv_target(k, j)
            here = (core == d) & (chip == c)

            @pl.when(needed & jnp.logical_not(here))
            def _():
                kv_copy(k, j).start()

            @pl.when(needed & here)
            def _():
                local_sem(r.kv.at[j], r.kvs.at[c], r.kv_recv.at[c]).start()

        return carry

    def q_copy(j):
        return remote(r.q.at[j], r.qs.at[slot], r.q_send.at[j], r.q_recv.at[slot], home_core, home(j), z)

    kv_start(0, 0)
    query_raw = nn(normed, r.wq[...])
    r.qraw[...] = query_raw
    for j in range(2):
        pair = query_raw[:, j * 128 : (j + 1) * 128]
        r.q[j] = pair_forward(pair, query_gain, cosine, sine).astype(BF16)
        here = (home(j) == c) & (home_core == d)

        @pl.when(jnp.logical_not(here))
        def _():
            q_copy(j).start()

        @pl.when(here)
        def _():
            local_sem(r.q.at[j], r.qs.at[slot], r.q_recv.at[slot]).start()

    lax.fori_loop(1, 4, kv_start, 0)

    load_wo.wait()
    mine = columns_of(d, 512)
    w_copies = z_send(
        lambda other: r.wall.at[mine, column],
        lambda step: r.wall.at[mine, column],
        r.w_sems,
        d,
        c,
        z,
    )

    transpose_into(r.normed_t, r.normed)
    load_cot.wait()
    transpose_into(r.cot_t, r.cot)

    r.acc[...] = jnp.zeros_like(r.acc)
    r.sums[...] = jnp.zeros_like(r.sums)
    for which in range(2):
        local_sem(r.q.at[0], r.qs.at[which], r.q_recv.at[which]).wait()
        first, second = spread_heads(r.qs[which], False)
        r.qz[which, 0:ROWS, :] = first
        r.qz[which, ROWS : 2 * ROWS, :] = second

    def kv_wait(block):
        local_sem(r.kv.at[0], r.kvs.at[block], r.kv_recv.at[block]).wait()

    def forward_tile(block, which, masked):
        keys = r.kvs[block]
        for head in range(2):
            rows = slice(head * ROWS, (head + 1) * ROWS)
            weights = jnp.exp2(nt(r.qz[which, rows, :], keys) * SCORE_SCALE)
            if masked:
                row = lax.broadcasted_iota(jnp.int32, weights.shape, 0)
                key = lax.broadcasted_iota(jnp.int32, weights.shape, 1)
                weights = jnp.where(row >= key, weights, 0.0)
            r.sums[which, rows, :] += weights[:, 0:128] + weights[:, 128:256] + weights[:, 256:384]
            r.acc[which, rows, :] += nn(weights.astype(BF16), keys)

    def hand_on(index, block):
        return remote(
            r.kvs.at[block],
            r.kvs.at[block],
            r.hand_send.at[index],
            r.kv_recv.at[block],
            1 - d,
            c,
            z,
        )

    kv_wait(low)
    kv_wait(high)
    hand_on(0, low).start()

    @pl.when(d == 1)
    def _():
        hand_on(1, high).start()

    forward_tile(low, 1, False)
    forward_tile(low, 0, True)
    forward_tile(high, 1, True)

    def forward_step(k, carry):
        first = jnp.where(k < 4, own(k), others(k - 4))
        below = first < low
        kv_wait(first)

        @pl.when(k < 4)
        def _():
            hand_on(2 * k, first).start()

        @pl.when(jnp.logical_not(below))
        def _():
            kv_wait(15 - first)

            @pl.when((k < 4) & (d == 1))
            def _():
                hand_on(2 * k + 1, 15 - first).start()

        forward_tile(first, 1, False)
        forward_tile(jnp.where(below, first, 15 - first), jnp.where(below, 0, 1), False)
        return carry

    lax.fori_loop(1, 8, forward_step, 0)

    def o_copy(which, step):
        block = high if which else low
        other = lax.rem(z + step, 4)
        there = r.oall.at[:, columns_of(z * 2 + j_role, 128)]
        arrived = r.o_recv.at[z * 2 + j_role]
        return r.os.at[which], there, r.o_send.at[which, step], arrived, s, block, other

    for which in range(2):
        total = jnp.sum(r.sums[which], axis=1, keepdims=True)
        result = r.acc[which] / total
        r.os[which] = jnp.where(
            lane < 64, pltpu.roll(result[:ROWS], 64, 1), result[ROWS:]
        ).astype(BF16)
        block = high if which else low
        here = (s == d) & (block == c)
        for step in (2, 1, 3):
            remote(*o_copy(which, step)).start()

        @pl.when(jnp.logical_not(here))
        def _():
            remote(*o_copy(which, 0)).start()

        @pl.when(here)
        def _():
            source, there, _, arrived = o_copy(which, 0)[:4]
            local_sem(source, there, arrived).start()

    forwards = []
    for copy, step in zip(w_copies, (2, 1, 3)):
        copy.wait_recv()
        theirs = columns_of(lax.rem(z + 4 - step, 4), 256)
        forward = remote(
            r.wall.at[mine, theirs],
            r.wall.at[mine, theirs],
            r.wc_sems.at[0, step - 1],
            r.wc_sems.at[1, step - 1],
            1 - d,
            c,
            z,
        )
        forward.start()
        forwards.append(forward)
    for which in range(2):
        total = jnp.sum(r.sums[which], axis=1, keepdims=True)
        logs = jnp.broadcast_to(jnp.log2(total), (2 * ROWS, 128))
        r.l2[which] = logs.T[0:8]
    for forward in forwards:
        forward.wait_recv()
    for source in range(4):
        for j in range(2):
            there = r.oall.at[:, source * 256 + j * 128 : source * 256 + (j + 1) * 128]
            local_sem(r.os.at[0], there, r.o_recv.at[source * 2 + j]).wait()

    def project_out(t, carry):
        columns = columns_of(t, 256)
        r.hidden[:, columns] = r.x[:, columns].astype(F32) + nt(r.oall[...], r.wall[columns, :])
        return carry

    lax.fori_loop(0, 4, project_out, 0)

    def second_norm(t, carry):
        rows = columns_of(t, 96)
        values = r.hidden[rows, :]
        factor = lax.rsqrt(jnp.mean(values * values, axis=1, keepdims=True) + epsilon)
        r.scale[rows, :] = jnp.broadcast_to(factor, (96, 128))
        r.mixed[rows, :] = (values * factor * r.feed_gain[...]).astype(BF16)
        return carry

    lax.fori_loop(0, 4, second_norm, 0)
    r.total[...] = jnp.zeros_like(r.total)
    load_wg.wait()
    load_wu.wait()
    load_wd.wait()

    def units(t, carry):
        columns = columns_of(t, 384)
        gate = nn(r.mixed[...], r.wg[:, columns])
        up = nn(r.mixed[...], r.wu[:, columns])
        sigmoid = 1.0 / (1.0 + jnp.exp(-gate))
        silu = gate * sigmoid
        r.inner[:, columns] = (silu * up).astype(BF16)
        grad_inner = nn(r.cot[...], r.wd[:, columns])
        r.grad_up[:, columns] = (grad_inner * silu).astype(BF16)
        r.grad_gate[:, columns] = (
            grad_inner * up * sigmoid * (1.0 + gate * (1.0 - sigmoid))
        ).astype(BF16)
        r.total[...] += nt(r.grad_gate[:, columns], r.wg[:, columns]) + nt(
            r.grad_up[:, columns], r.wu[:, columns]
        )
        return carry

    lax.fori_loop(0, 3, units, 0)
    for other in range(4):
        r.part_send[other] = r.total[other * 96 : (other + 1) * 96, :].astype(BF16)
    reduce_mixed = ZReduce(r.part_send, r.part_land, r.mixed_sems, d, c, z).start()

    def to_other_core(index, source, land):
        copy = remote(
            source.at[1 - d], land, r.core_sems.at[0, index], r.core_sems.at[1, index], 1 - d, c, z
        )
        copy.start()
        return copy

    def add_cores(copy, source, land):
        copy.wait_recv()

        def add(t, carry):
            source[d, t] = (source[d, t].astype(F32) + land[t].astype(F32)).astype(BF16)
            return carry

        lax.fori_loop(0, 4, add, 0)

    transpose_into(r.mixed_t, r.mixed)
    cores = []
    for index, (left, right, out, land) in enumerate(
        (
            (r.mixed_t, r.grad_gate, r.dw_g, r.land_g),
            (r.mixed_t, r.grad_up, r.dw_u, r.land_u),
            (r.cot_t, r.inner, r.dw_d, r.land_d),
        )
    ):

        def weights(t, carry):
            columns = columns_of(t, 384)
            value = nn(left[...], right[:, columns]).astype(BF16)
            out[:, :, :, :, columns] = value.reshape(2, 4, 4, 32, 384)
            return carry

        lax.fori_loop(0, 3, weights, 0)
        cores.append(to_other_core(index, out, land))
        if index == 0:
            reduce_mixed.relay()

    def project_down(t, carry):
        columns = columns_of(t, 256)
        value = nt(r.inner[...], r.wd[columns, :])
        for other in range(4):
            r.down_send[other, :, columns] = value[other * 96 : (other + 1) * 96].astype(BF16)
        return carry

    lax.fori_loop(0, 4, project_down, 0)

    rows = columns_of(z, 96)
    incoming = r.total[rows, :] + reduce_mixed.finish()
    values = r.hidden[rows, :]
    factor = r.scale[rows, 0:1]
    weighted = incoming * r.feed_gain[...]
    projected = jnp.sum(weighted * values, axis=1, keepdims=True) * (1.0 / 1024.0)
    grad_rows = (
        r.cot[rows, :].astype(F32)
        + factor * weighted
        - values * (factor * factor * factor * projected)
    )
    r.gains[...] = jnp.zeros_like(r.gains)
    r.gains[1:2, :] = jnp.sum(incoming * values * factor, axis=0, keepdims=True)
    r.grad_rows[...] = grad_rows
    r.branch[z] = grad_rows.astype(BF16)

    def attended(t, carry):
        columns = columns_of(t, 256)
        r.dob[:, columns] = nn(r.branch[z], r.wall[:, columns]).astype(BF16)
        return carry

    lax.fori_loop(0, 4, attended, 0)

    def do_copy(j, step):
        other = lax.rem(z + step, 4)
        source = r.dob.at[:, columns_of(other * 2 + j, 128)]
        there = r.dos.at[slot, columns_of(z, 96)]
        sems = (r.do_send.at[j, step], r.do_recv.at[slot, z])
        return source, there, *sems, home_core, home(j), other

    for j in range(2):
        for step in (2, 1, 3):
            remote(*do_copy(j, step)).start()
        here = (home(j) == c) & (home_core == d)

        @pl.when(jnp.logical_not(here))
        def _():
            remote(*do_copy(j, 0)).start()

        @pl.when(here)
        def _():
            source, there, _, arrived = do_copy(j, 0)[:4]
            local_sem(source, there, arrived).start()

    gather_branch = ZGather(r.branch, r.branch_sems, d, c, z).start()
    reduce_down = ZReduce(r.down_send, r.down_land, r.down_sems, d, c, z).start()

    weight_grads = (r.dw_g, r.dw_u, r.dw_d)
    lands = (r.land_g, r.land_u, r.land_d)
    sources = [
        weight_grads[index].at[d, :, :, :, start : start + width]
        for index, start, width, _ in FF_ITEMS
    ]
    sources += [r.late.at[d, :, :, :, start : start + width] for start, width, _ in LATE_ITEMS]
    sources += [r.chunk.at[d]]
    y_firsts = [item[3] for item in FF_ITEMS] + [item[2] for item in LATE_ITEMS] + [True]
    plane = [
        PlaneSum(
            i,
            sources[i],
            y_firsts[i],
            landings[2 * i],
            landings[2 * i + 1],
            (r.sum_first, r.sum_last),
        )
        for i in range(len(sources))
    ]
    gate_items, up_items, down_items = plane[0:2], plane[2:4], plane[4:6]
    late_items, gain_item = plane[6:8], plane[8]

    add_cores(cores[0], r.dw_g, r.land_g)
    for item in gate_items:
        item.start()

    r.dqt[...] = jnp.zeros_like(r.dqt)
    for which in range(2):
        for source in range(4):
            there = r.dos.at[which, source * 96 : (source + 1) * 96]
            local_sem(r.dob.at[:, 0:128], there, r.do_recv.at[which, source]).wait()
        first, second = spread_heads(r.dos[which], True)
        r.doz[which, 0:ROWS, :] = first
        r.doz[which, ROWS : 2 * ROWS, :] = second
        product = (r.dos[which].astype(F32) * r.os[which].astype(F32)).T
        r.delta[which, :, 0:ROWS] = jnp.broadcast_to(
            jnp.sum(product[0:64], axis=0, keepdims=True), (8, ROWS)
        )
        r.delta[which, :, ROWS : 2 * ROWS] = jnp.broadcast_to(
            jnp.sum(product[64:128], axis=0, keepdims=True), (8, ROWS)
        )

    key_scale = jnp.where(lane < 64, 0.125, 1.0)

    def backward_tile(block, which, masked):
        keys = r.kvs[block]
        keys_t = keys.T
        result = None
        for head in range(2):
            rows = slice(head * ROWS, (head + 1) * ROWS)
            q_rows = r.qz[which, rows, :]
            do_rows = r.doz[which, rows, :]
            weights = jnp.exp2(nt(keys, q_rows) * SCORE_SCALE - r.l2[which, 0:1, rows])
            if masked:
                key = lax.broadcasted_iota(jnp.int32, weights.shape, 0)
                row = lax.broadcasted_iota(jnp.int32, weights.shape, 1)
                weights = jnp.where(row >= key, weights, 0.0)
            score_grad = (weights * (nt(keys, do_rows) - r.delta[which, 0:1, rows])).astype(BF16)
            part = nn(score_grad, q_rows) + nn(weights.astype(BF16), do_rows)
            result = part if result is None else result + part
            r.dqt[which, :, rows] += nn(keys_t, score_grad)
        return result * key_scale

    def dkv_copy(block):
        return (
            r.dkv_out.at[block],
            r.dkv_in.at[j_role, x],
            r.dkv_send.at[block],
            r.dkv_recv.at[j_role, x],
            s,
            block,
            z,
        )

    def dkv_start(block):
        here = (s == d) & (block == c)

        @pl.when(jnp.logical_not(here))
        def _():
            remote(*dkv_copy(block)).start()

        @pl.when(here)
        def _():
            source, there, _, arrived = dkv_copy(block)[:4]
            local_sem(source, there, arrived).start()

    def of_both(block):
        return (block < 4) | ((block >= 4) & (block <= 8 + x))

    def class_of(block):
        return jnp.where(lower(block) < 4, 0, 1)

    def part_copy(block):
        index = lax.rem(block, 8)
        return remote(
            r.dkv_out.at[block],
            r.dkv_part.at[index],
            r.part_send_sem.at[block],
            r.part_recv_sem.at[index],
            1 - d,
            c,
            z,
        )

    def dispatch(block):
        both = of_both(block)

        @pl.when(both & (class_of(block) != d))
        def _():
            part_copy(block).start()

        @pl.when(jnp.logical_not(both))
        def _():
            dkv_start(block)

    def combine(block):
        index = lax.rem(block, 8)
        part_copy(block).wait_recv()
        r.dkv_out[block] = (
            r.dkv_out[block].astype(F32) + r.dkv_part[index].astype(F32)
        ).astype(BF16)
        dkv_start(block)

    def combine_own(i):
        first = own(i)
        combine(first)

        @pl.when((d == 1) & (first >= low))
        def _():
            combine(15 - first)

    r.dkv_out[low] = (backward_tile(low, 1, False) + backward_tile(low, 0, True)).astype(BF16)
    r.dkv_out[high] = backward_tile(high, 1, True).astype(BF16)
    dispatch(high)
    gather_branch.relay()
    reduce_down.relay()

    def backward_step(k, carry):
        odd = lax.rem(k, 2) == 1
        first = jnp.where(odd, others((k - 1) // 2), own(k // 2))
        below = first < low
        one = backward_tile(first, 1, False)
        two = backward_tile(jnp.where(below, first, 15 - first), jnp.where(below, 0, 1), False)

        @pl.when(below)
        def _():
            r.dkv_out[first] = (one + two).astype(BF16)
            dispatch(first)

        @pl.when(jnp.logical_not(below))
        def _():
            r.dkv_out[first] = one.astype(BF16)
            dispatch(first)
            r.dkv_out[15 - first] = two.astype(BF16)
            dispatch(15 - first)

        @pl.when(odd & (k >= 3))
        def _():
            combine_own((k - 3) // 2)

        return carry

    lax.fori_loop(1, 8, backward_step, 0)

    def dq_copy(which):
        block = high if which else low
        return (
            r.dq_out.at[which],
            r.dq_in.at[j_role],
            r.dq_send.at[which],
            r.dq_recv.at[j_role],
            s,
            block,
            z,
        )

    for which in range(2):
        flat = r.dqt[which].T * 0.125
        r.dq_out[which] = jnp.where(
            lane < 64, flat[:ROWS], pltpu.roll(flat[ROWS:], 64, 1)
        ).astype(BF16)
        block = high if which else low
        here = (s == d) & (block == c)

        @pl.when(jnp.logical_not(here))
        def _():
            remote(*dq_copy(which)).start()

        @pl.when(here)
        def _():
            source, there, _, arrived = dq_copy(which)[:4]
            local_sem(source, there, arrived).start()

    combine_own(3)
    add_cores(cores[1], r.dw_u, r.land_u)
    for item in up_items:
        item.start()

    block_rows = r.hidden[columns_of(z, 96), :] + r.down_send[z].astype(F32)
    r.block[z] = (block_rows + reduce_down.finish()).astype(BF16)
    gather_block = ZGather(r.block, r.block_sems, d, c, z).start()

    cosine, sine = tables(c, r.row_cos, r.row_sin, r.block_cos, r.block_sin)
    for j in range(2):
        local_sem(r.dq_out.at[0], r.dq_in.at[j], r.dq_recv.at[j]).wait()
    query_part = jnp.zeros((1, 128), F32)
    for j in range(2):
        columns = slice(j * 128, (j + 1) * 128)
        raw_grad, gain_part = pair_backward(
            r.dq_in[j].astype(F32), r.qraw[:, columns], query_gain, cosine, sine
        )
        r.grads[:, columns] = raw_grad.astype(BF16)
        query_part = query_part + gain_part
    r.gains[2:3, 0:128] = query_part + pltpu.roll(query_part, 64, 1)

    def project_query(t, carry):
        columns = columns_of(t, 256)
        r.total[:, columns] = nt(r.grads[:, 0:256], r.wq[columns, :])
        return carry

    lax.fori_loop(0, 4, project_query, 0)
    r.late[:, :, :, :, 0:256] = (
        nn(r.normed_t[...], r.grads[:, 0:256]).astype(BF16).reshape(2, 4, 4, 32, 256)
    )
    gather_branch.finish()
    for source in range(4):

        def move(t, carry):
            columns = columns_of(t, 128)
            r.mixed_t[columns, source * 96 : (source + 1) * 96] = r.branch[source, :, columns].T
            return carry

        lax.fori_loop(0, 8, move, 0)
    r.late[:, :, :, :, 512:768] = (
        nn(r.mixed_t[...], r.oall[:, column]).astype(BF16).reshape(2, 4, 4, 32, 256)
    )
    gather_block.relay()
    for item in gate_items:
        item.middle()

    for j in range(2):
        r.dkv[j] = jnp.zeros((ROWS, 128), F32)

    def collect(column, carry):
        @pl.when(c <= 15 - column)
        def _():
            for j in range(2):
                local_sem(
                    r.dkv_out.at[0], r.dkv_in.at[j, column], r.dkv_recv.at[j, column]
                ).wait()
                r.dkv[j] += r.dkv_in[j, column].astype(F32)

        return carry

    lax.fori_loop(0, 4, collect, 0)
    first, second = r.dkv[0], r.dkv[1]
    raw_grad, key_part = pair_backward(
        jnp.where(lane < 64, first, pltpu.roll(second, 64, 1)),
        r.kraw[...],
        key_gain,
        cosine,
        sine,
    )
    r.grads[:, 256:384] = raw_grad.astype(BF16)
    r.grads[:, 384:512] = jnp.where(lane < 64, pltpu.roll(first, 64, 1), second).astype(BF16)
    r.gains[3:4, 0:128] = key_part + pltpu.roll(key_part, 64, 1)

    def project_keys(t, carry):
        columns = columns_of(t, 256)
        value = (
            r.total[:, columns]
            + nt(r.grads[:, 256:384], r.wk[columns, :])
            + nt(r.grads[:, 384:512], r.wv[columns, :])
        ).astype(BF16)
        for other in range(4):
            r.last_send[other, :, columns] = value[other * 96 : (other + 1) * 96]
        return carry

    lax.fori_loop(0, 4, project_keys, 0)
    reduce_last = ZReduce(r.last_send, r.last_land, r.last_sems, d, c, z).start()
    add_cores(cores[2], r.dw_d, r.land_d)
    for item in down_items:
        item.start()
    r.late[:, :, :, :, 256:512] = (
        nn(r.normed_t[...], r.grads[:, 256:512]).astype(BF16).reshape(2, 4, 4, 32, 256)
    )
    late_core = to_other_core(3, r.late, r.late_land)
    reduce_last.relay()
    for item in up_items:
        item.middle()

    rows = columns_of(z, 96)
    incoming = r.last_send[z].astype(F32) + reduce_last.finish()
    values = r.x[rows, :].astype(F32)
    factor = lax.rsqrt(jnp.mean(values * values, axis=1, keepdims=True) + epsilon)
    weighted = incoming * r.attention_gain[...]
    projected = jnp.sum(weighted * values, axis=1, keepdims=True) * (1.0 / 1024.0)
    r.gains[0:1, :] = jnp.sum(incoming * values * factor, axis=0, keepdims=True)
    gather_gains = z_send(
        lambda other: r.gains, lambda step: r.gains_land.at[step - 1], r.gain_sems, d, c, z
    )
    r.rows_out[z] = (
        r.grad_rows[...] + factor * weighted - values * (factor * factor * factor * projected)
    ).astype(BF16)
    gather_rows = ZGather(r.rows_out, r.rows_sems, d, c, z).start()
    add_cores(late_core, r.late, r.late_land)
    for item in late_items:
        item.start()

    for copy in gather_gains:
        copy.wait_recv()
    r.chunk_in[...] = jnp.zeros_like(r.chunk_in)
    r.chunk_in[0:8, :] = r.gains[...] + r.gains_land[0] + r.gains_land[1] + r.gains_land[2]
    column_part = r.chunk_in[...].T
    row_kind = lax.rem(lax.broadcasted_iota(jnp.int32, (1024, 128), 0), 32)
    lane_index = lax.broadcasted_iota(jnp.int32, (1024, 128), 1)
    query_total, key_total = r.chunk_in[2:3, 0:128], r.chunk_in[3:4, 0:128]
    spread = jnp.where(row_kind == 0, query_total, jnp.where(row_kind == 1, key_total, 0.0))
    r.chunk[...] = (
        jnp.where(lane_index < 64, column_part, spread).astype(BF16).reshape(2, 4, 4, 32, 128)
    )
    chunk_core = to_other_core(4, r.chunk, r.chunk_land)
    gather_rows.relay()
    for item in down_items:
        item.middle()
    add_cores(chunk_core, r.chunk, r.chunk_land)
    gain_item.start()
    for item in late_items:
        item.middle()
    gain_item.middle()

    sums = (r.gate_sum, r.up_sum, r.down_sum)
    for item, (index, start, width, _) in zip(plane[:6], FF_ITEMS):
        sums[index][:, start : start + width] = item.finish()
    for item, (start, width, _) in zip(late_items, LATE_ITEMS):
        r.late_sum[:, start : start + width] = item.finish()
    r.gain_sum[...] = gain_item.finish()
    gather_block.finish()
    gather_rows.finish()

    copies = w_copies + forwards + cores + gather_gains + [late_core, chunk_core]
    for transfer in (
        reduce_mixed,
        gather_branch,
        reduce_down,
        gather_block,
        reduce_last,
        gather_rows,
    ):
        copies = copies + transfer.copies
    for copy in copies:
        copy.wait_send()
    for item in plane:
        item.sent()
    for j in range(2):

        @pl.when(jnp.logical_not((home(j) == c) & (home_core == d)))
        def _():
            q_copy(j).wait_send()
            remote(*do_copy(j, 0)).wait_send()

        for step in (1, 2, 3):
            remote(*do_copy(j, step)).wait_send()

    def kv_sent(k, carry):
        for j in range(2):
            core, chip, needed = kv_target(k, j)

            @pl.when(needed & jnp.logical_not((core == d) & (chip == c)))
            def _():
                kv_copy(k, j).wait_send()

        first = own(k)
        hand_on(2 * k, first).wait_send()

        @pl.when((d == 1) & (first >= low))
        def _():
            hand_on(2 * k + 1, 15 - first).wait_send()

        return carry

    lax.fori_loop(0, 4, kv_sent, 0)
    for which in range(2):
        block = high if which else low
        for step in (1, 2, 3):
            remote(*o_copy(which, step)).wait_send()

        @pl.when(jnp.logical_not((s == d) & (block == c)))
        def _():
            remote(*o_copy(which, 0)).wait_send()
            remote(*dq_copy(which)).wait_send()

    def dkv_sent(block, carry):
        both = of_both(block)
        mine = class_of(block) == d

        @pl.when((block <= high) & both & jnp.logical_not(mine))
        def _():
            part_copy(block).wait_send()

        owner_here = (s == d) & (block == c)

        @pl.when((block <= high) & (jnp.logical_not(both) | mine) & jnp.logical_not(owner_here))
        def _():
            remote(*dkv_copy(block)).wait_send()

        return carry

    lax.fori_loop(0, 16, dkv_sent, 0)


def emit_kernel(
    block, rows, gate, up, down, late, gains,
    block_out, input_grad, attention_gain, query_gain, key_gain,
    wq, wk, wv, wo, feed_gain, wg, wu, wd,
):
    d, c, _ = place()
    for part in range(4):
        block_out[part * 96 : (part + 1) * 96, :] = block[part]
        input_grad[part * 96 : (part + 1) * 96, :] = rows[part].astype(F32)
    wg[...] = gate[...]
    wu[...] = up[...]
    wd[...] = down[...]
    wq[...] = late[:, 0:256]
    wk[...] = late[:, 256:384]
    wv[...] = late[:, 384:512]
    wo[...] = late[:, 512:768]
    turned = gains[...].T
    attention_gain[...] = turned[0:1, :]
    feed_gain[...] = turned[1:2, :]
    first = 64 + 2 * (d * 16 + c)
    lane = lax.broadcasted_iota(jnp.int32, (1, 128), 1)
    pair = lax.broadcasted_iota(jnp.int32, (1, 2), 1)
    for row, out in ((0, query_gain), (1, key_gain)):
        values = gains[row : row + 1, :]
        one = jnp.sum(jnp.where(lane == first, values, 0.0), axis=1, keepdims=True)
        two = jnp.sum(jnp.where(lane == first + 1, values, 0.0), axis=1, keepdims=True)
        out[...] = jnp.where(pair == 0, one, two)


def shards(
    inputs,
    cotangent,
    attention_gain,
    query_gain,
    key_gain,
    w_query,
    key_weight,
    value_weight,
    w_out,
    feed_gain,
    w_gate,
    w_up,
    w_down,
):
    vmem, anywhere = pl.BlockSpec(memory_space=pltpu.VMEM), pl.BlockSpec(memory_space=pl.ANY)
    landings = []
    for width in SUM_WIDTHS:
        landings += [pltpu.VMEM((3, 4, 32, width), BF16), pltpu.VMEM((3, 32, width), BF16)]
    results = pl.pallas_call(
        block_kernel,
        out_shape=[jax.ShapeDtypeStruct(*spec) for spec in OUTPUTS.values()],
        in_specs=[vmem] * len(INPUTS) + [anywhere] * len(STREAMED),
        out_specs=[vmem] * len(OUTPUTS),
        scratch_shapes=[pltpu.VMEM(*spec) for spec in BUFFERS.values()]
        + [pltpu.SemaphoreType.DMA(shape) for shape in SEMAPHORES.values()]
        + landings,
        compiler_params=pltpu.CompilerParams(
            collective_id=1, has_side_effects=True, vmem_limit_bytes=VMEM_LIMIT
        ),
        name="block",
    )(
        inputs,
        attention_gain.reshape(1, 1024),
        w_query,
        key_weight,
        value_weight,
        query_gain.reshape(1, 64),
        key_gain.reshape(1, 64),
        *[jnp.asarray(table) for table in split_columns()],
        feed_gain.reshape(1, 1024),
        cotangent,
        w_out,
        w_gate,
        w_up,
        w_down,
    )
    shapes = [
        ((ROWS, 1024), BF16),
        ((ROWS, 1024), F32),
        ((1, 32), F32),
        ((1, 2), F32),
        ((1, 2), F32),
        ((32, 256), F32),
        ((32, 128), F32),
        ((32, 128), F32),
        ((32, 256), F32),
        ((1, 32), F32),
        ((32, 1152), F32),
        ((32, 1152), F32),
        ((32, 1152), F32),
    ]
    outputs = pl.pallas_call(
        emit_kernel,
        out_shape=[jax.ShapeDtypeStruct(*spec) for spec in shapes],
        in_specs=[vmem] * len(results),
        out_specs=[vmem] * len(shapes),
        compiler_params=pltpu.CompilerParams(vmem_limit_bytes=VMEM_LIMIT),
        name="emit",
    )(*results)
    return tuple(
        value.reshape(-1) if value.shape[0] == 1 else value for value in outputs
    )


def solution(mesh):
    both = ("dp", "ctx")
    by_head = P(None, "head")
    reduced = P(both, "head")
    return jax.shard_map(
        shards,
        mesh=mesh,
        in_specs=(
            P(both, None),
            P(both, None),
            P(),
            P(),
            P(),
            by_head,
            by_head,
            by_head,
            by_head,
            P(),
            by_head,
            by_head,
            by_head,
        ),
        out_specs=(
            P(both, None),
            P(both, None),
            P(both),
            P(both),
            P(both),
            reduced,
            reduced,
            reduced,
            reduced,
            P(both),
            reduced,
            reduced,
            reduced,
        ),
        check_vma=False,
    )
```

time: 1430 us -> 146 us (0.10)
  waiting for transfers between devices: 1030 us -> 0 us
  Pallas kernels: 0 us -> 144 us
  local copies, waits for them, and re-layouts: 107 us -> 0 us
  other arithmetic: 90.7 us -> 0 us
  matrix products: 89.9 us -> 0 us
  blocking collectives: 76.5 us -> 0 us
  between operations: 17.1 us -> 0.81 us
    reduce_scatter x6 -> x0, waiting for transfers between devices: 468 us -> none  [the longest x1 80.6 us: shards(): lax.psum_scatter(w_up_grad.astype(jnp.bfloat16), ('dp', 'ctx'), scatter_d...]
    unnamed x17 -> x0, waiting for transfers between devices: 339 us -> none
    pallas_call x0 -> x2, Pallas kernels: none -> 144 us  [the longest x1 141 us: shards(): pl.pallas_call(block_kernel, out_shape=[jax.ShapeDtypeStruct(*spec) for s...]
    psum x3 -> x0, waiting for transfers between devices: 139 us -> none  [the longest x1 53.9 us: shards(): lax.psum(down_part.astype(jnp.bfloat16), 'head').astype(jnp.float32)]
    dot_general x28 -> x0, matrix products: 89.9 us -> none  [the longest x7 20.4 us: contract_rows(): lax.dot_general(left_side, right_side, (((0,), (0,)), ((), ())), preferre...]
    all_gather x2 -> x0, waiting for transfers between devices: 85 us -> none  [the longest x1 46.3 us: shards(): lax.all_gather(value_bf, 'ctx', axis=0, tiled=True)]
    unnamed x1 -> x0, blocking collectives: 69 us -> none
    add x21 -> x0, other arithmetic: 33.9 us -> none  [the longest x16 27.8 us: backward_step(): grad_query + query_add]
  transfers between devices with their start and end apart: 14 -> 0, of which waited for: 14 -> 0; matrix products, arithmetic and copies ran while one was open for 5% -> 0% of each run, Pallas kernels for 0% -> 0%
where the time goes in v3:
time: 146 us; the launch traced here: 145 us
  Pallas kernels  144 us (99%)
    pallas_call x1, Pallas kernels, shards(): pl.pallas_call(block_kernel, out_shape=[jax.ShapeDtypeStruct(*spec) for s...  141 us
    pallas_call x1, Pallas kernels, shards(): pl.pallas_call(emit_kernel, out_shape=[jax.ShapeDtypeStruct(*spec) for sp...  3.21 us

profile of v3, /device:TPU:1, one launch (start us, length us, event | category | flops | bytes accessed | tf_op | source)
XLA Modules:
  0.0 144.8 jit_solution(9936537608004289421)
XLA Ops:
  0.6 140.8 %block.1 = (bf16[4,96,1024]{2,1,0:T(8,128)(2,1)}, bf16[4,96,1024]{2,1,0:T(8,128)(2,1)}, f32[32,1152]{1,0:T(8,128)}, f32[32,1152]{1,0:T(8,128)}, f32[32,1152]{1,0...) custom-call(bf16[384,1024]{1,0:T(8,128)(2,1)} %refs_0_.1, f32[1,1024]{1,0:T(1,128)} %bitcast.8, ...), custom_call_target="tpu_custom_call" | custom-call | tf_op jit(solution)/shard_map/block/pallas_call | solution.py:1290
  141.5 3.2 %emit.1 = (bf16[384,1024]{1,0:T(8,128)(2,1)}, f32[384,1024]{1,0:T(8,128)}, f32[1,32]{1,0:T(1,128)}, f32[1,2]{1,0:T(1,128)}, f32[1,2]{1,0:T(1,128)}, /*index=5*/f...) custom-call(bf16[4,96,1024]{2,1,0:T(8,128)(2,1)} %get-tuple-element., ...), custom_call_target="tpu_custom_call" | custom-call | tf_op jit(solution)/shard_map/emit/pallas_call | solution.py:1333

commit v4 on v3

--- a/solution.py
+++ b/solution.py
@@ -145,68 +145,63 @@
     return copies
 
 
-class ZReduce:
+class ZDirectReduce:
     def __init__(self, part, land, sems, d, c, z):
-        self.part, self.land, self.sems = part, land, sems
-        self.d, self.c = d, c
-        self.up, self.down, self.across = lax.rem(z + 1, 4), lax.rem(z + 3, 4), lax.rem(z + 2, 4)
-
-    def copy(self, index, source, there, plane):
+        self.args = (lambda other: part.at[other], lambda step: land.at[step - 1], sems, d, c, z)
+        self.land = land
+
+    def start(self):
+        self.copies = z_send(*self.args)
+        return self
+
+    def finish(self):
+        for copy in self.copies:
+            copy.wait_recv()
+        land = self.land
+        return land[0].astype(F32) + land[1].astype(F32) + land[2].astype(F32)
+
+
+class ZDirectGather:
+    def __init__(self, slots, sems, d, c, z):
+        self.args = (lambda other: slots.at[z], lambda step: slots.at[z], sems, d, c, z)
+
+    def start(self):
+        self.copies = z_send(*self.args)
+        return self
+
+    def finish(self):
+        for copy in self.copies:
+            copy.wait_recv()
+
+
+class ZGather:
+    def __init__(self, slots, sems, d, c, z):
+        self.slots, self.sems = slots, sems
+        self.d, self.c, self.z = d, c, z
+        self.up, self.down = lax.rem(z + 1, 4), lax.rem(z + 3, 4)
+
+    def copy(self, index, block, plane):
         copy = remote(
-            source, there, self.sems.at[0, index], self.sems.at[1, index], self.d, self.c, plane
+            block, block, self.sems.at[0, index], self.sems.at[1, index], self.d, self.c, plane
         )
         copy.start()
         return copy
 
     def start(self):
-        part, land = self.part, self.land
+        low, high = self.slots.at[self.z, 0:48], self.slots.at[self.z, 48:96]
         self.copies = [
-            self.copy(0, part.at[self.across, 0:48], land.at[0, 0:48], self.up),
-            self.copy(1, part.at[self.across, 48:96], land.at[0, 48:96], self.down),
-            self.copy(2, part.at[self.up, 48:96], land.at[1, 48:96], self.up),
-            self.copy(3, part.at[self.down, 0:48], land.at[2, 0:48], self.down),
+            self.copy(0, low, self.up),
+            self.copy(1, high, self.down),
+            self.copy(2, high, self.up),
+            self.copy(3, low, self.down),
         ]
         return self
 
     def relay(self):
-        part, land = self.part, self.land
-        for index, rows, plane in ((0, slice(0, 48), self.up), (1, slice(48, 96), self.down)):
-            self.copies[index].wait_recv()
-            part[plane, rows, :] = (
-                part[plane, rows, :].astype(F32) + land[0, rows, :].astype(F32)
-            ).astype(BF16)
-            self.copies.append(
-                self.copy(4 + index, part.at[plane, rows], land.at[1 + index, rows], plane)
-            )
-
-    def finish(self):
-        for copy in self.copies[2:]:
-            copy.wait_recv()
-        return self.land[1].astype(F32) + self.land[2].astype(F32)
-
-
-class ZGather(ZReduce):
-    def __init__(self, slots, sems, d, c, z):
-        super().__init__(slots, None, sems, d, c, z)
-        self.z = z
-
-    def start(self):
-        low, high = self.part.at[self.z, 0:48], self.part.at[self.z, 48:96]
-        self.copies = [
-            self.copy(0, low, low, self.up),
-            self.copy(1, high, high, self.down),
-            self.copy(2, high, high, self.up),
-            self.copy(3, low, low, self.down),
-        ]
-        return self
-
-    def relay(self):
         self.copies[0].wait_recv()
-        low = self.part.at[self.down, 0:48]
-        self.copies.append(self.copy(4, low, low, self.up))
+        self.copies.append(self.copy(4, self.slots.at[self.down, 0:48], self.up))
         self.copies[1].wait_recv()
-        high = self.part.at[self.up, 48:96]
-        self.copies.append(self.copy(5, high, high, self.down))
+        self.copies.append(self.copy(5, self.slots.at[self.up, 48:96], self.down))
 
     def finish(self):
         for copy in self.copies[2:]:
@@ -294,8 +289,13 @@
     (2, 0, 640, True),
     (2, 640, 512, False),
 )
-LATE_ITEMS = ((0, 384, True), (384, 384, False))
-SUM_WIDTHS = [item[2] for item in FF_ITEMS] + [item[1] for item in LATE_ITEMS] + [128]
+LATE_ITEMS = (
+    (0, 0, 256, True, 0),
+    (0, 256, 256, False, 512),
+    (1, 0, 128, True, 256),
+    (1, 128, 128, False, 384),
+)
+SUM_WIDTHS = [item[2] for item in FF_ITEMS + LATE_ITEMS] + [128]
 
 INPUTS = [
     "x",
@@ -377,13 +377,14 @@
     "grads": ((ROWS, 512), BF16),
     "last_send": ((4, 96, 1024), BF16),
     "last_land": ((3, 96, 1024), BF16),
-    "late": ((2, 4, 4, 32, 768), BF16),
-    "late_land": ((4, 4, 32, 768), BF16),
+    "late": ((2, 4, 4, 32, 512), BF16),
+    "late_land": ((4, 4, 32, 512), BF16),
+    "last": ((2, 4, 4, 32, 256), BF16),
+    "last_core": ((4, 4, 32, 256), BF16),
     "gains": ((8, 1024), F32),
-    "gains_land": ((3, 8, 1024), F32),
+    "gains_land": ((7, 8, 1024), F32),
     "chunk_in": ((128, 1024), F32),
-    "chunk": ((2, 4, 4, 32, 128), BF16),
-    "chunk_land": ((4, 4, 32, 128), BF16),
+    "chunk": ((4, 4, 32, 128), BF16),
 }
 SEMAPHORES = {
     "load": (5,),
@@ -410,7 +411,7 @@
     "part_send_sem": (16,),
     "part_recv_sem": (8,),
     "last_sems": (2, 6),
-    "gain_sems": (2, 3),
+    "gain_sems": (2, 7),
     "rows_sems": (2, 6),
     "sum_first": (2, len(SUM_WIDTHS), 3),
     "sum_last": (2, len(SUM_WIDTHS), 3),
@@ -472,6 +473,7 @@
     for step in (1, 2, 3):
         other = lax.rem(z + step, 4)
         signal(d, c, other)
+        signal(1 - d, c, other)
         for j in range(2):
             signal(home_core, home(j), other)
         for block in (low, high):
@@ -505,7 +507,7 @@
     key = pair_forward(key_raw, key_gain, cosine, sine)
     r.kv[0] = jnp.where(lane < 64, key, pltpu.roll(value, 64, 1)).astype(BF16)
     r.kv[1] = jnp.where(lane < 64, pltpu.roll(key, 64, 1), value).astype(BF16)
-    pl.semaphore_wait(barrier, 31 + 3 + 6 + 6)
+    pl.semaphore_wait(barrier, 31 + 6 + 6 + 6)
 
     def kv_target(k, j):
         column = lax.rem(jnp.where(home_core == 0, home_column + k, home_column - k + 4), 4)
@@ -732,7 +734,7 @@
     lax.fori_loop(0, 3, units, 0)
     for other in range(4):
         r.part_send[other] = r.total[other * 96 : (other + 1) * 96, :].astype(BF16)
-    reduce_mixed = ZReduce(r.part_send, r.part_land, r.mixed_sems, d, c, z).start()
+    reduce_mixed = ZDirectReduce(r.part_send, r.part_land, r.mixed_sems, d, c, z).start()
 
     def to_other_core(index, source, land):
         copy = remote(
@@ -750,13 +752,37 @@
 
         lax.fori_loop(0, 4, add, 0)
 
-    transpose_into(r.mixed_t, r.mixed)
+    weight_grads = (r.dw_g, r.dw_u, r.dw_d)
+    sources = [
+        weight_grads[index].at[d, :, :, :, start : start + width]
+        for index, start, width, _ in FF_ITEMS
+    ]
+    sources += [
+        (r.late, r.last)[index].at[d, :, :, :, start : start + width]
+        for index, start, width, _, _ in LATE_ITEMS
+    ]
+    sources += [r.chunk]
+    y_firsts = [item[3] for item in FF_ITEMS + LATE_ITEMS] + [True]
+    plane = [
+        PlaneSum(
+            i,
+            sources[i],
+            y_firsts[i],
+            landings[2 * i],
+            landings[2 * i + 1],
+            (r.sum_first, r.sum_last),
+        )
+        for i in range(len(sources))
+    ]
+    gate_items, up_items, down_items = plane[0:2], plane[2:4], plane[4:6]
+    late_items, last_items, gain_item = plane[6:8], plane[8:10], plane[10]
+
     cores = []
     for index, (left, right, out, land) in enumerate(
         (
+            (r.cot_t, r.inner, r.dw_d, r.land_d),
             (r.mixed_t, r.grad_gate, r.dw_g, r.land_g),
             (r.mixed_t, r.grad_up, r.dw_u, r.land_u),
-            (r.cot_t, r.inner, r.dw_d, r.land_d),
         )
     ):
 
@@ -769,7 +795,11 @@
         lax.fori_loop(0, 3, weights, 0)
         cores.append(to_other_core(index, out, land))
         if index == 0:
-            reduce_mixed.relay()
+            transpose_into(r.mixed_t, r.mixed)
+        elif index == 1:
+            add_cores(cores[0], r.dw_d, r.land_d)
+            for item in down_items:
+                item.start()
 
     def project_down(t, carry):
         columns = columns_of(t, 256)
@@ -779,6 +809,9 @@
         return carry
 
     lax.fori_loop(0, 4, project_down, 0)
+
+    add_cores(cores[1], r.dw_g, r.land_g)
+    add_cores(cores[2], r.dw_u, r.land_u)
 
     rows = columns_of(z, 96)
     incoming = r.total[rows, :] + reduce_mixed.finish()
@@ -824,33 +857,8 @@
             source, there, _, arrived = do_copy(j, 0)[:4]
             local_sem(source, there, arrived).start()
 
+    reduce_down = ZDirectReduce(r.down_send, r.down_land, r.down_sems, d, c, z).start()
     gather_branch = ZGather(r.branch, r.branch_sems, d, c, z).start()
-    reduce_down = ZReduce(r.down_send, r.down_land, r.down_sems, d, c, z).start()
-
-    weight_grads = (r.dw_g, r.dw_u, r.dw_d)
-    lands = (r.land_g, r.land_u, r.land_d)
-    sources = [
-        weight_grads[index].at[d, :, :, :, start : start + width]
-        for index, start, width, _ in FF_ITEMS
-    ]
-    sources += [r.late.at[d, :, :, :, start : start + width] for start, width, _ in LATE_ITEMS]
-    sources += [r.chunk.at[d]]
-    y_firsts = [item[3] for item in FF_ITEMS] + [item[2] for item in LATE_ITEMS] + [True]
-    plane = [
-        PlaneSum(
-            i,
-            sources[i],
-            y_firsts[i],
-            landings[2 * i],
-            landings[2 * i + 1],
-            (r.sum_first, r.sum_last),
-        )
-        for i in range(len(sources))
-    ]
-    gate_items, up_items, down_items = plane[0:2], plane[2:4], plane[4:6]
-    late_items, gain_item = plane[6:8], plane[8]
-
-    add_cores(cores[0], r.dw_g, r.land_g)
     for item in gate_items:
         item.start()
 
@@ -962,8 +970,6 @@
     r.dkv_out[low] = (backward_tile(low, 1, False) + backward_tile(low, 0, True)).astype(BF16)
     r.dkv_out[high] = backward_tile(high, 1, True).astype(BF16)
     dispatch(high)
-    gather_branch.relay()
-    reduce_down.relay()
 
     def backward_step(k, carry):
         odd = lax.rem(k, 2) == 1
@@ -990,7 +996,12 @@
 
         return carry
 
-    lax.fori_loop(1, 8, backward_step, 0)
+    lax.fori_loop(1, 5, backward_step, 0)
+    gather_branch.relay()
+    block_rows = r.hidden[columns_of(z, 96), :] + r.down_send[z].astype(F32)
+    r.block[z] = (block_rows + reduce_down.finish()).astype(BF16)
+    gather_block = ZGather(r.block, r.block_sems, d, c, z).start()
+    lax.fori_loop(5, 8, backward_step, 0)
 
     def dq_copy(which):
         block = high if which else low
@@ -1022,13 +1033,8 @@
             local_sem(source, there, arrived).start()
 
     combine_own(3)
-    add_cores(cores[1], r.dw_u, r.land_u)
     for item in up_items:
         item.start()
-
-    block_rows = r.hidden[columns_of(z, 96), :] + r.down_send[z].astype(F32)
-    r.block[z] = (block_rows + reduce_down.finish()).astype(BF16)
-    gather_block = ZGather(r.block, r.block_sems, d, c, z).start()
 
     cosine, sine = tables(c, r.row_cos, r.row_sin, r.block_cos, r.block_sin)
     for j in range(2):
@@ -1049,24 +1055,7 @@
         return carry
 
     lax.fori_loop(0, 4, project_query, 0)
-    r.late[:, :, :, :, 0:256] = (
-        nn(r.normed_t[...], r.grads[:, 0:256]).astype(BF16).reshape(2, 4, 4, 32, 256)
-    )
-    gather_branch.finish()
-    for source in range(4):
-
-        def move(t, carry):
-            columns = columns_of(t, 128)
-            r.mixed_t[columns, source * 96 : (source + 1) * 96] = r.branch[source, :, columns].T
-            return carry
-
-        lax.fori_loop(0, 8, move, 0)
-    r.late[:, :, :, :, 512:768] = (
-        nn(r.mixed_t[...], r.oall[:, column]).astype(BF16).reshape(2, 4, 4, 32, 256)
-    )
     gather_block.relay()
-    for item in gate_items:
-        item.middle()
 
     for j in range(2):
         r.dkv[j] = jnp.zeros((ROWS, 128), F32)
@@ -1107,15 +1096,34 @@
         return carry
 
     lax.fori_loop(0, 4, project_keys, 0)
-    reduce_last = ZReduce(r.last_send, r.last_land, r.last_sems, d, c, z).start()
-    add_cores(cores[2], r.dw_d, r.land_d)
-    for item in down_items:
-        item.start()
+    reduce_last = ZDirectReduce(r.last_send, r.last_land, r.last_sems, d, c, z).start()
+
+    r.late[:, :, :, :, 0:256] = (
+        nn(r.normed_t[...], r.grads[:, 0:256]).astype(BF16).reshape(2, 4, 4, 32, 256)
+    )
+    gather_branch.finish()
+    for source in range(4):
+
+        def move(t, carry):
+            columns = columns_of(t, 128)
+            r.mixed_t[columns, source * 96 : (source + 1) * 96] = r.branch[source, :, columns].T
+            return carry
+
+        lax.fori_loop(0, 8, move, 0)
     r.late[:, :, :, :, 256:512] = (
-        nn(r.normed_t[...], r.grads[:, 256:512]).astype(BF16).reshape(2, 4, 4, 32, 256)
+        nn(r.mixed_t[...], r.oall[:, column]).astype(BF16).reshape(2, 4, 4, 32, 256)
     )
     late_core = to_other_core(3, r.late, r.late_land)
-    reduce_last.relay()
+    r.last[...] = nn(r.normed_t[...], r.grads[:, 256:512]).astype(BF16).reshape(2, 4, 4, 32, 256)
+    last_core = to_other_core(4, r.last, r.last_core)
+    for item in down_items + gate_items:
+        item.middle()
+    add_cores(late_core, r.late, r.late_land)
+    for item in late_items:
+        item.start()
+    add_cores(last_core, r.last, r.last_core)
+    for item in last_items:
+        item.start()
     for item in up_items:
         item.middle()
 
@@ -1126,49 +1134,54 @@
     weighted = incoming * r.attention_gain[...]
     projected = jnp.sum(weighted * values, axis=1, keepdims=True) * (1.0 / 1024.0)
     r.gains[0:1, :] = jnp.sum(incoming * values * factor, axis=0, keepdims=True)
-    gather_gains = z_send(
-        lambda other: r.gains, lambda step: r.gains_land.at[step - 1], r.gain_sems, d, c, z
-    )
+    gather_gains = []
+    for step in range(1, 8):
+        copy = remote(
+            r.gains,
+            r.gains_land.at[step - 1],
+            r.gain_sems.at[0, step - 1],
+            r.gain_sems.at[1, step - 1],
+            d if step < 4 else 1 - d,
+            c,
+            lax.rem(z + step, 4),
+        )
+        copy.start()
+        gather_gains.append(copy)
     r.rows_out[z] = (
         r.grad_rows[...] + factor * weighted - values * (factor * factor * factor * projected)
     ).astype(BF16)
-    gather_rows = ZGather(r.rows_out, r.rows_sems, d, c, z).start()
-    add_cores(late_core, r.late, r.late_land)
-    for item in late_items:
-        item.start()
+    gather_rows = ZDirectGather(r.rows_out, r.rows_sems, d, c, z).start()
 
     for copy in gather_gains:
         copy.wait_recv()
     r.chunk_in[...] = jnp.zeros_like(r.chunk_in)
-    r.chunk_in[0:8, :] = r.gains[...] + r.gains_land[0] + r.gains_land[1] + r.gains_land[2]
-    column_part = r.chunk_in[...].T
-    row_kind = lax.rem(lax.broadcasted_iota(jnp.int32, (1024, 128), 0), 32)
-    lane_index = lax.broadcasted_iota(jnp.int32, (1024, 128), 1)
+    gain_total = r.gains[...]
+    for step in range(7):
+        gain_total = gain_total + r.gains_land[step]
+    r.chunk_in[0:8, :] = gain_total
+    column_part = r.chunk_in[:, columns_of(d, 512)].T
+    row_kind = lax.rem(lax.broadcasted_iota(jnp.int32, (512, 128), 0), 32)
+    lane_index = lax.broadcasted_iota(jnp.int32, (512, 128), 1)
     query_total, key_total = r.chunk_in[2:3, 0:128], r.chunk_in[3:4, 0:128]
     spread = jnp.where(row_kind == 0, query_total, jnp.where(row_kind == 1, key_total, 0.0))
     r.chunk[...] = (
-        jnp.where(lane_index < 64, column_part, spread).astype(BF16).reshape(2, 4, 4, 32, 128)
+        jnp.where(lane_index < 64, column_part, spread).astype(BF16).reshape(4, 4, 32, 128)
     )
-    chunk_core = to_other_core(4, r.chunk, r.chunk_land)
-    gather_rows.relay()
-    for item in down_items:
-        item.middle()
-    add_cores(chunk_core, r.chunk, r.chunk_land)
     gain_item.start()
-    for item in late_items:
+    for item in late_items + last_items:
         item.middle()
     gain_item.middle()
 
     sums = (r.gate_sum, r.up_sum, r.down_sum)
     for item, (index, start, width, _) in zip(plane[:6], FF_ITEMS):
         sums[index][:, start : start + width] = item.finish()
-    for item, (start, width, _) in zip(late_items, LATE_ITEMS):
+    for item, (_, _, width, _, start) in zip(late_items + last_items, LATE_ITEMS):
         r.late_sum[:, start : start + width] = item.finish()
     r.gain_sum[...] = gain_item.finish()
     gather_block.finish()
     gather_rows.finish()
 
-    copies = w_copies + forwards + cores + gather_gains + [late_core, chunk_core]
+    copies = w_copies + forwards + cores + gather_gains + [late_core, last_core]
     for transfer in (
         reduce_mixed,
         gather_branch,

time: 146 us -> 143 us (0.979)
  Pallas kernels: 144 us -> 142 us
    pallas_call x1, Pallas kernels: 141 us -> 139 us  [shards(): pl.pallas_call(block_kernel, out_shape=[jax.ShapeDtypeStruct(*spec) for s...]
where the time goes in v4:
time: 143 us
  Pallas kernels  142 us (99%)
    pallas_call x1, Pallas kernels, shards(): pl.pallas_call(block_kernel, out_shape=[jax.ShapeDtypeStruct(*spec) for s...  139 us
    pallas_call x1, Pallas kernels, shards(): pl.pallas_call(emit_kernel, out_shape=[jax.ShapeDtypeStruct(*spec) for sp...  3.21 us

profile of v4, /device:TPU:1, one launch (start us, length us, event | category | flops | bytes accessed | tf_op | source)
XLA Modules:
  0.0 142.7 jit_solution(7398621843662975502)
XLA Ops:
  0.6 138.7 %block.1 = (bf16[4,96,1024]{2,1,0:T(8,128)(2,1)}, bf16[4,96,1024]{2,1,0:T(8,128)(2,1)}, f32[32,1152]{1,0:T(8,128)}, f32[32,1152]{1,0:T(8,128)}, f32[32,1152]{1,0...) custom-call(bf16[384,1024]{1,0:T(8,128)(2,1)} %refs_0_.1, f32[1,1024]{1,0:T(1,128)} %bitcast.8, ...), custom_call_target="tpu_custom_call" | custom-call | tf_op jit(solution)/shard_map/block/pallas_call | solution.py:1303
  139.4 3.2 %emit.1 = (bf16[384,1024]{1,0:T(8,128)(2,1)}, f32[384,1024]{1,0:T(8,128)}, f32[1,32]{1,0:T(1,128)}, f32[1,2]{1,0:T(1,128)}, f32[1,2]{1,0:T(1,128)}, /*index=5*/f...) custom-call(bf16[4,96,1024]{2,1,0:T(8,128)(2,1)} %get-tuple-element., ...), custom_call_target="tpu_custom_call" | custom-call | tf_op jit(solution)/shard_map/emit/pallas_call | solution.py:1346

commit v5 on v4

--- a/solution.py
+++ b/solution.py
@@ -298,11 +298,7 @@
 SUM_WIDTHS = [item[2] for item in FF_ITEMS + LATE_ITEMS] + [128]
 
 INPUTS = [
-    "x",
     "attention_gain",
-    "wq",
-    "wk",
-    "wv",
     "query_gain",
     "key_gain",
     "row_cos",
@@ -311,7 +307,7 @@
     "block_sin",
     "feed_gain",
 ]
-STREAMED = ["cot", "wo", "wg", "wu", "wd"]
+STREAMED = ["x", "wk", "wv", "wq", "cot", "wo", "wg", "wu", "wd"]
 OUTPUTS = {
     "block": ((4, 96, 1024), BF16),
     "rows_out": ((4, 96, 1024), BF16),
@@ -322,6 +318,10 @@
     "gain_sum": ((32, 128), F32),
 }
 BUFFERS = {
+    "x": ((ROWS, 1024), BF16),
+    "wk": ((1024, 128), BF16),
+    "wv": ((1024, 128), BF16),
+    "wq": ((1024, 256), BF16),
     "cot": ((ROWS, 1024), BF16),
     "wg": ((1024, 1152), BF16),
     "wu": ((1024, 1152), BF16),
@@ -387,7 +387,7 @@
     "chunk": ((4, 4, 32, 128), BF16),
 }
 SEMAPHORES = {
-    "load": (5,),
+    "load": (9,),
     "q_send": (2,),
     "q_recv": (2,),
     "kv_send": (8,),
@@ -455,6 +455,18 @@
     column = columns_of(z, 256)
     lane = lanes()
 
+    load_wo = local_sem(r.hbm_wo, r.wall.at[:, column], r.load.at[0])
+    load_cot = local_sem(r.hbm_cot, r.cot, r.load.at[1])
+    load_wg = local_sem(r.hbm_wg, r.wg, r.load.at[2])
+    load_wu = local_sem(r.hbm_wu, r.wu, r.load.at[3])
+    load_wd = local_sem(r.hbm_wd, r.wd, r.load.at[4])
+    load_x = local_sem(r.hbm_x, r.x, r.load.at[5])
+    load_wk = local_sem(r.hbm_wk, r.wk, r.load.at[6])
+    load_wv = local_sem(r.hbm_wv, r.wv, r.load.at[7])
+    load_wq = local_sem(r.hbm_wq, r.wq, r.load.at[8])
+    for copy in (load_x, load_wk, load_wv, load_wq, load_wo):
+        copy.start()
+
     barrier = pltpu.get_barrier_semaphore()
 
     def signal(*device):
@@ -479,13 +491,7 @@
         for block in (low, high):
             signal(s, block, other)
 
-    load_wo = local_sem(r.hbm_wo, r.wall.at[:, column], r.load.at[0])
-    load_cot = local_sem(r.hbm_cot, r.cot, r.load.at[1])
-    load_wg = local_sem(r.hbm_wg, r.wg, r.load.at[2])
-    load_wu = local_sem(r.hbm_wu, r.wu, r.load.at[3])
-    load_wd = local_sem(r.hbm_wd, r.wd, r.load.at[4])
-    for copy in (load_wo, load_cot, load_wg, load_wu, load_wd):
-        copy.start()
+    load_x.wait()
 
     def first_norm(t, carry):
         rows = columns_of(t, 96)
@@ -501,6 +507,8 @@
         r.pair_gains[1:2, half : half + 64] = r.key_gain[...]
     query_gain, key_gain = r.pair_gains[0:1, :], r.pair_gains[1:2, :]
     cosine, sine = tables(c, r.row_cos, r.row_sin, r.block_cos, r.block_sin)
+    load_wk.wait()
+    load_wv.wait()
     key_raw = nn(normed, r.wk[...])
     r.kraw[...] = key_raw
     value = nn(normed, r.wv[...])
@@ -539,6 +547,7 @@
         return remote(r.q.at[j], r.qs.at[slot], r.q_send.at[j], r.q_recv.at[slot], home_core, home(j), z)
 
     kv_start(0, 0)
+    load_wq.wait()
     query_raw = nn(normed, r.wq[...])
     r.qraw[...] = query_raw
     for j in range(2):
@@ -555,6 +564,9 @@
             local_sem(r.q.at[j], r.qs.at[slot], r.q_recv.at[slot]).start()
 
     lax.fori_loop(1, 4, kv_start, 0)
+
+    for copy in (load_cot, load_wg, load_wu, load_wd):
+        copy.start()
 
     load_wo.wait()
     mine = columns_of(d, 512)
@@ -1313,15 +1325,15 @@
         ),
         name="block",
     )(
-        inputs,
         attention_gain.reshape(1, 1024),
-        w_query,
-        key_weight,
-        value_weight,
         query_gain.reshape(1, 64),
         key_gain.reshape(1, 64),
         *[jnp.asarray(table) for table in split_columns()],
         feed_gain.reshape(1, 1024),
+        inputs,
+        key_weight,
+        value_weight,
+        w_query,
         cotangent,
         w_out,
         w_gate,

time: 143 us -> 142 us (level)
  no operation moved by 1% of the time
where the time goes in v5:
time: 142 us
  Pallas kernels  141 us (99%)
    pallas_call x1, Pallas kernels, shards(): pl.pallas_call(block_kernel, out_shape=[jax.ShapeDtypeStruct(*spec) for s...  138 us
    pallas_call x1, Pallas kernels, shards(): pl.pallas_call(emit_kernel, out_shape=[jax.ShapeDtypeStruct(*spec) for sp...  3.21 us

profile of v5, /device:TPU:1, one launch (start us, length us, event | category | flops | bytes accessed | tf_op | source)
XLA Modules:
  0.0 142.1 jit_solution(12164160279098090113)
XLA Ops:
  0.6 138.0 %block.1 = (bf16[4,96,1024]{2,1,0:T(8,128)(2,1)}, bf16[4,96,1024]{2,1,0:T(8,128)(2,1)}, f32[32,1152]{1,0:T(8,128)}, f32[32,1152]{1,0:T(8,128)}, f32[32,1152]{1,0...) custom-call(f32[1,1024]{1,0:T(1,128)} %bitcast.8, f32[1,64]{1,0:T(1,128)} %bitcast.10, f32[1,64]{1,0:T(1,128)} %bitcast.11, ...), custom_call_target="tpu_custom_call" | custom-call | tf_op jit(solution)/shard_map/block/pallas_call | solution.py:1315
  138.7 3.2 %emit.1 = (bf16[384,1024]{1,0:T(8,128)(2,1)}, f32[384,1024]{1,0:T(8,128)}, f32[1,32]{1,0:T(1,128)}, f32[1,2]{1,0:T(1,128)}, f32[1,2]{1,0:T(1,128)}, /*index=5*/f...) custom-call(bf16[4,96,1024]{2,1,0:T(8,128)(2,1)} %get-tuple-element., ...), custom_call_target="tpu_custom_call" | custom-call | tf_op jit(solution)/shard_map/emit/pallas_call | solution.py:1358
